TPU v7x, 32 devices: a whole 2x2x4 slice. The times are simulated.
32 devices in a mesh: space: 16 (over z, y, core), vel: 2 (over x).
Axes of the slice: x: 2, y: 2, z: 4, core: 2. Of those that a mesh axis runs over, the one named last changes fastest.
Arguments:
- dist: float32 [13824, 8192], P('vel', 'space'), may hold values from 0.02 to 45, as said below
- free_stream: float32 [13824], P('vel'), may hold values from 0.36 to 14, as said below
- area_normal: float32 [18, 8192], P(None, 'space'), may hold values from -2.7 to 2.7
- cell_volume: float32 [8192], P('space'), may hold values from 0.5 to 2
- face_nbr: int32 [6, 8192], P(None, 'space'), may hold values from 0 to 1023
- face_type: int32 [6, 8192], P(None, 'space'), may hold values from 0 to 2, as said below
- send_list: int32 [4, 2048], P(None, 'space'), may hold values from 0 to 511
Outputs:
- dist_new: float32 [13824, 8192], P('vel', 'space')
Inputs may be any that keep to these rules, and one draw needn't show every extreme that they name: `dist`: every entry is positive. `free_stream`: every entry is positive. `face_nbr`: an entry s at or above 512 names received slot s - 512; entries are read only where face_type is 0. `face_type`: 0 interior or partition face, 1 inflow, 2 outflow. `send_list`: local cell numbers of the sending partition.
All inputs are finite; a program needn't handle non-finite values.
Results may differ from a plain program's by a relative error of at most 0.0003.
Values sent between devices are 32-bit elements; how exact they have to be, the bound alone decides.
No kernel may reach another device: no remote copies, remote signals or barrier semaphores. Data moves between devices by JAX's collectives and lax.ppermute only.
A program may use at most 256 MiB of HBM per device.

v0:
```python
import math

import jax
import jax.numpy as jnp
from jax import lax
from jax.sharding import PartitionSpec as P

NODES = 24


CFL = 0.9
MU_REF = 60.0
OMEGA = 0.81
PRANDTL = 2.0 / 3.0
neighbour_steps = (1, -1, 2, -2)


def passed_along(block, axis, distance):
    devices = range(lax.axis_size(axis))
    route = [((i - distance) % len(devices), i) for i in devices]
    return lax.ppermute(block, axis, route)


def grid_speeds(vel_index):
    spacing = 24.0 / NODES
    half = (NODES - 1) / 2.0
    first = (vel_index // (NODES * NODES)).astype(jnp.float32)
    second = (vel_index // NODES % NODES).astype(jnp.float32)
    last_axis = (vel_index % NODES).astype(jnp.float32)
    return ((first - half) * spacing, (second - half) * spacing, (last_axis - half) * spacing)


def project(table, field):
    return jnp.dot(
        table, field, precision=lax.Precision.HIGHEST, preferred_element_type=jnp.float32
    )


def hydrodynamic_variables(integral_averages):
    specific_matter_amount = integral_averages[0]
    mean_gas_speed = [integral_averages[1 + axis] / specific_matter_amount for axis in range(3)]
    particle_contribution = mean_gas_speed[0] ** 2 + mean_gas_speed[1] ** 2 + mean_gas_speed[2] ** 2
    local_thermal_level = (
        2.0 * integral_averages[4] / specific_matter_amount - particle_contribution
    ) / 3.0
    return (specific_matter_amount, mean_gas_speed, local_thermal_level)


def local(dist, free_stream, area_normal, cell_volume, face_nbr, face_type, send_list):
    vel_local = dist.shape[0]
    cell_count = dist.shape[1]
    vel_index = lax.axis_index("vel") * vel_local + jnp.arange(vel_local, dtype=jnp.int32)
    speeds = grid_speeds(vel_index)
    spacing = 24.0 / NODES
    weight = spacing**3
    top_speed = (NODES - 1) / 2.0 * spacing * math.sqrt(3.0)
    normals = area_normal.reshape(6, 3, cell_count)
    face_areas = jnp.sqrt(jnp.sum(normals * normals, axis=1))
    cell_limit = cell_volume / (top_speed * jnp.sum(face_areas, axis=0))
    time_step = CFL * lax.pmin(jnp.min(cell_limit), "space")
    step_ratio = time_step / cell_volume
    outgoing = [jnp.take(dist, send_list[direction], axis=1) for direction in range(4)]
    arrived = [
        passed_along(outgoing[direction], "space", neighbour_steps[direction])
        for direction in range(4)
    ]
    columns = [speeds[axis][:, None] for axis in range(3)]
    speed_sq = speeds[0] ** 2 + speeds[1] ** 2 + speeds[2] ** 2
    base_table = (
        jnp.stack([jnp.ones_like(speeds[0]), speeds[0], speeds[1], speeds[2], 0.5 * speed_sq])
        * weight
    )
    invariant_quantities = lax.psum(project(base_table, dist), "vel")
    specific_matter_amount, mean_gas_speed, local_thermal_level = hydrodynamic_variables(
        invariant_quantities
    )
    rel_old = [columns[axis] - mean_gas_speed[axis] for axis in range(3)]
    rel_old_sq = rel_old[0] ** 2 + rel_old[1] ** 2 + rel_old[2] ** 2
    local_heat = jnp.stack(
        [0.5 * weight * jnp.sum(rel_old[axis] * rel_old_sq * dist, axis=0) for axis in range(3)]
    )
    heat_flux = lax.psum(local_heat, "vel")
    extended = jnp.concatenate([dist] + arrived, axis=1)
    flux_total = jnp.zeros_like(dist)
    for face_slot in range(6):
        normal_speed = (
            columns[0] * normals[face_slot, 0]
            + columns[1] * normals[face_slot, 1]
            + columns[2] * normals[face_slot, 2]
        )
        outside = jnp.take(extended, face_nbr[face_slot], axis=1)
        face_kind = face_type[face_slot]
        outside = jnp.where(
            face_kind == 0, outside, jnp.where(face_kind == 1, free_stream[:, None], dist)
        )
        flux_total = flux_total + jnp.where(
            normal_speed > 0, normal_speed * dist, normal_speed * outside
        )
    flux_moments = lax.psum(project(base_table, flux_total), "vel")
    new_moments = invariant_quantities - step_ratio[None, :] * flux_moments
    density_new, mean_new, temp_new = hydrodynamic_variables(new_moments)
    relax_time = MU_REF * temp_new**OMEGA / (density_new * temp_new)
    relax_ratio = time_step / relax_time
    rel_new = [columns[axis] - mean_new[axis] for axis in range(3)]
    rel_sq = rel_new[0] ** 2 + rel_new[1] ** 2 + rel_new[2] ** 2
    maxwell = (
        density_new * (2.0 * math.pi * temp_new) ** (-1.5) * jnp.exp(-rel_sq / (2.0 * temp_new))
    )
    along_heat = rel_new[0] * heat_flux[0] + rel_new[1] * heat_flux[1] + rel_new[2] * heat_flux[2]
    shakhov = maxwell * (
        1.0
        + (1.0 - PRANDTL)
        * along_heat
        / (5.0 * density_new * temp_new * temp_new)
        * (rel_sq / temp_new - 5.0)
    )
    transported = dist - step_ratio[None, :] * flux_total
    return (transported + relax_ratio * shakhov) / (1.0 + relax_ratio)


def solution(mesh):
    return jax.shard_map(
        local,
        mesh=mesh,
        in_specs=(
            P("vel", "space"),
            P("vel"),
            P(None, "space"),
            P("space"),
            P(None, "space"),
            P(None, "space"),
            P(None, "space"),
        ),
        out_specs=P("vel", "space"),
        check_vma=False,
    )
```

profile of v0, /device:TPU:0, one launch (start us, length us, event | category | flops | bytes accessed | tf_op | source)
XLA Modules:
  0.0 572.3 jit_solution(17847165975950220548)
XLA Ops:
  0.0 15.1 %copy.47 = f32[6912,512]{0,1:T(8,128)} copy(f32[6912,512]{1,0:T(8,128)} %param.11) | data formatting | bytes 28311552 | tf_op args[0]
  15.1 0.6 compare_and_fusion.6
  15.7 8.4 %gather_fusion = f32[128,6912]{1,0:T(8,128)S(1)} fusion(f32[6912,512]{0,1:T(8,128)} %copy.47, s32[1024]{0:T(1024)S(1)} %pad_clamp_fusion.9), kind=kCustom, calls=%fused_computation.clone | custom fusion | bytes 7078400 | tf_op jit(solution)/shard_map/jit(_take)/gather | solution.py:62
  24.1 2.1 select_bitcast_fusion.3
  26.1 0.5 collective-permute-start
  26.6 0.6 pad_clamp_fusion.8
  27.2 8.4 %gather_fusion.1 = f32[128,6912]{1,0:T(8,128)S(1)} fusion(f32[6912,512]{0,1:T(8,128)} %copy.47, s32[1024]{0:T(1024)S(1)} %pad_clamp_fusion.8), kind=kCustom, calls=%fused_computation.2.clone | custom fusion | bytes 7078400 | tf_op jit(solution)/shard_map/jit(_take)/gather | solution.py:62
  35.6 2.0 select_bitcast_fusion.2
  37.6 5.0 collective-permute-start.1
  42.7 8.4 %gather_fusion.2 = f32[128,6912]{1,0:T(8,128)S(1)} fusion(f32[6912,512]{0,1:T(8,128)} %copy.47, s32[1024]{0:T(1024)S(1)} %pad_clamp_fusion.7), kind=kCustom, calls=%fused_computation.3.clone | custom fusion | bytes 7078400 | tf_op jit(solution)/shard_map/jit(_take)/gather | solution.py:62
  51.0 2.1 select_bitcast_fusion.1
  53.3 0.6 pad_clamp_fusion.6
  53.9 8.5 %gather_fusion.3 = f32[128,6912]{1,0:T(8,128)S(1)} fusion(f32[6912,512]{0,1:T(8,128)} %copy.47, s32[1024]{0:T(1024)} %pad_clamp_fusion.6), kind=kCustom, calls=%fused_computation.4.clone | custom fusion | bytes 7078400 | tf_op jit(solution)/shard_map/jit(_take)/gather | solution.py:62
  62.4 2.7 select_bitcast_fusion
  65.1 4.7 collective-permute-start.3
  69.8 0.7 fusion.50
  70.5 0.6 fusion.55
  71.1 1.0 fusion.62
  72.1 1.1 add_multiply_fusion
  73.3 0.6 compare_select_fusion.4
  73.9 0.5 compare_select_fusion.5
  74.5 0.6 compare_select_fusion.2
  75.1 0.6 compare_select_fusion.3
  75.7 0.5 compare_select_fusion
  76.2 0.6 compare_select_fusion.1
  76.8 1.4 reshape.240
  78.2 0.6 stack_broadcast_in_dim.3
  78.8 1.7 stack.4
  80.5 9.4 %fusion.74 = f32[5,512]{1,0:T(8,128)} fusion(f32[5,6912]{1,0:T(8,128)} %stack.4, f32[6912,512]{1,0:T(8,128)} %param.11), kind=kOutput, calls=%fused_computation.194 | convolution fusion | flops 212336640 | bytes 14304256 | tf_op jit(solution)/shard_map/dot_general | solution.py:34
  90.0 9.2 %psum.21 = f32[5,512]{1,0:T(8,128)S(1)} all-reduce(f32[5,512]{1,0:T(8,128)} %fusion.74), channel_id=1, replica_groups=mesh['space'=16,'vel'=2] {'vel'}, use_global_device_ids=true, to_apply=%region_4.7 | all-reduce | flops 2560 | bytes 20480 | tf_op jit(solution)/shard_map/psum | solution.py:73
  99.3 0.8 multiply_reduce_fusion
  100.1 13.1 %fusion.21 = (f32[512]{0:T(512)S(1)}, f32[512]{0:T(512)S(1)}, f32[512]{0:T(512)S(1)}) fusion(f32[6912,512]{0,1:T(8,128)} %copy.47, f32[512]{0:T(512)S(1)} %bitcast.158, f32[512]{0:T(512)S(1)} %bitcast.157, f32[512]{0:T(512)S(1)} %bitcast.156, f32[6912]{0:T(1024)} %fusion.55, f32[6912]{0:T(1024)} %get-tuple-element.85, f32[6912]{0:T(1024)} %get-tuple-element.84), kind=kLoop, calls=%fused_computation.43 | loop fusion | flops 60160512 | bytes 14251008 | tf_op jit(solution)/shard_map/reduce_sum | solution.py:80
  113.3 0.6 pad_clamp_fusion.4
  113.9 0.6 fusion.69
  114.5 0.5 broadcast_multiply_fusion.2
  115.0 0.5 broadcast_multiply_fusion.1
  115.5 0.6 broadcast_multiply_fusion
  116.1 0.6 pad_clamp_fusion.2
  116.7 166.4 %pmin.7 = f32[]{:T(128)} all-reduce(f32[]{:T(128)} %fusion.69), channel_id=1, replica_groups=mesh['space'=16,'vel'=2] {'space'}, use_global_device_ids=true, to_apply=%region_3.4 | all-reduce | flops 1 | bytes 8 | tf_op jit(solution)/shard_map/pmin | solution.py:60
  283.7 1.3 pad_clamp_fusion
  284.9 1.3 pad_maximum_fusion
  286.2 1.6 compare_reduce_fusion.11
  287.9 1.3 compare_and_fusion
  289.1 1.3 compare_and_fusion.2
  290.4 1.3 broadcast_divide_fusion
  291.6 1.3 compare_and_fusion.4
  292.9 1.6 fusion.71
  294.5 11.0 %constant_dynamic-update-slice_fusion.4 = f32[6912,1024]{0,1:T(8,128)} fusion(f32[6912,512]{0,1:T(8,128)} %copy.47), kind=kLoop, calls=%fused_computation.126 | loop fusion | bytes 28311552
  305.5 4.0 constant_dynamic-update-slice_fusion.3
  309.5 4.0 constant_dynamic-update-slice_fusion.2
  313.4 4.0 constant_dynamic-update-slice_fusion.1
  317.4 2.1 constant_dynamic-update-slice_fusion
  319.5 22.9 %gather_fusion.4 = f32[512,6912]{1,0:T(8,128)} fusion(f32[6912,1024]{0,1:T(8,128)} %constant_dynamic-update-slice_fusion, s32[1024]{0:T(1024)S(1)} %copy-done.17), kind=kCustom, calls=%fused_computation.1.clone | custom fusion | bytes 28313600 | tf_op jit(solution)/shard_map/jit(_take)/gather | solution.py:91
  342.4 23.3 %gather_fusion.5 = f32[512,6912]{1,0:T(8,128)} fusion(f32[6912,1024]{0,1:T(8,128)} %constant_dynamic-update-slice_fusion, s32[1024]{0:T(1024)S(1)} %copy-done.16), kind=kCustom, calls=%fused_computation.5.clone | custom fusion | bytes 28313600 | tf_op jit(solution)/shard_map/jit(_take)/gather | solution.py:91
  365.7 22.9 %gather_fusion.6 = f32[512,6912]{1,0:T(8,128)} fusion(f32[6912,1024]{0,1:T(8,128)} %constant_dynamic-update-slice_fusion, s32[1024]{0:T(1024)S(1)} %copy-done.19), kind=kCustom, calls=%fused_computation.6.clone | custom fusion | bytes 28313600 | tf_op jit(solution)/shard_map/jit(_take)/gather | solution.py:91
  388.6 23.2 %gather_fusion.7 = f32[512,6912]{1,0:T(8,128)} fusion(f32[6912,1024]{0,1:T(8,128)} %constant_dynamic-update-slice_fusion, s32[1024]{0:T(1024)S(1)} %copy-done.18), kind=kCustom, calls=%fused_computation.7.clone | custom fusion | bytes 28313600 | tf_op jit(solution)/shard_map/jit(_take)/gather | solution.py:91
  411.8 23.1 %gather_fusion.8 = f32[512,6912]{1,0:T(8,128)} fusion(f32[6912,1024]{0,1:T(8,128)} %constant_dynamic-update-slice_fusion, s32[1024]{0:T(1024)S(1)} %copy-done.21), kind=kCustom, calls=%fused_computation.8.clone | custom fusion | bytes 28313600 | tf_op jit(solution)/shard_map/jit(_take)/gather | solution.py:91
  435.3 23.1 %gather_fusion.9 = f32[512,6912]{1,0:T(8,128)} fusion(f32[6912,1024]{0,1:T(8,128)} %constant_dynamic-update-slice_fusion, s32[1024]{0:T(1024)S(1)} %copy-done.20), kind=kCustom, calls=%fused_computation.9.clone | custom fusion | bytes 28313600 | tf_op jit(solution)/shard_map/jit(_take)/gather | solution.py:91
  458.7 50.3 %fusion.27 = f32[6912,512]{0,1:T(8,128)S(1)} fusion(f32[512,6912]{1,0:T(8,128)} %gather_fusion.9, f32[512,6912]{1,0:T(8,128)} %gather_fusion.8, f32[512,6912]{1,0:T(8,128)} %gather_fusion.7, f32[512,6912]{1,0:T(8,128)} %gather_fusion.6, f32[512,6912]{1,0:T(8,128)} %gather_fusion.5, f32[512,6912]{1,0:T(8,128)} %gather_fusion.4, f32[6912,512]{0,1:T(8,128)} %copy.47, ...), kind=kLoop, calls=%fused_computation.50 | loop fusion | flops 272498688 | bytes 113402880 | tf_op jit(solution)/shard_map/add | solution.py:96
  509.0 5.0 copy-done
  514.1 11.7 %fusion.75 = f32[5,512]{1,0:T(8,128)S(1)} fusion(f32[5,6912]{1,0:T(8,128)S(1)} %copy-done.1, f32[6912,512]{0,1:T(8,128)S(1)} %fusion.27), kind=kOutput, calls=%fused_computation.195 | convolution fusion | flops 212336640 | bytes 14304256 | tf_op jit(solution)/shard_map/dot_general | solution.py:34
  525.8 8.7 %all-reduce = (f32[5,512]{1,0:T(8,128)S(1)}, f32[3,512]{1,0:T(4,128)S(1)}) all-reduce(f32[5,512]{1,0:T(8,128)S(1)} %fusion.75, f32[3,512]{1,0:T(4,128)S(1)} %copy-done.7), channel_id=1, replica_groups=mesh['space'=16,'vel'=2] {'vel'}, use_global_device_ids=true, to_apply=%region_5.8 | all-reduce | flops 4096 | bytes 32768 | tf_op jit(solution)/shard_map/psum | solution.py:99
  534.6 22.1 %fusion.17 = f32[6912,512]{0,1:T(8,128)} fusion(f32[6912,512]{0,1:T(8,128)} %copy.47, f32[6912,512]{0,1:T(8,128)} %copy-done, f32[512]{0:T(512)S(1)} %bitcast.162, f32[512]{0:T(512)S(1)} %bitcast.166, f32[512]{0:T(512)S(1)} %bitcast.164, f32[512]{0:T(512)S(1)} %bitcast.160, f32[512]{0:T(512)S(1)} %bitcast.161, f32[512]{0:T(512)S(1)} %bitcast.159, ...), kind=kLoop, calls=%fused_computation.39 | loop fusion | flops 99090432 | bytes 42576896 | tf_op jit(solution)/shard_map/div | solution.py:118
  556.7 15.1 %copy.51 = f32[6912,512]{1,0:T(8,128)} copy(f32[6912,512]{0,1:T(8,128)} %fusion.17) | data formatting | bytes 28311552 | tf_op jit(solution)/shard_map/div | solution.py:118
  (143 shorter events, 0.6 us)
Async XLA Ops:
  0.0 15.1 %copy-start.46 = (s32[4,128]{1,0:T(4,128)S(1)}, s32[4,128]{1,0:T(4,128)}, u32[]{:S(2)}) copy-start(s32[4,128]{1,0:T(4,128)} %param.17) | copy-start | bytes 6148
  26.1 279.3 %collective-permute-start = (f32[6912,128]{0,1:T(8,128)}, f32[6912,128]{0,1:T(8,128)}, u32[]{:S(2)}, u32[]{:S(2)}) collective-permute-start(f32[6912,128]{0,1:T(8,128)} %select_bitcast_fusion.3), channel_id=1, source_target_pairs={{30,0},{0,2},{2,4},{4,6},{6,8},{8,10},{10,12},{12,14},{14,16},{16,... | collective-permute-start | bytes 10616840 | tf_op jit(solution)/shard_map/ppermute | solution.py:21
  27.2 15.4 %copy-start.48 = (s32[128]{0:T(128)S(1)}, s32[128]{0:T(128)}, u32[]{:S(2)}) copy-start(s32[128]{0:T(128)} %get-tuple-element.77) | copy-start | bytes 1540
  37.6 271.8 %collective-permute-start.1 = (f32[6912,128]{0,1:T(8,128)}, f32[6912,128]{0,1:T(8,128)}, u32[]{:S(2)}, u32[]{:S(2)}) collective-permute-start(f32[6912,128]{0,1:T(8,128)} %select_bitcast_fusion.2), channel_id=1, source_target_pairs={{2,0},{4,2},{6,4},{8,6},{10,8},{12,10},{14,12},{16,14},{18,16},{20... | collective-permute-start | bytes 10616840 | tf_op jit(solution)/shard_map/ppermute | solution.py:21
  42.7 10.6 %copy-start.47 = (s32[128]{0:T(128)S(1)}, s32[128]{0:T(128)}, u32[]{:S(2)}) copy-start(s32[128]{0:T(128)} %get-tuple-element.32) | copy-start | bytes 1540
  53.1 260.3 %collective-permute-start.2 = (f32[6912,128]{0,1:T(8,128)}, f32[6912,128]{0,1:T(8,128)}, u32[]{:S(2)}, u32[]{:S(2)}) collective-permute-start(f32[6912,128]{0,1:T(8,128)} %select_bitcast_fusion.1), channel_id=1, source_target_pairs={{28,0},{30,2},{0,4},{2,6},{4,8},{6,10},{8,12},{10,14},{12,16},{14,... | collective-permute-start | bytes 10616840 | tf_op jit(solution)/shard_map/ppermute | solution.py:21
  53.9 19.4 %copy-start.22 = (s32[6,512]{1,0:T(8,128)S(1)}, s32[6,512]{1,0:T(8,128)}, u32[]{:S(2)}) copy-start(s32[6,512]{1,0:T(8,128)} %param.15) | copy-start | bytes 36868
  65.1 252.3 %collective-permute-start.3 = (f32[6912,128]{0,1:T(8,128)}, f32[6912,128]{0,1:T(8,128)S(1)}, u32[]{:S(2)}, u32[]{:S(2)}) collective-permute-start(f32[6912,128]{0,1:T(8,128)} %select_bitcast_fusion), channel_id=1, source_target_pairs={{4,0},{6,2},{8,4},{10,6},{12,8},{14,10},{16,12},{18,14},{20,16},{2... | collective-permute-start | bytes 10616840 | tf_op jit(solution)/shard_map/ppermute | solution.py:21
  73.3 2.9 copy-start.15
  99.2 206.3 %copy-start.5 = (f32[5,512]{1,0:T(8,128)}, f32[5,512]{1,0:T(8,128)S(1)}, u32[]{:S(2)}) copy-start(f32[5,512]{1,0:T(8,128)S(1)} %psum.21) | copy-start | bytes 30724
  99.2 14.0 %copy-start.44 = (s32[512]{0:T(512)S(1)}, s32[512]{0:T(512)}, u32[]{:S(2)}) copy-start(s32[512]{0:T(512)} %compare_select_fusion.4) | copy-start | bytes 6148
  99.2 14.0 %copy-start.45 = (s32[512]{0:T(512)S(1)}, s32[512]{0:T(512)}, u32[]{:S(2)}) copy-start(s32[512]{0:T(512)} %compare_select_fusion.5) | copy-start | bytes 6148
  99.2 14.7 %copy-start.41 = (f32[512]{0:T(512)S(1)}, f32[512]{0:T(512)}, u32[]{:S(2)}) copy-start(f32[512]{0:T(512)} %param.14) | copy-start | bytes 6148
  99.2 16.9 %copy-start.42 = (s32[512]{0:T(512)S(1)}, s32[512]{0:T(512)}, u32[]{:S(2)}) copy-start(s32[512]{0:T(512)} %compare_select_fusion.2) | copy-start | bytes 6148
  99.2 16.9 %copy-start.43 = (s32[512]{0:T(512)S(1)}, s32[512]{0:T(512)}, u32[]{:S(2)}) copy-start(s32[512]{0:T(512)} %compare_select_fusion.3) | copy-start | bytes 6148
  305.4 14.1 %copy-start.17 = (s32[1024]{0:T(1024)S(1)}, s32[1024]{0:T(1024)}, u32[]{:S(2)}) copy-start(s32[1024]{0:T(1024)} %get-tuple-element.83) | copy-start | bytes 12292
  319.5 22.9 %copy-start.16 = (s32[1024]{0:T(1024)S(1)}, s32[1024]{0:T(1024)}, u32[]{:S(2)}) copy-start(s32[1024]{0:T(1024)} %get-tuple-element.82) | copy-start | bytes 12292
  342.4 23.3 %copy-start.19 = (s32[1024]{0:T(1024)S(1)}, s32[1024]{0:T(1024)}, u32[]{:S(2)}) copy-start(s32[1024]{0:T(1024)} %get-tuple-element.81) | copy-start | bytes 12292
  365.7 22.9 %copy-start.18 = (s32[1024]{0:T(1024)S(1)}, s32[1024]{0:T(1024)}, u32[]{:S(2)}) copy-start(s32[1024]{0:T(1024)} %get-tuple-element.80) | copy-start | bytes 12292
  388.6 23.2 %copy-start.21 = (s32[1024]{0:T(1024)S(1)}, s32[1024]{0:T(1024)}, u32[]{:S(2)}) copy-start(s32[1024]{0:T(1024)} %get-tuple-element.79) | copy-start | bytes 12292
  411.8 23.1 %copy-start.20 = (s32[1024]{0:T(1024)S(1)}, s32[1024]{0:T(1024)}, u32[]{:S(2)}) copy-start(s32[1024]{0:T(1024)} %get-tuple-element.78) | copy-start | bytes 12292
  434.9 23.4 %copy-start.2 = (f32[6912]{0:T(1024)S(1)}, f32[6912]{0:T(1024)}, u32[]{:S(2)}) copy-start(f32[6912]{0:T(1024)} %get-tuple-element.84) | copy-start | bytes 82948
  434.9 23.4 %copy-start.3 = (f32[6912]{0:T(1024)S(1)}, f32[6912]{0:T(1024)}, u32[]{:S(2)}) copy-start(f32[6912]{0:T(1024)} %get-tuple-element.85) | copy-start | bytes 82948
  434.9 23.4 %copy-start.4 = (f32[6912]{0:T(1024)S(1)}, f32[6912]{0:T(1024)}, u32[]{:S(2)}) copy-start(f32[6912]{0:T(1024)} %fusion.55) | copy-start | bytes 82948
  434.9 23.4 %copy-start.8 = (f32[6912]{0:T(1024)S(1)}, f32[6912]{0:T(1024)}, u32[]{:S(2)}) copy-start(f32[6912]{0:T(1024)} %param.12) | copy-start | bytes 82948
  434.9 23.4 %copy-start.23 = (f32[1,1,512]{2,1,0:T(1,128)S(1)}, f32[1,1,512]{2,1,0:T(1,128)}, u32[]{:S(2)}) copy-start(f32[1,1,512]{2,1,0:T(1,128)} %get-tuple-element.39) | copy-start | bytes 6148
  434.9 23.4 %copy-start.24 = (f32[1,1,512]{2,1,0:T(1,128)S(1)}, f32[1,1,512]{2,1,0:T(1,128)}, u32[]{:S(2)}) copy-start(f32[1,1,512]{2,1,0:T(1,128)} %get-tuple-element.40) | copy-start | bytes 6148
  434.9 23.4 %copy-start.25 = (f32[1,1,512]{2,1,0:T(1,128)S(1)}, f32[1,1,512]{2,1,0:T(1,128)}, u32[]{:S(2)}) copy-start(f32[1,1,512]{2,1,0:T(1,128)} %get-tuple-element.41) | copy-start | bytes 6148
  435.0 23.4 %copy-start.26 = (f32[1,1,512]{2,1,0:T(1,128)S(1)}, f32[1,1,512]{2,1,0:T(1,128)}, u32[]{:S(2)}) copy-start(f32[1,1,512]{2,1,0:T(1,128)} %get-tuple-element.42) | copy-start | bytes 6148
  435.0 23.4 %copy-start.27 = (f32[1,1,512]{2,1,0:T(1,128)S(1)}, f32[1,1,512]{2,1,0:T(1,128)}, u32[]{:S(2)}) copy-start(f32[1,1,512]{2,1,0:T(1,128)} %get-tuple-element.43) | copy-start | bytes 6148
  435.0 23.4 %copy-start.28 = (f32[1,1,512]{2,1,0:T(1,128)S(1)}, f32[1,1,512]{2,1,0:T(1,128)}, u32[]{:S(2)}) copy-start(f32[1,1,512]{2,1,0:T(1,128)} %get-tuple-element.44) | copy-start | bytes 6148
  435.0 23.4 %copy-start.29 = (f32[1,1,512]{2,1,0:T(1,128)S(1)}, f32[1,1,512]{2,1,0:T(1,128)}, u32[]{:S(2)}) copy-start(f32[1,1,512]{2,1,0:T(1,128)} %get-tuple-element.45) | copy-start | bytes 6148
  435.0 23.4 %copy-start.30 = (f32[1,1,512]{2,1,0:T(1,128)S(1)}, f32[1,1,512]{2,1,0:T(1,128)}, u32[]{:S(2)}) copy-start(f32[1,1,512]{2,1,0:T(1,128)} %get-tuple-element.46) | copy-start | bytes 6148
  435.0 23.4 %copy-start.31 = (f32[1,1,512]{2,1,0:T(1,128)S(1)}, f32[1,1,512]{2,1,0:T(1,128)}, u32[]{:S(2)}) copy-start(f32[1,1,512]{2,1,0:T(1,128)} %get-tuple-element.47) | copy-start | bytes 6148
  435.0 23.4 %copy-start.32 = (f32[1,1,512]{2,1,0:T(1,128)S(1)}, f32[1,1,512]{2,1,0:T(1,128)}, u32[]{:S(2)}) copy-start(f32[1,1,512]{2,1,0:T(1,128)} %get-tuple-element.48) | copy-start | bytes 6148
  435.0 23.4 %copy-start.33 = (f32[1,1,512]{2,1,0:T(1,128)S(1)}, f32[1,1,512]{2,1,0:T(1,128)}, u32[]{:S(2)}) copy-start(f32[1,1,512]{2,1,0:T(1,128)} %get-tuple-element.49) | copy-start | bytes 6148
  435.0 23.4 %copy-start.34 = (f32[1,1,512]{2,1,0:T(1,128)S(1)}, f32[1,1,512]{2,1,0:T(1,128)}, u32[]{:S(2)}) copy-start(f32[1,1,512]{2,1,0:T(1,128)} %get-tuple-element.50) | copy-start | bytes 6148
  435.0 23.4 %copy-start.35 = (f32[1,1,512]{2,1,0:T(1,128)S(1)}, f32[1,1,512]{2,1,0:T(1,128)}, u32[]{:S(2)}) copy-start(f32[1,1,512]{2,1,0:T(1,128)} %get-tuple-element.51) | copy-start | bytes 6148
  435.1 23.4 %copy-start.36 = (f32[1,1,512]{2,1,0:T(1,128)S(1)}, f32[1,1,512]{2,1,0:T(1,128)}, u32[]{:S(2)}) copy-start(f32[1,1,512]{2,1,0:T(1,128)} %get-tuple-element.52) | copy-start | bytes 6148
  435.1 23.4 %copy-start.37 = (f32[1,1,512]{2,1,0:T(1,128)S(1)}, f32[1,1,512]{2,1,0:T(1,128)}, u32[]{:S(2)}) copy-start(f32[1,1,512]{2,1,0:T(1,128)} %get-tuple-element.53) | copy-start | bytes 6148
  435.1 23.4 %copy-start.38 = (f32[1,1,512]{2,1,0:T(1,128)S(1)}, f32[1,1,512]{2,1,0:T(1,128)}, u32[]{:S(2)}) copy-start(f32[1,1,512]{2,1,0:T(1,128)} %get-tuple-element.54) | copy-start | bytes 6148
  435.1 23.4 %copy-start.39 = (f32[1,1,512]{2,1,0:T(1,128)S(1)}, f32[1,1,512]{2,1,0:T(1,128)}, u32[]{:S(2)}) copy-start(f32[1,1,512]{2,1,0:T(1,128)} %get-tuple-element.55) | copy-start | bytes 6148
  435.1 23.4 %copy-start.40 = (f32[1,1,512]{2,1,0:T(1,128)S(1)}, f32[1,1,512]{2,1,0:T(1,128)}, u32[]{:S(2)}) copy-start(f32[1,1,512]{2,1,0:T(1,128)} %get-tuple-element.56) | copy-start | bytes 6148
  435.1 23.4 %copy-start.49 = (pred[512]{0:T(512)(128)(4,1)S(1)}, pred[512]{0:T(512)(128)(4,1)}, u32[]{:S(2)}) copy-start(pred[512]{0:T(512)(128)(4,1)} %get-tuple-element.10) | copy-start | bytes 1540
  435.1 23.4 %copy-start.50 = (pred[512]{0:T(512)(128)(4,1)S(1)}, pred[512]{0:T(512)(128)(4,1)}, u32[]{:S(2)}) copy-start(pred[512]{0:T(512)(128)(4,1)} %get-tuple-element.11) | copy-start | bytes 1540
  435.1 23.4 %copy-start.51 = (pred[512]{0:T(512)(128)(4,1)S(1)}, pred[512]{0:T(512)(128)(4,1)}, u32[]{:S(2)}) copy-start(pred[512]{0:T(512)(128)(4,1)} %get-tuple-element.12) | copy-start | bytes 1540
  435.1 23.4 %copy-start.52 = (pred[512]{0:T(512)(128)(4,1)S(1)}, pred[512]{0:T(512)(128)(4,1)}, u32[]{:S(2)}) copy-start(pred[512]{0:T(512)(128)(4,1)} %get-tuple-element.13) | copy-start | bytes 1540
  435.1 23.4 %copy-start.53 = (pred[512]{0:T(512)(128)(4,1)S(1)}, pred[512]{0:T(512)(128)(4,1)}, u32[]{:S(2)}) copy-start(pred[512]{0:T(512)(128)(4,1)} %get-tuple-element.14) | copy-start | bytes 1540
  435.2 23.4 %copy-start.54 = (pred[512]{0:T(512)(128)(4,1)S(1)}, pred[512]{0:T(512)(128)(4,1)}, u32[]{:S(2)}) copy-start(pred[512]{0:T(512)(128)(4,1)} %get-tuple-element.15) | copy-start | bytes 1540
  435.2 23.4 %copy-start.55 = (pred[512]{0:T(512)(128)(4,1)S(1)}, pred[512]{0:T(512)(128)(4,1)}, u32[]{:S(2)}) copy-start(pred[512]{0:T(512)(128)(4,1)} %get-tuple-element.16) | copy-start | bytes 1540
  435.2 23.4 %copy-start.56 = (pred[512]{0:T(512)(128)(4,1)S(1)}, pred[512]{0:T(512)(128)(4,1)}, u32[]{:S(2)}) copy-start(pred[512]{0:T(512)(128)(4,1)} %get-tuple-element.17) | copy-start | bytes 1540
  435.2 23.4 %copy-start.57 = (pred[512]{0:T(512)(128)(4,1)S(1)}, pred[512]{0:T(512)(128)(4,1)}, u32[]{:S(2)}) copy-start(pred[512]{0:T(512)(128)(4,1)} %get-tuple-element.18) | copy-start | bytes 1540
  435.2 23.4 %copy-start.58 = (pred[512]{0:T(512)(128)(4,1)S(1)}, pred[512]{0:T(512)(128)(4,1)}, u32[]{:S(2)}) copy-start(pred[512]{0:T(512)(128)(4,1)} %get-tuple-element.19) | copy-start | bytes 1540
  435.2 23.4 %copy-start.59 = (pred[512]{0:T(512)(128)(4,1)S(1)}, pred[512]{0:T(512)(128)(4,1)}, u32[]{:S(2)}) copy-start(pred[512]{0:T(512)(128)(4,1)} %get-tuple-element.20) | copy-start | bytes 1540
  435.2 23.4 %copy-start.60 = (pred[512]{0:T(512)(128)(4,1)S(1)}, pred[512]{0:T(512)(128)(4,1)}, u32[]{:S(2)}) copy-start(pred[512]{0:T(512)(128)(4,1)} %get-tuple-element.21) | copy-start | bytes 1540
  435.2 23.4 %copy-start.61 = (pred[512]{0:T(512)(128)(4,1)S(1)}, pred[512]{0:T(512)(128)(4,1)}, u32[]{:S(2)}) copy-start(pred[512]{0:T(512)(128)(4,1)} %get-tuple-element.90) | copy-start | bytes 1540
  435.2 23.4 %copy-start.62 = (pred[512]{0:T(512)(128)(4,1)S(1)}, pred[512]{0:T(512)(128)(4,1)}, u32[]{:S(2)}) copy-start(pred[512]{0:T(512)(128)(4,1)} %get-tuple-element.91) | copy-start | bytes 1540
  435.2 23.4 %copy-start.63 = (pred[512]{0:T(512)(128)(4,1)S(1)}, pred[512]{0:T(512)(128)(4,1)}, u32[]{:S(2)}) copy-start(pred[512]{0:T(512)(128)(4,1)} %get-tuple-element.92) | copy-start | bytes 1540
  435.3 23.4 %copy-start.64 = (pred[512]{0:T(512)(128)(4,1)S(1)}, pred[512]{0:T(512)(128)(4,1)}, u32[]{:S(2)}) copy-start(pred[512]{0:T(512)(128)(4,1)} %get-tuple-element.93) | copy-start | bytes 1540
  458.7 55.4 %copy-start.1 = (f32[5,6912]{1,0:T(8,128)S(1)}, f32[5,6912]{1,0:T(8,128)}, u32[]{:S(2)}) copy-start(f32[5,6912]{1,0:T(8,128)} %stack.4) | copy-start | bytes 414724
  509.0 5.0 copy-start
  514.1 11.7 %copy-start.7 = (f32[3,512]{1,0:T(4,128)S(1)}, f32[3,512]{1,0:T(4,128)}, u32[]{:S(2)}) copy-start(f32[3,512]{1,0:T(4,128)} %pad_maximum_fusion) | copy-start | bytes 18436
  514.1 20.4 %copy-start.6 = (f32[5,512]{1,0:T(8,128)S(1)}, f32[5,512]{1,0:T(8,128)}, u32[]{:S(2)}) copy-start(f32[5,512]{1,0:T(8,128)} %copy-done.5) | copy-start | bytes 30724
  514.1 20.4 %copy-start.9 = (f32[512]{0:T(512)S(1)}, f32[512]{0:T(512)}, u32[]{:S(2)}) copy-start(f32[512]{0:T(512)} %broadcast_divide_fusion) | copy-start | bytes 6148
  (5 other events, 7.2 us)
where the time goes:
time: 581 us; the launch traced here: 572 us
  local copies, waits for them, and re-layouts  238 us (41%)
  blocking collectives  184 us (32%)
  other arithmetic  117 us (20%)
  matrix products  21.1 us (4%)
  starting transfers between devices  10.3 us (2%)
    pmin x1, blocking collectives, local(): time_step = CFL * lax.pmin(jnp.min(cell_limit), 'space')  166 us
    gather x6, local copies, waits for them, and re-layouts, local(): outside = jnp.take(extended, face_nbr[face_slot], axis=1)  138 us
    add x1, other arithmetic, local(): flux_total + jnp.where(normal_speed > 0, normal_speed * dist, normal_spee...  50.3 us
    unnamed x135, local copies, waits for them, and re-layouts  43.3 us
    gather x4, local copies, waits for them, and re-layouts, local(): jnp.take(dist, send_list[direction], axis=1)  33.6 us
    div x1, other arithmetic, local(): return (transported + relax_ratio * shakhov) / (1.0 + relax_ratio)  22.1 us
    dot_general x2, matrix products, project(): jnp.dot(table, field, precision=lax.Precision.HIGHEST, preferred_element_...  21.1 us
    div x1, local copies, waits for them, and re-layouts, local(): return (transported + relax_ratio * shakhov) / (1.0 + relax_ratio)  15.1 us
  transfers between devices with their start and end apart: 4, of which 0 were waited for; matrix products, arithmetic and copies ran while one was open for 18% of the time, Pallas kernels for 0%

commit v1 on v0

v1 whole, which is shorter than its diff:
```python
import functools
import math

import jax
import jax.numpy as jnp
from jax import lax
from jax.experimental import pallas as pl
from jax.experimental.pallas import tpu as pltpu
from jax.sharding import PartitionSpec as P

NODES = 24
PLANE = NODES * NODES
HALF = (NODES - 1) / 2.0
FACES = 6
CFL = 0.9
MU_REF = 60.0
OMEGA = 0.81
PRANDTL = 2.0 / 3.0
neighbour_steps = (1, -1, 2, -2)

LANES = 128
SUB = 8
F32 = jnp.float32
BF16 = jnp.bfloat16
VMEM_LIMIT = 56 * 1024 * 1024


def passed_along(block, axis, distance):
    count = lax.axis_size(axis)
    route = [((i - distance) % count, i) for i in range(count)]
    return lax.ppermute(block, axis, route)


def chunk_plan(planes):
    if planes < 3:
        return [1] * planes
    rounds = max(1, -(-(planes - 2) // 3))
    inner = [(planes - 2) // rounds + (i < (planes - 2) % rounds) for i in range(rounds)]
    return [1] + inner + [1]


def put_split(src_ref, split_ref, at, step=48):
    rows, width = src_ref.shape
    full = split_ref.shape[1] // 2

    @pl.loop(0, rows // step)
    def _(i):
        here = pl.ds(pl.multiple_of(i * step, 16), step)
        value = src_ref[here, :]
        upper = value.astype(BF16)
        split_ref[here, at : at + width] = upper
        split_ref[here, full + at : full + at + width] = (value - upper.astype(F32)).astype(BF16)


def put_one_hot(pick_ref, at, row, step=64):
    height, width = pick_ref.shape[0], row.shape[1]

    @pl.loop(0, height // step)
    def _(i):
        first = pl.multiple_of(i * step, 16)
        index = lax.broadcasted_iota(jnp.int32, (step, width), 0) + first
        pick_ref[pl.ds(first, step), at : at + width] = jnp.where(index == row, 1.0, 0.0).astype(BF16)


def picked(split, pick):
    return jnp.dot(split, jnp.concatenate([pick, pick], axis=0), preferred_element_type=F32)


def send_kernel(dist_ref, send_ref, *refs):
    outs, (split_ref, pick_ref) = refs[:-2], refs[-2:]
    width = send_ref.shape[1]

    @pl.when(pl.program_id(0) == 0)
    def _():
        for o in range(len(outs)):
            put_one_hot(pick_ref, o * width, send_ref[o : o + 1, :])

    put_split(dist_ref, split_ref, 0)
    out = picked(split_ref[...], pick_ref[...])
    for o, out_ref in enumerate(outs):
        out_ref[...] = out[:, o * width : (o + 1) * width]


def rows8(row):
    return jnp.broadcast_to(row, (SUB, row.shape[-1]))


def put_normals(normal_ref, x_ref, y_ref, z_ref):
    cells = normal_ref.shape[1]
    last = lax.broadcasted_iota(jnp.int32, (NODES, cells), 0).astype(F32) - HALF
    total = [jnp.zeros((1, cells), F32)] * 3
    for k in range(FACES + 1):
        parts = [normal_ref[3 * k + a : 3 * k + a + 1, :] for a in range(3)] if k < FACES else total
        if k < FACES:
            total = [total[a] + parts[a] for a in range(3)]
        x_ref[k * SUB : (k + 1) * SUB, :] = rows8(parts[0])
        y_ref[k * SUB : (k + 1) * SUB, :] = rows8(parts[1])
        z_ref[k * NODES : (k + 1) * NODES, :] = last * parts[2]


def last_speeds():
    index = lax.broadcasted_iota(jnp.int32, (SUB, LANES), 0).astype(F32) - HALF
    return [index + float(j * SUB) for j in range(NODES // SUB)]


def z_sums(tiles, speeds, powers):
    sums, terms = [], list(tiles)
    for p in range(powers):
        if p:
            terms = [t * c for t, c in zip(terms, speeds)]
        sums.append(terms[0] + terms[1] + terms[2])
    return sums


def rest_of_moments(sums, first):
    energy = 0.5 * (first * first * sums[0, 0] + sums[0, 1 + 1] + sums[2, 0])
    return [sums[0, 0], first * sums[0, 0], sums[0, 1], sums[1, 0], energy]


def add_rows(acc_ref, values, lanes):
    for m, value in enumerate(values):
        acc_ref[m * SUB : (m + 1) * SUB, lanes] += value


def sum_rows(acc_ref, count):
    return [jnp.sum(acc_ref[m * SUB : (m + 1) * SUB, :], axis=0, keepdims=True) for m in range(count)]


FLUX_KEYS = ((0, 0), (0, 1), (0, 2), (1, 0), (2, 0))
DIST_KEYS = ((0, 0), (0, 1), (0, 2), (0, 3), (1, 0), (1, 1), (1, 2), (2, 0), (2, 1), (3, 0))


def grow(carry, keys, sums, second):
    powers = [None, second, second * second, second * second * second]
    return tuple(
        c + (sums[i] if j == 0 else sums[i] * powers[j]) for c, (i, j) in zip(carry, keys)
    )


def near_kernel(
    plane_ref, dist_ref, stream_ref, normal_ref, nbr_ref, kind_ref, after_ref,
    flux_ref, dist_sum_ref, flux_sum_ref, far_ref,
    split_ref, pick_ref, out_ref, x_ref, y_ref, z_ref, inflow_ref, dist_acc, flux_acc,
):
    step = pl.program_id(0)
    cells = dist_ref.shape[1]

    @pl.when(step == 0)
    def _():
        own = lax.broadcasted_iota(jnp.int32, (1, cells), 1)
        for k in range(FACES):
            nbr, kind = nbr_ref[k : k + 1, :], kind_ref[k : k + 1, :]
            near = jnp.where((kind == 0) & (nbr < cells), nbr, jnp.where(kind == 2, own, -1))
            far = jnp.where((kind == 0) & (nbr >= cells), nbr - cells, -1)
            put_one_hot(pick_ref, k * cells, near)
            put_one_hot(far_ref, k * cells, far)
            inflow_ref[k * SUB : (k + 1) * SUB, :] = rows8(jnp.where(kind == 1, 1.0, 0.0))
        put_normals(normal_ref, x_ref, y_ref, z_ref)
        dist_acc[...] = jnp.zeros_like(dist_acc)
        flux_acc[...] = jnp.zeros_like(flux_acc)

    put_split(dist_ref, split_ref, 0)
    for k in range(FACES):
        out_ref[k] = picked(split_ref[...], pick_ref[:, k * cells : (k + 1) * cells])
    first = (plane_ref[0] + step).astype(F32) - HALF
    speeds = last_speeds()
    tiles = range(NODES // SUB)
    for t in range(cells // LANES):
        lanes = slice(t * LANES, (t + 1) * LANES)
        base_x = [x_ref[k * SUB : (k + 1) * SUB, lanes] * first for k in range(FACES + 1)]

        def body(y, carry, lanes=lanes, base_x=base_x):
            second = y.astype(F32) - HALF
            rows = [pl.ds(pl.multiple_of(y * NODES + j * SUB, SUB), SUB) for j in tiles]
            own = [dist_ref[r, lanes] for r in rows]
            stream = [stream_ref[r, :] for r in rows]
            acc, low = [0.0 for _ in tiles], [0.0 for _ in tiles]
            for k in range(FACES):
                base = base_x[k] + y_ref[k * SUB : (k + 1) * SUB, lanes] * second
                inflow = inflow_ref[k * SUB : (k + 1) * SUB, lanes] > 0.5
                for j in tiles:
                    z = z_ref[k * NODES + j * SUB : k * NODES + (j + 1) * SUB, lanes]
                    inward = jnp.minimum(base + z, 0.0)
                    outside = jnp.where(inflow, stream[j], out_ref[k, rows[j], lanes])
                    acc[j] += inward * outside
                    low[j] += inward
            k = FACES
            base = base_x[k] + y_ref[k * SUB : (k + 1) * SUB, lanes] * second
            flux = []
            for j in tiles:
                z = z_ref[k * NODES + j * SUB : k * NODES + (j + 1) * SUB, lanes]
                flux.append(acc[j] + (base + z - low[j]) * own[j])
                flux_ref[rows[j], lanes] = flux[j]
            dist_part = grow(carry[0], DIST_KEYS, z_sums(own, speeds, 4), second)
            flux_part = grow(carry[1], FLUX_KEYS, z_sums(flux, speeds, 3), second)
            return dist_part, flux_part

        zero = jnp.zeros((SUB, LANES), F32)
        dist_part, flux_part = lax.fori_loop(
            0, NODES, body, ((zero,) * len(DIST_KEYS), (zero,) * len(FLUX_KEYS))
        )
        s = dict(zip(DIST_KEYS, dist_part))
        square = first * first
        add_rows(
            dist_acc,
            rest_of_moments(s, first)
            + [
                square * s[0, 0], s[0, 2], s[2, 0],
                first * s[0, 1], first * s[1, 0], s[1, 1],
                first * (square * s[0, 0] + s[0, 2] + s[2, 0]),
                square * s[0, 1] + s[0, 3] + s[2, 1],
                square * s[1, 0] + s[1, 2] + s[3, 0],
            ],
            lanes,
        )
        add_rows(flux_acc, rest_of_moments(dict(zip(FLUX_KEYS, flux_part)), first), lanes)

    @pl.when(step == pl.num_programs(0) - 1)
    def _():
        dist_sum_ref[...] = jnp.concatenate(
            sum_rows(dist_acc, 14) + [jnp.zeros((2, cells), F32)], axis=0
        )
        flux_sum_ref[...] = jnp.concatenate(
            sum_rows(flux_acc, 5) + [jnp.zeros((3, cells), F32)], axis=0
        )


def far_kernel(
    sends, plane_ref, time_ref, dist_ref, flux_ref, far_ref, normal_ref, volume_ref, before_ref, *refs
):
    arrived, refs = refs[:sends], refs[sends:]
    moved_ref, flux_sum_ref, split_ref, out_ref, x_ref, y_ref, z_ref, flux_acc, ratio_ref = refs
    step = pl.program_id(0)
    cells = dist_ref.shape[1]

    @pl.when(step == 0)
    def _():
        put_normals(normal_ref, x_ref, y_ref, z_ref)
        flux_acc[...] = jnp.zeros_like(flux_acc)
        ratio_ref[...] = rows8(time_ref[0, 0] / volume_ref[...])

    for o, block_ref in enumerate(arrived):
        put_split(block_ref, split_ref, o * block_ref.shape[1])
    for k in range(FACES):
        out_ref[k] = picked(split_ref[...], far_ref[:, k * cells : (k + 1) * cells])
    first = (plane_ref[0] + step).astype(F32) - HALF
    speeds = last_speeds()
    tiles = range(NODES // SUB)
    for t in range(cells // LANES):
        lanes = slice(t * LANES, (t + 1) * LANES)
        base_x = [x_ref[k * SUB : (k + 1) * SUB, lanes] * first for k in range(FACES)]
        ratio = ratio_ref[:, lanes]

        def body(y, carry, lanes=lanes, base_x=base_x, ratio=ratio):
            second = y.astype(F32) - HALF
            rows = [pl.ds(pl.multiple_of(y * NODES + j * SUB, SUB), SUB) for j in tiles]
            acc = [0.0 for _ in tiles]
            for k in range(FACES):
                base = base_x[k] + y_ref[k * SUB : (k + 1) * SUB, lanes] * second
                for j in tiles:
                    z = z_ref[k * NODES + j * SUB : k * NODES + (j + 1) * SUB, lanes]
                    acc[j] += jnp.minimum(base + z, 0.0) * out_ref[k, rows[j], lanes]
            for j in tiles:
                moved_ref[rows[j], lanes] = dist_ref[rows[j], lanes] - ratio * (
                    flux_ref[rows[j], lanes] + acc[j]
                )
            return grow(carry, FLUX_KEYS, z_sums(acc, speeds, 3), second)

        zero = jnp.zeros((SUB, LANES), F32)
        part = lax.fori_loop(0, NODES, body, (zero,) * len(FLUX_KEYS))
        add_rows(flux_acc, rest_of_moments(dict(zip(FLUX_KEYS, part)), first), lanes)

    @pl.when(step == pl.num_programs(0) - 1)
    def _():
        flux_sum_ref[...] = before_ref[...] + jnp.concatenate(
            sum_rows(flux_acc, 5) + [jnp.zeros((3, cells), F32)], axis=0
        )


def hydrodynamic_variables(moments):
    density = moments[0]
    mean = [moments[1 + axis] / density for axis in range(3)]
    square = mean[0] ** 2 + mean[1] ** 2 + mean[2] ** 2
    return density, mean, (2.0 * moments[4] / density - square) / 3.0


def relax_kernel(
    plane_ref, time_ref, moved_ref, dist_sum_ref, flux_sum_ref, volume_ref, out_ref,
    x_ref, y_ref, z_ref, cell_ref,
):
    step = pl.program_id(0)
    cells = moved_ref.shape[1]

    @pl.when(step == 0)
    def _():
        time_step = time_ref[0, 0]
        ratio = time_step / volume_ref[...]
        sums = [dist_sum_ref[m : m + 1, :] for m in range(14)]
        density, mean, _ = hydrodynamic_variables(sums)
        xx, yy, zz, xy, xz, yz = sums[5:11]
        pairs = ((xx, xy, xz), (xy, yy, yz), (xz, yz, zz))
        square = mean[0] ** 2 + mean[1] ** 2 + mean[2] ** 2
        heat = []
        for a in range(3):
            cross = mean[0] * pairs[a][0] + mean[1] * pairs[a][1] + mean[2] * pairs[a][2]
            heat.append(
                0.5
                * (
                    sums[11 + a] - mean[a] * (2.0 * sums[4]) - 2.0 * cross
                    + 2.0 * mean[a] * square * density
                )
            )
        new = [sums[m] - ratio * flux_sum_ref[m : m + 1, :] for m in range(5)]
        density, mean, temp = hydrodynamic_variables(new)
        relax_time = MU_REF * jnp.exp(OMEGA * jnp.log(temp)) / (density * temp)
        relax = time_step / relax_time
        keep = 1.0 / (1.0 + relax)
        root = lax.rsqrt(2.0 * math.pi * temp)
        front = relax * keep * density * root * root * root
        along = (1.0 - PRANDTL) / (5.0 * density * temp * temp)
        for m, row in enumerate((keep, mean[0], temp, heat[0] * along, front)):
            cell_ref[m * SUB : (m + 1) * SUB, :] = rows8(row)
        nodes = lax.broadcasted_iota(jnp.int32, (NODES, cells), 0).astype(F32) - HALF
        for a, ref in ((1, y_ref), (2, z_ref)):
            rel = nodes - mean[a]
            square = rel * rel / temp
            for i, table in enumerate((jnp.exp(-0.5 * square), square, rel * heat[a] * along)):
                if a == 2:
                    ref[i * NODES : (i + 1) * NODES, :] = table
                    continue
                for y in range(NODES):
                    ref[i, y] = rows8(table[y : y + 1, :])

    keep, mean, temp, heat, front = [
        cell_ref[m * SUB : (m + 1) * SUB, :] for m in range(5)
    ]
    rel = (plane_ref[0] + step).astype(F32) - HALF - mean
    square = rel * rel / temp
    x_ref[0] = front * jnp.exp(-0.5 * square)
    x_ref[1] = square - 5.0
    x_ref[2] = rel * heat
    tiles = range(NODES // SUB)
    for t in range(cells // LANES):
        lanes = slice(t * LANES, (t + 1) * LANES)
        from_x = [x_ref[i, :, lanes] for i in range(3)]
        keep = cell_ref[0:SUB, lanes]

        @pl.loop(0, NODES)
        def _(y, lanes=lanes, from_x=from_x, keep=keep):
            from_y = [y_ref[i, y, :, lanes] for i in range(3)]
            peak = from_x[0] * from_y[0]
            square = from_x[1] + from_y[1]
            along = from_x[2] + from_y[2]
            for j in tiles:
                row = pl.ds(pl.multiple_of(y * NODES + j * SUB, SUB), SUB)
                z = [z_ref[i * NODES + j * SUB : i * NODES + (j + 1) * SUB, lanes] for i in range(3)]
                shape = (along + z[2]) * (square + z[1]) + 1.0
                out_ref[row, lanes] = moved_ref[row, lanes] * keep + peak * z[0] * shape


def params():
    return pltpu.CompilerParams(
        vmem_limit_bytes=VMEM_LIMIT, dimension_semantics=("arbitrary",)
    )


def whole(*shape):
    return pl.BlockSpec(shape, lambda i: (0,) * len(shape))


def planes_from(first, width):
    return pl.BlockSpec((PLANE, width), lambda i: (first + i, 0))


SMEM = pl.BlockSpec(memory_space=pltpu.SMEM)


def gather_sends(dist, send_list, first, planes):
    cells, (dirs, width) = dist.shape[1], send_list.shape
    rows = planes * PLANE
    return pl.pallas_call(
        send_kernel,
        grid=(planes,),
        in_specs=[planes_from(first, cells), whole(dirs, width)],
        out_specs=[planes_from(0, width)] * dirs,
        out_shape=[jax.ShapeDtypeStruct((rows, width), F32)] * dirs,
        scratch_shapes=[
            pltpu.VMEM((PLANE, 2 * cells), BF16),
            pltpu.VMEM((cells, dirs * width), BF16),
        ],
        compiler_params=params(),
        cost_estimate=pl.CostEstimate(
            flops=rows * 4 * cells * dirs * width,
            bytes_accessed=4 * rows * (cells + dirs * width),
            transcendentals=0,
        ),
        name="listed_cells",
    )(dist, send_list)


def near_faces(plane, dist, stream, normals, face_nbr, face_type, slots, after):
    rows, cells = dist.shape
    planes = rows // PLANE
    return pl.pallas_call(
        near_kernel,
        grid=(planes,),
        in_specs=[
            SMEM, planes_from(0, cells), planes_from(0, LANES),
            whole(3 * FACES, cells), whole(FACES, cells), whole(FACES, cells),
            pl.BlockSpec(memory_space=pl.ANY),
        ],
        out_specs=[
            planes_from(0, cells), whole(16, cells), whole(8, cells), whole(slots, FACES * cells),
        ],
        out_shape=[
            jax.ShapeDtypeStruct((rows, cells), F32),
            jax.ShapeDtypeStruct((16, cells), F32),
            jax.ShapeDtypeStruct((8, cells), F32),
            jax.ShapeDtypeStruct((slots, FACES * cells), BF16),
        ],
        scratch_shapes=[
            pltpu.VMEM((PLANE, 2 * cells), BF16),
            pltpu.VMEM((cells, FACES * cells), BF16),
            pltpu.VMEM((FACES, PLANE, cells), F32),
            pltpu.VMEM(((FACES + 1) * SUB, cells), F32),
            pltpu.VMEM(((FACES + 1) * SUB, cells), F32),
            pltpu.VMEM(((FACES + 1) * NODES, cells), F32),
            pltpu.VMEM((FACES * SUB, cells), F32),
            pltpu.VMEM((14 * SUB, cells), F32),
            pltpu.VMEM((5 * SUB, cells), F32),
        ],
        compiler_params=params(),
        cost_estimate=pl.CostEstimate(
            flops=rows * 4 * cells * FACES * cells + 80 * rows * cells,
            bytes_accessed=4 * rows * 2 * cells,
            transcendentals=0,
        ),
        name="near_faces",
    )(plane, dist, stream, normals, face_nbr, face_type, after)


def far_faces(plane, time_step, dist, flux, pick, normals, volume, before, arrived, first, planes):
    cells = dist.shape[1]
    rows = planes * PLANE
    slots = pick.shape[0]
    return pl.pallas_call(
        functools.partial(far_kernel, len(arrived)),
        grid=(planes,),
        in_specs=[
            SMEM, SMEM, planes_from(first, cells), planes_from(first, cells),
            whole(slots, FACES * cells), whole(3 * FACES, cells), whole(1, cells), whole(8, cells),
        ]
        + [planes_from(0, block.shape[1]) for block in arrived],
        out_specs=[planes_from(first, cells), whole(8, cells)],
        out_shape=[
            jax.ShapeDtypeStruct(flux.shape, F32),
            jax.ShapeDtypeStruct((8, cells), F32),
        ],
        scratch_shapes=[
            pltpu.VMEM((PLANE, 2 * slots), BF16),
            pltpu.VMEM((FACES, PLANE, cells), F32),
            pltpu.VMEM(((FACES + 1) * SUB, cells), F32),
            pltpu.VMEM(((FACES + 1) * SUB, cells), F32),
            pltpu.VMEM(((FACES + 1) * NODES, cells), F32),
            pltpu.VMEM((5 * SUB, cells), F32),
            pltpu.VMEM((SUB, cells), F32),
        ],
        input_output_aliases={3: 0},
        compiler_params=params(),
        cost_estimate=pl.CostEstimate(
            flops=rows * 4 * slots * FACES * cells + 40 * rows * cells,
            bytes_accessed=4 * rows * (3 * cells + slots),
            transcendentals=0,
        ),
        name="far_faces",
    )(plane + first, time_step, dist, flux, pick, normals, volume, before, *arrived)


def relaxed(plane, time_step, moved, dist_sum, flux_sum, volume):
    rows, cells = moved.shape
    return pl.pallas_call(
        relax_kernel,
        grid=(rows // PLANE,),
        in_specs=[
            SMEM, SMEM, planes_from(0, cells), whole(16, cells), whole(8, cells), whole(1, cells),
        ],
        out_specs=planes_from(0, cells),
        out_shape=jax.ShapeDtypeStruct((rows, cells), F32),
        scratch_shapes=[
            pltpu.VMEM((3, SUB, cells), F32),
            pltpu.VMEM((3, NODES, SUB, cells), F32),
            pltpu.VMEM((3 * NODES, cells), F32),
            pltpu.VMEM((5 * SUB, cells), F32),
        ],
        compiler_params=params(),
        cost_estimate=pl.CostEstimate(
            flops=10 * rows * cells, bytes_accessed=8 * rows * cells, transcendentals=0
        ),
        name="relaxed",
    )(plane, time_step, moved, dist_sum, flux_sum, volume)


def least_over(value, axis):
    shift = 1
    while shift < lax.axis_size(axis):
        value = jnp.minimum(value, passed_along(value, axis, shift))
        shift *= 2
    return value


def local(dist, free_stream, area_normal, cell_volume, face_nbr, face_type, send_list):
    rows, cells = dist.shape
    planes = rows // PLANE
    dirs, width = send_list.shape
    plane = (lax.axis_index("vel") * planes).astype(jnp.int32).reshape(1)
    top_speed = HALF * math.sqrt(3.0)
    normals = area_normal.reshape(FACES, 3, cells)
    face_areas = jnp.sqrt(jnp.sum(normals * normals, axis=1))
    cell_limit = cell_volume / (top_speed * jnp.sum(face_areas, axis=0))
    time_step = CFL * least_over(jnp.min(cell_limit).reshape(1, 1), "space")
    volume = cell_volume.reshape(1, cells)

    arrived, first = [], 0
    for count in chunk_plan(planes):
        blocks = gather_sends(dist, send_list, first, count)
        moved = [
            passed_along(block, "space", distance)
            for block, distance in zip(blocks, neighbour_steps)
        ]
        arrived.append((first, count, moved))
        first += count
    stream = jnp.broadcast_to(free_stream[:, None], (rows, LANES))
    flux, dist_sum, flux_sum, pick = near_faces(
        plane, dist, stream, area_normal, face_nbr, face_type, dirs * width, blocks[-1]
    )
    dist_sum = lax.psum(dist_sum, "vel")
    for first, count, blocks in arrived:
        flux, flux_sum = far_faces(
            plane, time_step, dist, flux, pick, area_normal, volume, flux_sum, blocks, first, count
        )
    flux_sum = lax.psum(flux_sum, "vel")
    return relaxed(plane, time_step, flux, dist_sum, flux_sum, volume)


def solution(mesh):
    return jax.shard_map(
        local,
        mesh=mesh,
        in_specs=(
            P("vel", "space"),
            P("vel"),
            P(None, "space"),
            P("space"),
            P(None, "space"),
            P(None, "space"),
            P(None, "space"),
        ),
        out_specs=P("vel", "space"),
        check_vma=False,
    )
```

time: 581 us -> 415 us (0.71); the launches traced: 572 us -> 414 us
  Pallas kernels: 0 us -> 266 us
  local copies, waits for them, and re-layouts: 238 us -> 8.18 us
  blocking collectives: 184 us -> 9.12 us
  other arithmetic: 117 us -> 0.76 us
  starting transfers between devices: 10.3 us -> 73.6 us
  waiting for transfers between devices: 0.01 us -> 52.8 us
  matrix products: 21.1 us -> 0 us
    pallas_call x0 -> x14, Pallas kernels: none -> 266 us  [the longest x6 113 us: far_faces(): pl.pallas_call(functools.partial(far_kernel, len(arrived)), grid=(planes,...]
    gather x10 -> x0, local copies, waits for them, and re-layouts: 172 us -> none  [the longest x6 138 us: local(): outside = jnp.take(extended, face_nbr[face_slot], axis=1)]
    pmin x1 -> x0, blocking collectives: 166 us -> none  [local(): time_step = CFL * lax.pmin(jnp.min(cell_limit), 'space')]
    ppermute x4 -> x28, starting transfers between devices: 10.3 us -> 73.6 us  [passed_along(): return lax.ppermute(block, axis, route)]
    ppermute x4 -> x28, waiting for transfers between devices: 0.01 us -> 52.8 us  [passed_along(): return lax.ppermute(block, axis, route)]
    add x2 -> x0, other arithmetic: 50.4 us -> none  [the longest x1 50.3 us: local(): flux_total + jnp.where(normal_speed > 0, normal_speed * dist, normal_spee...]
    unnamed x135 -> x74, local copies, waits for them, and re-layouts: 43.3 us -> 4.11 us
    div x3 -> x0, other arithmetic: 23.4 us -> none  [the longest x1 22.1 us: local(): return (transported + relax_ratio * shakhov) / (1.0 + relax_ratio)]
  transfers between devices with their start and end apart: 4 -> 28, of which waited for: 0 -> 7; matrix products, arithmetic and copies ran while one was open for 18% -> 1% of each run, Pallas kernels for 0% -> 56%
where the time goes in v1:
time: 415 us; the launch traced here: 414 us
  Pallas kernels  266 us (64%)
  starting transfers between devices  73.6 us (18%)
  waiting for transfers between devices  52.8 us (13%)
  blocking collectives  9.12 us (2%)
  local copies, waits for them, and re-layouts  8.18 us (2%)
    pallas_call x6, Pallas kernels, far_faces(): pl.pallas_call(functools.partial(far_kernel, len(arrived)), grid=(planes,...  113 us
    pallas_call x1, Pallas kernels, near_faces(): pl.pallas_call(near_kernel, grid=(planes,), in_specs=[SMEM, planes_from(0...  104 us
    ppermute x28, starting transfers between devices, passed_along(): return lax.ppermute(block, axis, route)  73.6 us
    ppermute x28, waiting for transfers between devices, passed_along(): return lax.ppermute(block, axis, route)  52.8 us
    pallas_call x6, Pallas kernels, gather_sends(): pl.pallas_call(send_kernel, grid=(planes,), in_specs=[planes_from(first,...  28.9 us
    pallas_call x1, Pallas kernels, relaxed(): pl.pallas_call(relax_kernel, grid=(rows // PLANE,), in_specs=[SMEM, SMEM,...  19.4 us
    psum x1, blocking collectives, local(): dist_sum = lax.psum(dist_sum, 'vel')  9.12 us
  transfers between devices with their start and end apart: 28, of which 7 were waited for; matrix products, arithmetic and copies ran while one was open for 1% of the time, Pallas kernels for 56%

profile of v1, /device:TPU:0, one launch (start us, length us, event | category | flops | bytes accessed | tf_op | source)
XLA Modules:
  0.0 414.4 jit_solution(180509144256145528)
XLA Ops:
  0.0 3.5 listed_cells.7
  3.5 0.5 collective-permute-start.4
  4.0 5.0 %collective-permute-start.5 = (f32[576,128]{1,0:T(8,128)}, f32[576,128]{1,0:T(8,128)S(1)}, u32[]{:S(2)}, u32[]{:S(2)}) collective-permute-start(f32[576,128]{1,0:T(8,128)} %get-tuple-element.50), channel_id=1, source_target_pairs={{2,0},{4,2},{6,4},{8,6},{10,8},{12,10},{14,12},{16,14},{18,16},{20... | collective-permute-start | bytes 884744 | tf_op jit(solution)/shard_map/ppermute | solution.py:31
  9.1 0.7 fusion
  9.8 0.0 collective-permute-start
  9.8 0.0 collective-permute-start.6
  9.8 6.2 %listed_cells.8 = (f32[1728,128]{1,0:T(8,128)}, f32[1728,128]{1,0:T(8,128)}, f32[1728,128]{1,0:T(8,128)}, f32[1728,128]{1,0:T(8,128)}) custom-call(f32[6912,512]{1,0:T(8,128)} %dist_ref.25, s32[4,128]{1,0:T(4,128)} %send_ref.11), custom_call_target="tpu_custom_call" | custom-call | flops 1811939328 | bytes 7077888 | tf_op jit(solution)/shard_map/listed_cells/pallas_call | solution.py:381
  16.0 1.7 collective-permute-start.10
  17.7 3.7 listed_cells.6
  21.4 0.0 collective-permute-done
  22.7 15.9 %collective-permute-start.1 = (f32[1,1]{1,0:T(1,128)}, f32[1,1]{1,0:T(1,128)}, u32[]{:S(2)}, u32[]{:S(2)}) collective-permute-start(f32[1,1]{1,0:T(1,128)} %min.12), channel_id=1, source_target_pairs={{28,0},{30,2},{0,4},{2,6},{4,8},{6,10},{8,12},{10,14},{12,16},{14,... | collective-permute-start | bytes 20 | tf_op jit(solution)/shard_map/ppermute | solution.py:31
  38.6 2.5 collective-permute-done.1
  41.8 1.4 collective-permute-start.2
  43.1 4.0 collective-permute-done.2
  47.8 1.4 collective-permute-start.3
  49.2 3.2 collective-permute-done.3
  52.4 1.2 collective-permute-start.11
  53.6 0.1 collective-permute-start.8
  53.7 0.0 collective-permute-done.5.refs_1_
  53.7 4.5 %collective-permute-start.9 = (f32[1728,128]{1,0:T(8,128)S(1)}, f32[1728,128]{1,0:T(8,128)S(1)}, u32[]{:S(2)}, u32[]{:S(2)}) collective-permute-start(f32[1728,128]{1,0:T(8,128)S(1)} %copy-done.21), channel_id=1, source_target_pairs={{2,0},{4,2},{6,4},{8,6},{10,8},{12,10},{14,12},{16,14},{18,16},{20... | collective-permute-start | bytes 2654216 | tf_op jit(solution)/shard_map/ppermute | solution.py:31
  58.2 4.1 broadcast_in_dim.2.stream_ref
  62.2 104.4 %near_faces.1 = (f32[6912,512]{1,0:T(8,128)}, f32[16,512]{1,0:T(8,128)}, f32[8,512]{1,0:T(8,128)}, bf16[512,3072]{1,0:T(8,128)(2,1)}) custom-call(s32[1]{0:T(128)} %bitcast.plane_ref, f32[6912,512]{1,0:T(8,128)} %dist_ref.25, f32[6912,128]{1,0:T(8,128)} %broadcast_in_dim.2.stream_ref, f32[18,512]{1,0:T(8,128)} %normal_ref.13, s32[6,512]{1,0:T(8,128)} %nbr_ref.1, ...), custom_call_target="tpu_custom_call" | custom-call | flops 43769659392 | bytes 28311552 | tf_op jit(solution)/shard_map/near_faces/pallas_call | solution.py:404
  166.7 0.0 copy-start.12
  166.7 0.1 collective-permute-start.7
  166.8 4.6 %listed_cells.10 = (f32[1152,128]{1,0:T(8,128)}, f32[1152,128]{1,0:T(8,128)}, f32[1152,128]{1,0:T(8,128)}, f32[1152,128]{1,0:T(8,128)}) custom-call(f32[6912,512]{1,0:T(8,128)} %dist_ref.25, s32[4,128]{1,0:T(4,128)} %send_ref.11), custom_call_target="tpu_custom_call" | custom-call | flops 1207959552 | bytes 4718592 | tf_op jit(solution)/shard_map/listed_cells/pallas_call | solution.py:381
  171.4 4.6 %listed_cells.11 = (f32[1152,128]{1,0:T(8,128)}, f32[1152,128]{1,0:T(8,128)}, f32[1152,128]{1,0:T(8,128)}, f32[1152,128]{1,0:T(8,128)}) custom-call(f32[6912,512]{1,0:T(8,128)} %dist_ref.25, s32[4,128]{1,0:T(4,128)} %send_ref.11), custom_call_target="tpu_custom_call" | custom-call | flops 1207959552 | bytes 4718592 | tf_op jit(solution)/shard_map/listed_cells/pallas_call | solution.py:381
  175.9 6.3 %listed_cells.9 = (f32[1728,128]{1,0:T(8,128)}, f32[1728,128]{1,0:T(8,128)}, f32[1728,128]{1,0:T(8,128)}, f32[1728,128]{1,0:T(8,128)}) custom-call(f32[6912,512]{1,0:T(8,128)} %dist_ref.25, s32[4,128]{1,0:T(4,128)} %send_ref.11), custom_call_target="tpu_custom_call" | custom-call | flops 1811939328 | bytes 7077888 | tf_op jit(solution)/shard_map/listed_cells/pallas_call | solution.py:381
  182.9 0.3 collective-permute-start.27
  183.2 0.4 copy-done.15
  183.6 11.2 %far_faces.6 = (f32[6912,512]{1,0:T(8,128)}, f32[8,512]{1,0:T(8,128)}) custom-call(s32[1]{0:T(128)} %bitcast.plane_ref, f32[1,1]{1,0:T(1,128)S(6)} %mul.23.time_ref, f32[6912,512]{1,0:T(8,128)} %dist_ref.25, f32[6912,512]{1,0:T(8,128)} %get-tuple-element.46.flux_ref, bf16[512,3072]{1,0:T(8,128)(2,1)} %get-tuple-element.47.far_ref, ...), custom_call_target="tpu_custom_call", output_to_operand_aliasing={{0}: (3, {})} | custom-call | flops 3635675136 | bytes 4718592 | tf_op jit(solution)/shard_map/far_faces/pallas_call | solution.py:446
  194.9 0.2 collective-permute-start.12
  195.1 4.3 %collective-permute-start.13 = (f32[1728,128]{1,0:T(8,128)}, f32[1728,128]{1,0:T(8,128)S(1)}, u32[]{:S(2)}, u32[]{:S(2)}) collective-permute-start(f32[1728,128]{1,0:T(8,128)} %get-tuple-element.62), channel_id=1, source_target_pairs={{2,0},{4,2},{6,4},{8,6},{10,8},{12,10},{14,12},{16,14},{18,16},{20... | collective-permute-start | bytes 2654216 | tf_op jit(solution)/shard_map/ppermute | solution.py:31
  199.4 4.7 %collective-permute-start.15 = (f32[1728,128]{1,0:T(8,128)S(1)}, f32[1728,128]{1,0:T(8,128)S(1)}, u32[]{:S(2)}, u32[]{:S(2)}) collective-permute-start(f32[1728,128]{1,0:T(8,128)S(1)} %copy-done.27), channel_id=1, source_target_pairs={{4,0},{6,2},{8,4},{10,6},{12,8},{14,10},{16,12},{18,14},{20,16},{2... | collective-permute-start | bytes 2654216 | tf_op jit(solution)/shard_map/ppermute | solution.py:31
  204.2 26.4 %far_faces.7 = (f32[6912,512]{1,0:T(8,128)}, f32[8,512]{1,0:T(8,128)}) custom-call(s32[1]{0:T(128)S(6)} %add.23.plane_ref, f32[1,1]{1,0:T(1,128)S(6)} %mul.23.time_ref, f32[6912,512]{1,0:T(8,128)} %dist_ref.25, f32[6912,512]{1,0:T(8,128)} %get-tuple-element.53.flux_ref, ...), custom_call_target="tpu_custom_call", output_to_operand_aliasing={{0}: (3, {})} | custom-call | flops 10907025408 | bytes 14155776 | tf_op jit(solution)/shard_map/far_faces/pallas_call | solution.py:446
  230.6 0.0 copy-start.28
  230.6 11.5 %collective-permute-start.16 = (f32[1152,128]{1,0:T(8,128)}, f32[1152,128]{1,0:T(8,128)S(1)}, u32[]{:S(2)}, u32[]{:S(2)}) collective-permute-start(f32[1152,128]{1,0:T(8,128)} %get-tuple-element.67), channel_id=1, source_target_pairs={{30,0},{0,2},{2,4},{4,6},{6,8},{8,10},{10,12},{12,14},{14,16},{16,... | collective-permute-start | bytes 1769480 | tf_op jit(solution)/shard_map/ppermute | solution.py:31
  242.1 0.9 copy-done.29
  243.1 11.5 %collective-permute-done.14.refs_2_ = f32[1728,128]{1,0:T(8,128)} collective-permute-done((f32[1728,128]{1,0:T(8,128)}, f32[1728,128]{1,0:T(8,128)}, u32[]{:S(2)}, u32[]{:S(2)}) %collective-permute-start.14) | collective-permute-done | bytes 884768 | tf_op jit(solution)/shard_map/ppermute | solution.py:31
  254.6 2.5 collective-permute-start.18
  257.1 20.7 %collective-permute-done.15.refs_3_ = f32[1728,128]{1,0:T(8,128)S(1)} collective-permute-done((f32[1728,128]{1,0:T(8,128)S(1)}, f32[1728,128]{1,0:T(8,128)S(1)}, u32[]{:S(2)}, u32[]{:S(2)}) %collective-permute-start.15) | collective-permute-done | bytes 884768 | tf_op jit(solution)/shard_map/ppermute | solution.py:31
  277.8 0.9 copy-done.30
  278.7 26.5 %far_faces.8 = (f32[6912,512]{1,0:T(8,128)}, f32[8,512]{1,0:T(8,128)}) custom-call(s32[1]{0:T(128)S(6)} %add.22.plane_ref, f32[1,1]{1,0:T(1,128)S(6)} %mul.23.time_ref, f32[6912,512]{1,0:T(8,128)} %dist_ref.25, f32[6912,512]{1,0:T(8,128)} %get-tuple-element.59.flux_ref, ...), custom_call_target="tpu_custom_call", output_to_operand_aliasing={{0}: (3, {})} | custom-call | flops 10907025408 | bytes 14155776 | tf_op jit(solution)/shard_map/far_faces/pallas_call | solution.py:446
  305.1 0.0 copy-start.1
  305.2 0.1 collective-permute-start.20
  305.2 4.4 %collective-permute-start.21 = (f32[1152,128]{1,0:T(8,128)}, f32[1152,128]{1,0:T(8,128)S(1)}, u32[]{:S(2)}, u32[]{:S(2)}) collective-permute-start(f32[1152,128]{1,0:T(8,128)} %get-tuple-element.74), channel_id=1, source_target_pairs={{2,0},{4,2},{6,4},{8,6},{10,8},{12,10},{14,12},{16,14},{18,16},{20... | collective-permute-start | bytes 1769480 | tf_op jit(solution)/shard_map/ppermute | solution.py:31
  309.7 0.1 collective-permute-start.22
  309.8 5.0 %collective-permute-start.23 = (f32[1152,128]{1,0:T(8,128)S(1)}, f32[1152,128]{1,0:T(8,128)S(1)}, u32[]{:S(2)}, u32[]{:S(2)}) collective-permute-start(f32[1152,128]{1,0:T(8,128)S(1)} %copy-done.31), channel_id=1, source_target_pairs={{4,0},{6,2},{8,4},{10,6},{12,8},{14,10},{16,12},{18,14},{20,16},{2... | collective-permute-start | bytes 1769480 | tf_op jit(solution)/shard_map/ppermute | solution.py:31
  314.8 19.1 %far_faces.9 = (f32[6912,512]{1,0:T(8,128)}, f32[8,512]{1,0:T(8,128)}) custom-call(s32[1]{0:T(128)S(6)} %add.21.plane_ref, f32[1,1]{1,0:T(1,128)S(6)} %mul.23.time_ref, f32[6912,512]{1,0:T(8,128)} %dist_ref.25, f32[6912,512]{1,0:T(8,128)} %get-tuple-element.65.flux_ref, ...), custom_call_target="tpu_custom_call", output_to_operand_aliasing={{0}: (3, {})} | custom-call | flops 7271350272 | bytes 9437184 | tf_op jit(solution)/shard_map/far_faces/pallas_call | solution.py:446
  333.9 0.0 copy-start.2
  333.9 6.5 %collective-permute-start.24 = (f32[576,128]{1,0:T(8,128)S(1)}, f32[576,128]{1,0:T(8,128)S(1)}, u32[]{:S(2)}, u32[]{:S(2)}) collective-permute-start(f32[576,128]{1,0:T(8,128)S(1)} %copy-done.35), channel_id=1, source_target_pairs={{30,0},{0,2},{2,4},{4,6},{6,8},{8,10},{10,12},{12,14},{14,16},{16,... | collective-permute-start | bytes 884744 | tf_op jit(solution)/shard_map/ppermute | solution.py:31
  340.4 0.1 collective-permute-start.25
  340.4 2.9 collective-permute-done.22.refs_2_
  343.4 2.5 collective-permute-start.26
  345.9 8.0 %collective-permute-done.23.refs_3_ = f32[1152,128]{1,0:T(8,128)S(1)} collective-permute-done((f32[1152,128]{1,0:T(8,128)S(1)}, f32[1152,128]{1,0:T(8,128)S(1)}, u32[]{:S(2)}, u32[]{:S(2)}) %collective-permute-start.23) | collective-permute-done | bytes 589856 | tf_op jit(solution)/shard_map/ppermute | solution.py:31
  353.8 0.8 copy-done.8
  354.7 19.1 %far_faces.10 = (f32[6912,512]{1,0:T(8,128)}, f32[8,512]{1,0:T(8,128)}) custom-call(s32[1]{0:T(128)S(6)} %add.20.plane_ref, f32[1,1]{1,0:T(1,128)S(6)} %mul.23.time_ref, f32[6912,512]{1,0:T(8,128)} %dist_ref.25, f32[6912,512]{1,0:T(8,128)} %get-tuple-element.71.flux_ref, ...), custom_call_target="tpu_custom_call", output_to_operand_aliasing={{0}: (3, {})} | custom-call | flops 7271350272 | bytes 9437184 | tf_op jit(solution)/shard_map/far_faces/pallas_call | solution.py:446
  373.8 0.0 copy-start.13
  373.8 0.6 copy-done.9
  374.5 0.1 copy-done.13
  374.6 0.1 copy-done.14
  374.6 0.1 copy-done.16
  374.8 11.2 %far_faces.11 = (f32[6912,512]{1,0:T(8,128)}, f32[8,512]{1,0:T(8,128)}) custom-call(s32[1]{0:T(128)S(6)} %add.19.plane_ref, f32[1,1]{1,0:T(1,128)S(6)} %mul.23.time_ref, f32[6912,512]{1,0:T(8,128)} %dist_ref.25, f32[6912,512]{1,0:T(8,128)} %get-tuple-element.77.flux_ref, ...), custom_call_target="tpu_custom_call", output_to_operand_aliasing={{0}: (3, {})} | custom-call | flops 3635675136 | bytes 4718592 | tf_op jit(solution)/shard_map/far_faces/pallas_call | solution.py:446
  385.9 9.1 %all-reduce = (f32[16,512]{1,0:T(8,128)}, f32[8,512]{1,0:T(8,128)}) all-reduce(f32[16,512]{1,0:T(8,128)S(1)} %copy-done.18, f32[8,512]{1,0:T(8,128)} %get-tuple-element.84), channel_id=1, replica_groups=mesh['space'=16,'vel'=2] {'vel'}, use_global_device_ids=true, to_apply=%region_3.0 | all-reduce | flops 12288 | bytes 98304 | tf_op jit(solution)/shard_map/psum | solution.py:536
  395.0 19.4 %relaxed.1 = f32[6912,512]{1,0:T(8,128)} custom-call(s32[1]{0:T(128)} %bitcast.plane_ref, f32[1,1]{1,0:T(1,128)S(6)} %mul.23.time_ref, f32[6912,512]{1,0:T(8,128)} %get-tuple-element.82.moved_ref, f32[16,512]{1,0:T(8,128)} %get-tuple-element.85.dist_sum_ref, f32[8,512]{1,0:T(8,128)} %get-tuple-element.86.flux_sum_ref, f32[1,512]{1,0:T(1,128)} %bitcast.9), custom_call_target="tpu_custom_call" | custom-call | flops 35389440 | bytes 28311552 | tf_op jit(solution)/shard_map/relaxed/pallas_call | solution.py:481
  (87 shorter events, 0.3 us)
Async XLA Ops:
  0.0 9.0 %copy-start = (f32[18,512]{1,0:T(8,128)S(1)}, f32[18,512]{1,0:T(8,128)}, u32[]{:S(2)}) copy-start(f32[18,512]{1,0:T(8,128)} %normal_ref.13) | copy-start | bytes 110596
  0.0 9.1 %copy-start.17 = (f32[512]{0:T(512)S(1)}, f32[512]{0:T(512)}, u32[]{:S(2)}) copy-start(f32[512]{0:T(512)} %param.10) | copy-start | bytes 6148
  3.5 50.1 %collective-permute-start.4 = (f32[576,128]{1,0:T(8,128)}, f32[576,128]{1,0:T(8,128)S(1)}, u32[]{:S(2)}, u32[]{:S(2)}) collective-permute-start(f32[576,128]{1,0:T(8,128)} %get-tuple-element.49), channel_id=1, source_target_pairs={{30,0},{0,2},{2,4},{4,6},{6,8},{8,10},{10,12},{12,14},{14,16},{16,... | collective-permute-start | bytes 884744 | tf_op jit(solution)/shard_map/ppermute | solution.py:31
  4.0 49.7 %collective-permute-start.5 = (f32[576,128]{1,0:T(8,128)}, f32[576,128]{1,0:T(8,128)S(1)}, u32[]{:S(2)}, u32[]{:S(2)}) collective-permute-start(f32[576,128]{1,0:T(8,128)} %get-tuple-element.50), channel_id=1, source_target_pairs={{2,0},{4,2},{6,4},{8,6},{10,8},{12,10},{14,12},{16,14},{18,16},{20... | collective-permute-start | bytes 884744 | tf_op jit(solution)/shard_map/ppermute | solution.py:31
  9.8 11.6 %collective-permute-start = (f32[1,1]{1,0:T(1,128)}, f32[1,1]{1,0:T(1,128)}, u32[]{:S(2)}, u32[]{:S(2)}) collective-permute-start(f32[1,1]{1,0:T(1,128)} %bitcast.1), channel_id=1, source_target_pairs={{30,0},{0,2},{2,4},{4,6},{6,8},{8,10},{10,12},{12,14},{14,16},{16,... | collective-permute-start | bytes 20 | tf_op jit(solution)/shard_map/ppermute | solution.py:31
  9.8 48.4 %copy-start.19 = (f32[6912]{0:T(1024)S(1)}, f32[6912]{0:T(1024)}, u32[]{:S(2)}) copy-start(f32[6912]{0:T(1024)} %param.8) | copy-start | bytes 82948
  9.8 156.9 %collective-permute-start.6 = (f32[576,128]{1,0:T(8,128)}, f32[576,128]{1,0:T(8,128)S(1)}, u32[]{:S(2)}, u32[]{:S(2)}) collective-permute-start(f32[576,128]{1,0:T(8,128)} %get-tuple-element.51), channel_id=1, source_target_pairs={{28,0},{30,2},{0,4},{2,6},{4,8},{6,10},{8,12},{10,14},{12,16},{14,... | collective-permute-start | bytes 884744 | tf_op jit(solution)/shard_map/ppermute | solution.py:31
  16.0 37.7 %copy-start.21 = (f32[1728,128]{1,0:T(8,128)S(1)}, f32[1728,128]{1,0:T(8,128)}, u32[]{:S(2)}) copy-start(f32[1728,128]{1,0:T(8,128)} %get-tuple-element.56) | copy-start | bytes 2654212
  16.0 178.8 %collective-permute-start.10 = (f32[1728,128]{1,0:T(8,128)}, f32[1728,128]{1,0:T(8,128)S(1)}, u32[]{:S(2)}, u32[]{:S(2)}) collective-permute-start(f32[1728,128]{1,0:T(8,128)} %get-tuple-element.57), channel_id=1, source_target_pairs={{28,0},{30,2},{0,4},{2,6},{4,8},{6,10},{8,12},{10,14},{12,16},{14,... | collective-permute-start | bytes 2654216 | tf_op jit(solution)/shard_map/ppermute | solution.py:31
  17.7 34.7 %copy-start.23 = (f32[1728,128]{1,0:T(8,128)S(1)}, f32[1728,128]{1,0:T(8,128)}, u32[]{:S(2)}) copy-start(f32[1728,128]{1,0:T(8,128)} %get-tuple-element.58) | copy-start | bytes 2654212
  17.7 35.9 %copy-start.22 = (f32[1728,128]{1,0:T(8,128)S(1)}, f32[1728,128]{1,0:T(8,128)}, u32[]{:S(2)}) copy-start(f32[1728,128]{1,0:T(8,128)} %get-tuple-element.55) | copy-start | bytes 2654212
  22.7 18.4 %collective-permute-start.1 = (f32[1,1]{1,0:T(1,128)}, f32[1,1]{1,0:T(1,128)}, u32[]{:S(2)}, u32[]{:S(2)}) collective-permute-start(f32[1,1]{1,0:T(1,128)} %min.12), channel_id=1, source_target_pairs={{28,0},{30,2},{0,4},{2,6},{4,8},{6,10},{8,12},{10,14},{12,16},{14,... | collective-permute-start | bytes 20 | tf_op jit(solution)/shard_map/ppermute | solution.py:31
  41.8 5.3 %collective-permute-start.2 = (f32[1,1]{1,0:T(1,128)}, f32[1,1]{1,0:T(1,128)}, u32[]{:S(2)}, u32[]{:S(2)}) collective-permute-start(f32[1,1]{1,0:T(1,128)} %min.13), channel_id=1, source_target_pairs={{24,0},{26,2},{28,4},{30,6},{0,8},{2,10},{4,12},{6,14},{8,16},{10,... | collective-permute-start | bytes 20 | tf_op jit(solution)/shard_map/ppermute | solution.py:31
  47.8 4.6 %collective-permute-start.3 = (f32[1,1]{1,0:T(1,128)}, f32[1,1]{1,0:T(1,128)}, u32[]{:S(2)}, u32[]{:S(2)}) collective-permute-start(f32[1,1]{1,0:T(1,128)} %min.14), channel_id=1, source_target_pairs={{16,0},{18,2},{20,4},{22,6},{24,8},{26,10},{28,12},{30,14},{0,16},... | collective-permute-start | bytes 20 | tf_op jit(solution)/shard_map/ppermute | solution.py:31
  52.4 142.6 %collective-permute-start.11 = (f32[1728,128]{1,0:T(8,128)S(1)}, f32[1728,128]{1,0:T(8,128)S(1)}, u32[]{:S(2)}, u32[]{:S(2)}) collective-permute-start(f32[1728,128]{1,0:T(8,128)S(1)} %copy-done.23), channel_id=1, source_target_pairs={{4,0},{6,2},{8,4},{10,6},{12,8},{14,10},{16,12},{18,14},{20,16},{2... | collective-permute-start | bytes 2654216 | tf_op jit(solution)/shard_map/ppermute | solution.py:31
  53.6 113.1 %copy-start.10 = (f32[576,128]{1,0:T(8,128)}, f32[576,128]{1,0:T(8,128)S(1)}, u32[]{:S(2)}) copy-start(f32[576,128]{1,0:T(8,128)S(1)} %collective-permute-done.4.refs_0_) | copy-start | bytes 884740
  53.6 145.8 %collective-permute-start.8 = (f32[1728,128]{1,0:T(8,128)S(1)}, f32[1728,128]{1,0:T(8,128)S(1)}, u32[]{:S(2)}, u32[]{:S(2)}) collective-permute-start(f32[1728,128]{1,0:T(8,128)S(1)} %copy-done.22), channel_id=1, source_target_pairs={{30,0},{0,2},{2,4},{4,6},{6,8},{8,10},{10,12},{12,14},{14,16},{16,... | collective-permute-start | bytes 2654216 | tf_op jit(solution)/shard_map/ppermute | solution.py:31
  53.7 113.0 %copy-start.11 = (f32[576,128]{1,0:T(8,128)}, f32[576,128]{1,0:T(8,128)S(1)}, u32[]{:S(2)}) copy-start(f32[576,128]{1,0:T(8,128)S(1)} %collective-permute-done.5.refs_1_) | copy-start | bytes 884740
  53.7 145.7 %collective-permute-start.9 = (f32[1728,128]{1,0:T(8,128)S(1)}, f32[1728,128]{1,0:T(8,128)S(1)}, u32[]{:S(2)}, u32[]{:S(2)}) collective-permute-start(f32[1728,128]{1,0:T(8,128)S(1)} %copy-done.21), channel_id=1, source_target_pairs={{2,0},{4,2},{6,4},{8,6},{10,8},{12,10},{14,12},{16,14},{18,16},{20... | collective-permute-start | bytes 2654216 | tf_op jit(solution)/shard_map/ppermute | solution.py:31
  62.2 104.5 %copy-start.36 = (f32[576,128]{1,0:T(8,128)S(1)}, f32[576,128]{1,0:T(8,128)}, u32[]{:S(2)}) copy-start(f32[576,128]{1,0:T(8,128)} %get-tuple-element.52) | copy-start | bytes 884740
  166.7 9.2 %copy-start.12 = (f32[576,128]{1,0:T(8,128)}, f32[576,128]{1,0:T(8,128)S(1)}, u32[]{:S(2)}) copy-start(f32[576,128]{1,0:T(8,128)S(1)} %collective-permute-done.6.refs_2_) | copy-start | bytes 884740
  166.7 16.2 %collective-permute-start.7 = (f32[576,128]{1,0:T(8,128)S(1)}, f32[576,128]{1,0:T(8,128)S(1)}, u32[]{:S(2)}, u32[]{:S(2)}) collective-permute-start(f32[576,128]{1,0:T(8,128)S(1)} %copy-done.36), channel_id=1, source_target_pairs={{4,0},{6,2},{8,4},{10,6},{12,8},{14,10},{16,12},{18,14},{20,16},{2... | collective-permute-start | bytes 884744 | tf_op jit(solution)/shard_map/ppermute | solution.py:31
  182.9 0.7 copy-start.15
  182.9 190.8 %collective-permute-start.27 = (f32[576,128]{1,0:T(8,128)}, f32[576,128]{1,0:T(8,128)S(1)}, u32[]{:S(2)}, u32[]{:S(2)}) collective-permute-start(f32[576,128]{1,0:T(8,128)} %get-tuple-element.45.after_ref), channel_id=1, source_target_pairs={{4,0},{6,2},{8,4},{10,6},{12,8},{14,10},{16,12},{18,14},{20,16},{2... | collective-permute-start | bytes 884744 | tf_op jit(solution)/shard_map/ppermute | solution.py:31
  183.6 15.8 %copy-start.27 = (f32[1728,128]{1,0:T(8,128)S(1)}, f32[1728,128]{1,0:T(8,128)}, u32[]{:S(2)}) copy-start(f32[1728,128]{1,0:T(8,128)} %get-tuple-element.64) | copy-start | bytes 2654212
  194.9 9.3 %copy-start.20 = (f32[1728,128]{1,0:T(8,128)}, f32[1728,128]{1,0:T(8,128)S(1)}, u32[]{:S(2)}) copy-start(f32[1728,128]{1,0:T(8,128)S(1)} %collective-permute-done.10.refs_2_) | copy-start | bytes 2654212
  194.9 35.7 %collective-permute-start.12 = (f32[1728,128]{1,0:T(8,128)}, f32[1728,128]{1,0:T(8,128)S(1)}, u32[]{:S(2)}, u32[]{:S(2)}) collective-permute-start(f32[1728,128]{1,0:T(8,128)} %get-tuple-element.61), channel_id=1, source_target_pairs={{30,0},{0,2},{2,4},{4,6},{6,8},{8,10},{10,12},{12,14},{14,16},{16,... | collective-permute-start | bytes 2654216 | tf_op jit(solution)/shard_map/ppermute | solution.py:31
  195.1 9.1 %copy-start.24 = (f32[1728,128]{1,0:T(8,128)}, f32[1728,128]{1,0:T(8,128)S(1)}, u32[]{:S(2)}) copy-start(f32[1728,128]{1,0:T(8,128)S(1)} %collective-permute-done.11.refs_3_) | copy-start | bytes 2654212
  195.1 47.1 %collective-permute-start.13 = (f32[1728,128]{1,0:T(8,128)}, f32[1728,128]{1,0:T(8,128)S(1)}, u32[]{:S(2)}, u32[]{:S(2)}) collective-permute-start(f32[1728,128]{1,0:T(8,128)} %get-tuple-element.62), channel_id=1, source_target_pairs={{2,0},{4,2},{6,4},{8,6},{10,8},{12,10},{14,12},{16,14},{18,16},{20... | collective-permute-start | bytes 2654216 | tf_op jit(solution)/shard_map/ppermute | solution.py:31
  199.4 4.8 %copy-start.25 = (f32[1728,128]{1,0:T(8,128)}, f32[1728,128]{1,0:T(8,128)S(1)}, u32[]{:S(2)}) copy-start(f32[1728,128]{1,0:T(8,128)S(1)} %collective-permute-done.8.refs_0_) | copy-start | bytes 2654212
  199.4 55.2 %collective-permute-start.14 = (f32[1728,128]{1,0:T(8,128)}, f32[1728,128]{1,0:T(8,128)}, u32[]{:S(2)}, u32[]{:S(2)}) collective-permute-start(f32[1728,128]{1,0:T(8,128)} %get-tuple-element.63), channel_id=1, source_target_pairs={{28,0},{30,2},{0,4},{2,6},{4,8},{6,10},{8,12},{10,14},{12,16},{14,... | collective-permute-start | bytes 2654216 | tf_op jit(solution)/shard_map/ppermute | solution.py:31
  199.4 4.8 %copy-start.26 = (f32[1728,128]{1,0:T(8,128)}, f32[1728,128]{1,0:T(8,128)S(1)}, u32[]{:S(2)}) copy-start(f32[1728,128]{1,0:T(8,128)S(1)} %collective-permute-done.9.refs_1_) | copy-start | bytes 2654212
  199.4 78.3 %collective-permute-start.15 = (f32[1728,128]{1,0:T(8,128)S(1)}, f32[1728,128]{1,0:T(8,128)S(1)}, u32[]{:S(2)}, u32[]{:S(2)}) collective-permute-start(f32[1728,128]{1,0:T(8,128)S(1)} %copy-done.27), channel_id=1, source_target_pairs={{4,0},{6,2},{8,4},{10,6},{12,8},{14,10},{16,12},{18,14},{20,16},{2... | collective-permute-start | bytes 2654216 | tf_op jit(solution)/shard_map/ppermute | solution.py:31
  230.6 47.2 %copy-start.28 = (f32[1728,128]{1,0:T(8,128)}, f32[1728,128]{1,0:T(8,128)S(1)}, u32[]{:S(2)}) copy-start(f32[1728,128]{1,0:T(8,128)S(1)} %collective-permute-done.12.refs_0_) | copy-start | bytes 2654212
  230.6 74.5 %collective-permute-start.16 = (f32[1152,128]{1,0:T(8,128)}, f32[1152,128]{1,0:T(8,128)S(1)}, u32[]{:S(2)}, u32[]{:S(2)}) collective-permute-start(f32[1152,128]{1,0:T(8,128)} %get-tuple-element.67), channel_id=1, source_target_pairs={{30,0},{0,2},{2,4},{4,6},{6,8},{8,10},{10,12},{12,14},{14,16},{16,... | collective-permute-start | bytes 1769480 | tf_op jit(solution)/shard_map/ppermute | solution.py:31
  242.1 0.9 copy-start.29
  243.1 62.2 %collective-permute-start.17 = (f32[1152,128]{1,0:T(8,128)}, f32[1152,128]{1,0:T(8,128)S(1)}, u32[]{:S(2)}, u32[]{:S(2)}) collective-permute-start(f32[1152,128]{1,0:T(8,128)} %get-tuple-element.68), channel_id=1, source_target_pairs={{2,0},{4,2},{6,4},{8,6},{10,8},{12,10},{14,12},{16,14},{18,16},{20... | collective-permute-start | bytes 1769480 | tf_op jit(solution)/shard_map/ppermute | solution.py:31
  254.6 55.1 %collective-permute-start.18 = (f32[1152,128]{1,0:T(8,128)}, f32[1152,128]{1,0:T(8,128)S(1)}, u32[]{:S(2)}, u32[]{:S(2)}) collective-permute-start(f32[1152,128]{1,0:T(8,128)} %get-tuple-element.69), channel_id=1, source_target_pairs={{28,0},{30,2},{0,4},{2,6},{4,8},{6,10},{8,12},{10,14},{12,16},{14,... | collective-permute-start | bytes 1769480 | tf_op jit(solution)/shard_map/ppermute | solution.py:31
  277.7 0.9 copy-start.30
  277.8 32.0 %collective-permute-start.19 = (f32[1152,128]{1,0:T(8,128)}, f32[1152,128]{1,0:T(8,128)S(1)}, u32[]{:S(2)}, u32[]{:S(2)}) collective-permute-start(f32[1152,128]{1,0:T(8,128)} %get-tuple-element.70), channel_id=1, source_target_pairs={{4,0},{6,2},{8,4},{10,6},{12,8},{14,10},{16,12},{18,14},{20,16},{2... | collective-permute-start | bytes 1769480 | tf_op jit(solution)/shard_map/ppermute | solution.py:31
  278.7 31.0 %copy-start.32 = (f32[1152,128]{1,0:T(8,128)S(1)}, f32[1152,128]{1,0:T(8,128)}, u32[]{:S(2)}) copy-start(f32[1152,128]{1,0:T(8,128)} %get-tuple-element.75) | copy-start | bytes 1769476
  278.7 31.1 %copy-start.31 = (f32[1152,128]{1,0:T(8,128)S(1)}, f32[1152,128]{1,0:T(8,128)}, u32[]{:S(2)}) copy-start(f32[1152,128]{1,0:T(8,128)} %get-tuple-element.76) | copy-start | bytes 1769476
  305.1 9.6 %copy-start.1 = (f32[1152,128]{1,0:T(8,128)}, f32[1152,128]{1,0:T(8,128)S(1)}, u32[]{:S(2)}) copy-start(f32[1152,128]{1,0:T(8,128)S(1)} %collective-permute-done.16.refs_0_) | copy-start | bytes 1769476
  305.2 28.7 %collective-permute-start.20 = (f32[1152,128]{1,0:T(8,128)}, f32[1152,128]{1,0:T(8,128)S(1)}, u32[]{:S(2)}, u32[]{:S(2)}) collective-permute-start(f32[1152,128]{1,0:T(8,128)} %get-tuple-element.73), channel_id=1, source_target_pairs={{30,0},{0,2},{2,4},{4,6},{6,8},{8,10},{10,12},{12,14},{14,16},{16,... | collective-permute-start | bytes 1769480 | tf_op jit(solution)/shard_map/ppermute | solution.py:31
  305.2 9.5 %copy-start.3 = (f32[1152,128]{1,0:T(8,128)}, f32[1152,128]{1,0:T(8,128)S(1)}, u32[]{:S(2)}) copy-start(f32[1152,128]{1,0:T(8,128)S(1)} %collective-permute-done.17.refs_1_) | copy-start | bytes 1769476
  305.2 35.1 %collective-permute-start.21 = (f32[1152,128]{1,0:T(8,128)}, f32[1152,128]{1,0:T(8,128)S(1)}, u32[]{:S(2)}, u32[]{:S(2)}) collective-permute-start(f32[1152,128]{1,0:T(8,128)} %get-tuple-element.74), channel_id=1, source_target_pairs={{2,0},{4,2},{6,4},{8,6},{10,8},{12,10},{14,12},{16,14},{18,16},{20... | collective-permute-start | bytes 1769480 | tf_op jit(solution)/shard_map/ppermute | solution.py:31
  309.7 5.1 %copy-start.5 = (f32[1152,128]{1,0:T(8,128)}, f32[1152,128]{1,0:T(8,128)S(1)}, u32[]{:S(2)}) copy-start(f32[1152,128]{1,0:T(8,128)S(1)} %collective-permute-done.18.refs_2_) | copy-start | bytes 1769476
  309.7 33.7 %collective-permute-start.22 = (f32[1152,128]{1,0:T(8,128)S(1)}, f32[1152,128]{1,0:T(8,128)S(1)}, u32[]{:S(2)}, u32[]{:S(2)}) collective-permute-start(f32[1152,128]{1,0:T(8,128)S(1)} %copy-done.32), channel_id=1, source_target_pairs={{28,0},{30,2},{0,4},{2,6},{4,8},{6,10},{8,12},{10,14},{12,16},{14,... | collective-permute-start | bytes 1769480 | tf_op jit(solution)/shard_map/ppermute | solution.py:31
  309.7 5.0 %copy-start.7 = (f32[1152,128]{1,0:T(8,128)}, f32[1152,128]{1,0:T(8,128)S(1)}, u32[]{:S(2)}) copy-start(f32[1152,128]{1,0:T(8,128)S(1)} %collective-permute-done.19.refs_3_) | copy-start | bytes 1769476
  309.8 44.1 %collective-permute-start.23 = (f32[1152,128]{1,0:T(8,128)S(1)}, f32[1152,128]{1,0:T(8,128)S(1)}, u32[]{:S(2)}, u32[]{:S(2)}) collective-permute-start(f32[1152,128]{1,0:T(8,128)S(1)} %copy-done.31), channel_id=1, source_target_pairs={{4,0},{6,2},{8,4},{10,6},{12,8},{14,10},{16,12},{18,14},{20,16},{2... | collective-permute-start | bytes 1769480 | tf_op jit(solution)/shard_map/ppermute | solution.py:31
  314.7 19.1 %copy-start.35 = (f32[576,128]{1,0:T(8,128)S(1)}, f32[576,128]{1,0:T(8,128)}, u32[]{:S(2)}) copy-start(f32[576,128]{1,0:T(8,128)} %get-tuple-element.79) | copy-start | bytes 884740
  314.7 25.6 %copy-start.34 = (f32[576,128]{1,0:T(8,128)S(1)}, f32[576,128]{1,0:T(8,128)}, u32[]{:S(2)}) copy-start(f32[576,128]{1,0:T(8,128)} %get-tuple-element.80) | copy-start | bytes 884740
  314.8 28.6 %copy-start.33 = (f32[576,128]{1,0:T(8,128)S(1)}, f32[576,128]{1,0:T(8,128)}, u32[]{:S(2)}) copy-start(f32[576,128]{1,0:T(8,128)} %get-tuple-element.81) | copy-start | bytes 884740
  333.9 20.0 %copy-start.2 = (f32[1152,128]{1,0:T(8,128)}, f32[1152,128]{1,0:T(8,128)S(1)}, u32[]{:S(2)}) copy-start(f32[1152,128]{1,0:T(8,128)S(1)} %collective-permute-done.20.refs_0_) | copy-start | bytes 1769476
  333.9 39.9 %collective-permute-start.24 = (f32[576,128]{1,0:T(8,128)S(1)}, f32[576,128]{1,0:T(8,128)S(1)}, u32[]{:S(2)}, u32[]{:S(2)}) collective-permute-start(f32[576,128]{1,0:T(8,128)S(1)} %copy-done.35), channel_id=1, source_target_pairs={{30,0},{0,2},{2,4},{4,6},{6,8},{8,10},{10,12},{12,14},{14,16},{16,... | collective-permute-start | bytes 884744 | tf_op jit(solution)/shard_map/ppermute | solution.py:31
  340.3 13.5 %copy-start.4 = (f32[1152,128]{1,0:T(8,128)}, f32[1152,128]{1,0:T(8,128)S(1)}, u32[]{:S(2)}) copy-start(f32[1152,128]{1,0:T(8,128)S(1)} %collective-permute-done.21.refs_1_) | copy-start | bytes 1769476
  340.4 33.4 %collective-permute-start.25 = (f32[576,128]{1,0:T(8,128)S(1)}, f32[576,128]{1,0:T(8,128)S(1)}, u32[]{:S(2)}, u32[]{:S(2)}) collective-permute-start(f32[576,128]{1,0:T(8,128)S(1)} %copy-done.34), channel_id=1, source_target_pairs={{2,0},{4,2},{6,4},{8,6},{10,8},{12,10},{14,12},{16,14},{18,16},{20... | collective-permute-start | bytes 884744 | tf_op jit(solution)/shard_map/ppermute | solution.py:31
  343.4 10.5 %copy-start.6 = (f32[1152,128]{1,0:T(8,128)}, f32[1152,128]{1,0:T(8,128)S(1)}, u32[]{:S(2)}) copy-start(f32[1152,128]{1,0:T(8,128)S(1)} %collective-permute-done.22.refs_2_) | copy-start | bytes 1769476
  343.4 30.4 %collective-permute-start.26 = (f32[576,128]{1,0:T(8,128)S(1)}, f32[576,128]{1,0:T(8,128)S(1)}, u32[]{:S(2)}, u32[]{:S(2)}) collective-permute-start(f32[576,128]{1,0:T(8,128)S(1)} %copy-done.33), channel_id=1, source_target_pairs={{28,0},{30,2},{0,4},{2,6},{4,8},{6,10},{8,12},{10,14},{12,16},{14,... | collective-permute-start | bytes 884744 | tf_op jit(solution)/shard_map/ppermute | solution.py:31
  353.8 0.8 copy-start.8
  373.8 0.8 copy-start.13
  373.8 0.8 copy-start.14
  373.8 0.9 copy-start.16
  374.7 11.2 %copy-start.18 = (f32[16,512]{1,0:T(8,128)S(1)}, f32[16,512]{1,0:T(8,128)}, u32[]{:S(2)}) copy-start(f32[16,512]{1,0:T(8,128)} %get-tuple-element.83) | copy-start | bytes 98308
  (1 other events, 0.7 us)

commit v2 on v0

v2 whole, which is shorter than its diff:
```python
import functools
import math

import jax
import jax.numpy as jnp
from jax import lax
from jax.experimental import pallas as pl
from jax.experimental.pallas import tpu as pltpu
from jax.sharding import PartitionSpec as P

NODES = 24
PLANE = NODES * NODES
HALF = (NODES - 1) / 2.0
FACES = 6
CFL = 0.9
MU_REF = 60.0
OMEGA = 0.81
PRANDTL = 2.0 / 3.0
neighbour_steps = (1, -1, 2, -2)

LANES = 128
SUB = 8
F32 = jnp.float32
VMEM_LIMIT = 60 * 1024 * 1024


def passed_along(block, axis, distance):
    count = lax.axis_size(axis)
    route = [((i - distance) % count, i) for i in range(count)]
    return lax.ppermute(block, axis, route)


def swapped(block, axis, start):
    count = lax.axis_size(axis)
    route = []
    for i in range(start, start + count, 2):
        route += [(i % count, (i + 1) % count), ((i + 1) % count, i % count)]
    return lax.ppermute(block, axis, route)


def summed_over(value, axis):
    count = lax.axis_size(axis)
    if count & (count - 1):
        return lax.psum(value, axis)
    reach = 1
    while reach < count:
        value = value + lax.ppermute(value, axis, [(i, i ^ reach) for i in range(count)])
        reach *= 2
    return value


def tiles_of(rows, i):
    return min(SUB, -(-rows // LANES) - i * SUB)


def turn(dist_ref, turned_ref):
    cells = dist_ref.shape[1]
    for s in range(SUB):
        for t in range(cells // LANES):
            block = dist_ref[s * LANES : (s + 1) * LANES, t * LANES : (t + 1) * LANES]
            turned_ref[pl.ds(t * LANES * SUB + s, LANES, stride=SUB), :] = block.T


def pick_rows(list_ref, row, turned_ref, picked_ref, out_ref):
    width = out_ref.shape[1]

    @pl.loop(0, width, unroll=8)
    def _(j):
        source = pl.ds(pl.multiple_of(list_ref[row, j] * SUB, SUB), SUB)
        picked_ref[pl.ds(pl.multiple_of(j * SUB, SUB), SUB), :] = turned_ref[source, :]

    for s in range(out_ref.shape[0]):
        out_ref[s] = picked_ref[pl.ds(s, width, stride=SUB), :]


def pick_lists(place_ref, list_ref, turned_ref, picked_ref, cross_ref, ahead_ref, back_ref):
    pick_rows(list_ref, 1 - place_ref[1], turned_ref, picked_ref, cross_ref)
    pick_rows(list_ref, 2, turned_ref, picked_ref, ahead_ref)
    pick_rows(list_ref, 3, turned_ref, picked_ref, back_ref)


def first_send_kernel(place_ref, list_ref, dist_ref, cross_ref, ahead_ref, back_ref, turned_ref, picked_ref):
    turn(dist_ref, turned_ref)
    pick_lists(place_ref, list_ref, turned_ref, picked_ref, cross_ref, ahead_ref, back_ref)


def send_kernel(place_ref, list_ref, turned_ref, after_ref, cross_ref, ahead_ref, back_ref, picked_ref):
    pick_lists(place_ref, list_ref, turned_ref.at[0], picked_ref, cross_ref, ahead_ref, back_ref)


def turn_kernel(place_ref, list_ref, dist_ref, after_ref, turned_ref, pair_ref, picked_ref):
    turn(dist_ref, turned_ref.at[0])
    pick_rows(list_ref, place_ref[1], turned_ref.at[0], picked_ref, pair_ref)


def rows8(row):
    return jnp.broadcast_to(row, (SUB, row.shape[-1]))


def last_speeds():
    index = lax.broadcasted_iota(jnp.int32, (SUB, LANES), 0).astype(F32) - HALF
    return [index + float(j * SUB) for j in range(NODES // SUB)]


def z_sums(tiles, speeds, powers):
    sums, terms = [], list(tiles)
    for p in range(powers):
        if p:
            terms = [t * c for t, c in zip(terms, speeds)]
        sums.append(terms[0] + terms[1] + terms[2])
    return sums


def rest_of_moments(sums, first):
    energy = 0.5 * (first * first * sums[0, 0] + sums[0, 1 + 1] + sums[2, 0])
    return [sums[0, 0], first * sums[0, 0], sums[0, 1], sums[1, 0], energy]


def add_rows(acc_ref, values, lanes):
    for m, value in enumerate(values):
        acc_ref[m * SUB : (m + 1) * SUB, lanes] += value


def sum_rows(acc_ref, count):
    return [jnp.sum(acc_ref[m * SUB : (m + 1) * SUB, :], axis=0, keepdims=True) for m in range(count)]


FLUX_KEYS = ((0, 0), (0, 1), (0, 2), (1, 0), (2, 0))
DIST_KEYS = ((0, 0), (0, 1), (0, 2), (0, 3), (1, 0), (1, 1), (1, 2), (2, 0), (2, 1), (3, 0))


def grow(carry, keys, sums, second):
    powers = [None, second, second * second, second * second * second]
    return tuple(
        c + (sums[i] if j == 0 else sums[i] * powers[j]) for c, (i, j) in zip(carry, keys)
    )


def moment_kernel(place_ref, dist_ref, after_ref, dist_sum_ref, zero_ref, dist_acc):
    step = pl.program_id(0)
    cells = dist_ref.shape[1]

    @pl.when(step == 0)
    def _():
        dist_acc[...] = jnp.zeros_like(dist_acc)

    speeds = last_speeds()
    tiles = range(NODES // SUB)
    first = (place_ref[0] + step).astype(F32) - HALF
    for t in range(cells // LANES):
        lanes = slice(t * LANES, (t + 1) * LANES)

        def body(y, carry, lanes=lanes):
            second = y.astype(F32) - HALF
            rows = [pl.ds(pl.multiple_of(y * NODES + j * SUB, SUB), SUB) for j in tiles]
            own = [dist_ref[r, lanes] for r in rows]
            return grow(carry, DIST_KEYS, z_sums(own, speeds, 4), second)

        zero = jnp.zeros((SUB, LANES), F32)
        part = lax.fori_loop(0, NODES, body, (zero,) * len(DIST_KEYS), unroll=4)
        s = dict(zip(DIST_KEYS, part))
        square = first * first
        add_rows(
            dist_acc,
            rest_of_moments(s, first)
            + [
                square * s[0, 0], s[0, 2], s[2, 0],
                first * s[0, 1], first * s[1, 0], s[1, 1],
                first * (square * s[0, 0] + s[0, 2] + s[2, 0]),
                square * s[0, 1] + s[0, 3] + s[2, 1],
                square * s[1, 0] + s[1, 2] + s[3, 0],
            ],
            lanes,
        )

    @pl.when(step == pl.num_programs(0) - 1)
    def _():
        dist_sum_ref[...] = jnp.concatenate(
            sum_rows(dist_acc, 14) + [jnp.zeros((2, cells), F32)], axis=0
        )
        zero_ref[...] = jnp.zeros_like(zero_ref)


def speeds_at(index):
    first = jnp.floor((index + 0.5) * (1.0 / PLANE))
    rest = index - PLANE * first
    second = jnp.floor((rest + 0.5) * (1.0 / NODES))
    return first - HALF, second - HALF, rest - NODES * second - HALF


def face_kernel(
    rows, start, place_ref, time_ref, index_ref, normal_ref, stream_ref, dist_ref, turned_ref,
    volume_ref, before_ref, pair_ref, cross_ref, ahead_ref, back_ref, *refs,
):
    moved_ref, flux_sum_ref, table_ref, flux_ref, flux_acc, ratio_ref = refs[-6:]
    cells, width = dist_ref.shape[1], pair_ref.shape[1]
    odd = place_ref[1]

    table_ref[0 : cells * SUB, :] = turned_ref[0]
    for block_ref, slot in ((pair_ref, 1 - odd), (cross_ref, odd), (ahead_ref, 2), (back_ref, 3)):
        for s in range(cross_ref.shape[0]):
            base = (cells + slot * width) * SUB + s
            table_ref[pl.ds(base, width, stride=SUB), :] = block_ref[s]
    inflow = cells + 4 * width
    table_ref[inflow * SUB : (inflow + 1) * SUB, :] = stream_ref[...]

    at = lax.broadcasted_iota(jnp.int32, (SUB, LANES), 0) * LANES
    at = at + lax.broadcasted_iota(jnp.int32, (SUB, LANES), 1) + (place_ref[0] * PLANE + start)
    speeds = speeds_at(at.astype(F32))

    @pl.loop(0, cells, unroll=4)
    def _(c):
        own = table_ref[pl.ds(pl.multiple_of(c * SUB, SUB), SUB), :]
        acc = low = full = None
        for k in range(FACES):
            source = pl.ds(pl.multiple_of(index_ref[k, c], SUB), SUB)
            normal = [normal_ref[3 * k + a, c] for a in range(3)]
            speed = speeds[0] * normal[0] + speeds[1] * normal[1] + speeds[2] * normal[2]
            inward = jnp.minimum(speed, 0.0)
            part = inward * table_ref[source, :]
            acc = part if k == 0 else acc + part
            low = inward if k == 0 else low + inward
            full = speed if k == 0 else full + speed
        flux_ref[pl.ds(pl.multiple_of(c * SUB, SUB), SUB), :] = acc + (full - low) * own

    ratio_ref[...] = rows8(time_ref[0, 0] / volume_ref[...])
    flux_acc[...] = jnp.zeros_like(flux_acc)
    for s in range(cross_ref.shape[0]):
        for t in range(cells // LANES):
            lanes = slice(t * LANES, (t + 1) * LANES)
            block = flux_ref[pl.ds(t * LANES * SUB + s, LANES, stride=SUB), :].T
            ratio = ratio_ref[:, lanes]
            sums = [None] * 5
            for r in range(LANES // SUB):
                row = s * LANES + r * SUB
                flux = block[r * SUB : (r + 1) * SUB, :]
                moved_ref[row : row + SUB, lanes] = dist_ref[row : row + SUB, lanes] - ratio * flux
                if start + row >= rows:
                    continue
                index = lax.broadcasted_iota(jnp.int32, (SUB, LANES), 0) + (
                    place_ref[0] * PLANE + start + row
                )
                c = speeds_at(index.astype(F32))
                square = 0.5 * (c[0] * c[0] + c[1] * c[1] + c[2] * c[2])
                parts = [flux, c[0] * flux, c[1] * flux, c[2] * flux, square * flux]
                sums = [p if q is None else q + p for q, p in zip(sums, parts)]
            if sums[0] is not None:
                add_rows(flux_acc, sums, lanes)
    flux_sum_ref[...] = before_ref[...] + jnp.concatenate(
        sum_rows(flux_acc, 5) + [jnp.zeros((3, cells), F32)], axis=0
    )


def hydrodynamic_variables(moments):
    density = moments[0]
    mean = [moments[1 + axis] / density for axis in range(3)]
    square = mean[0] ** 2 + mean[1] ** 2 + mean[2] ** 2
    return density, mean, (2.0 * moments[4] / density - square) / 3.0


def relax_kernel(
    planes, place_ref, time_ref, moved_ref, dist_sum_ref, flux_sum_ref, volume_ref, out_ref,
    x_ref, y_ref, z_ref, cell_ref,
):
    step = pl.program_id(0)
    cells = moved_ref.shape[1]

    @pl.when(step == 0)
    def _():
        time_step = time_ref[0, 0]
        ratio = time_step / volume_ref[...]
        sums = [dist_sum_ref[m : m + 1, :] for m in range(14)]
        density, mean, _ = hydrodynamic_variables(sums)
        xx, yy, zz, xy, xz, yz = sums[5:11]
        pairs = ((xx, xy, xz), (xy, yy, yz), (xz, yz, zz))
        square = mean[0] ** 2 + mean[1] ** 2 + mean[2] ** 2
        heat = []
        for a in range(3):
            cross = mean[0] * pairs[a][0] + mean[1] * pairs[a][1] + mean[2] * pairs[a][2]
            heat.append(
                0.5
                * (
                    sums[11 + a] - mean[a] * (2.0 * sums[4]) - 2.0 * cross
                    + 2.0 * mean[a] * square * density
                )
            )
        new = [sums[m] - ratio * flux_sum_ref[m : m + 1, :] for m in range(5)]
        density, mean, temp = hydrodynamic_variables(new)
        relax_time = MU_REF * jnp.exp(OMEGA * jnp.log(temp)) / (density * temp)
        relax = time_step / relax_time
        keep = 1.0 / (1.0 + relax)
        root = lax.rsqrt(2.0 * math.pi * temp)
        front = relax * keep * density * root * root * root
        along = (1.0 - PRANDTL) / (5.0 * density * temp * temp)
        for m, row in enumerate((keep, mean[0], temp, heat[0] * along, front)):
            cell_ref[m * SUB : (m + 1) * SUB, :] = rows8(row)
        nodes = lax.broadcasted_iota(jnp.int32, (NODES, cells), 0).astype(F32) - HALF
        for a, ref in ((1, y_ref), (2, z_ref)):
            rel = nodes - mean[a]
            square = rel * rel / temp
            for i, table in enumerate((jnp.exp(-0.5 * square), square, rel * heat[a] * along)):
                if a == 2:
                    ref[i * NODES : (i + 1) * NODES, :] = table
                    continue
                for y in range(NODES):
                    ref[i, y] = rows8(table[y : y + 1, :])

    keep, mean, temp, heat, front = [
        cell_ref[m * SUB : (m + 1) * SUB, :] for m in range(5)
    ]
    for p in range(planes):
        rel = (place_ref[0] + step * planes + p).astype(F32) - HALF - mean
        square = rel * rel / temp
        x_ref[0] = front * jnp.exp(-0.5 * square)
        x_ref[1] = square - 5.0
        x_ref[2] = rel * heat

        @pl.loop(0, NODES, unroll=2)
        def _(y, p=p):
            for t in range(cells // LANES):
                lanes = slice(t * LANES, (t + 1) * LANES)
                peak = x_ref[0, :, lanes] * y_ref[0, y, :, lanes]
                square = x_ref[1, :, lanes] + y_ref[1, y, :, lanes]
                along = x_ref[2, :, lanes] + y_ref[2, y, :, lanes]
                for j in range(NODES // SUB):
                    row = pl.ds(pl.multiple_of(p * PLANE + y * NODES + j * SUB, SUB), SUB)
                    z = [
                        z_ref[i * NODES + j * SUB : i * NODES + (j + 1) * SUB, lanes]
                        for i in range(3)
                    ]
                    shape = (along + z[2]) * (square + z[1]) + 1.0
                    moved = moved_ref[row, lanes] * cell_ref[0:SUB, lanes]
                    out_ref[row, lanes] = moved + peak * z[0] * shape


def params():
    return pltpu.CompilerParams(
        vmem_limit_bytes=VMEM_LIMIT, dimension_semantics=("arbitrary",)
    )


def whole(*shape):
    return pl.BlockSpec(shape, lambda i: (0,) * len(shape))


def planes_from(first, width, planes=1):
    return pl.BlockSpec((planes * PLANE, width), lambda i: (first // planes + i, 0))


SMEM = pl.BlockSpec(memory_space=pltpu.SMEM)
ANY = pl.BlockSpec(memory_space=pl.ANY)


def first_sends(place, lists, dist):
    cells, width = dist.shape[1], lists.shape[1]
    tiles = tiles_of(dist.shape[0], 0)
    block = SUB * LANES
    return pl.pallas_call(
        first_send_kernel,
        grid=(1,),
        in_specs=[SMEM, SMEM, pl.BlockSpec((block, cells), lambda i: (0, 0))],
        out_specs=[whole(tiles, width, LANES)] * 3,
        out_shape=[jax.ShapeDtypeStruct((tiles, width, LANES), F32)] * 3,
        scratch_shapes=[pltpu.VMEM((cells * SUB, LANES), F32), pltpu.VMEM((width * SUB, LANES), F32)],
        compiler_params=params(),
        cost_estimate=pl.CostEstimate(
            flops=0, bytes_accessed=4 * block * (cells + 3 * width), transcendentals=0
        ),
        name="first_sends",
    )(place, lists, dist)


def turned_cells(place, lists, dist, after):
    (rows, cells), width = dist.shape, lists.shape[1]
    block = SUB * LANES
    rounds = -(-rows // block)
    return pl.pallas_call(
        turn_kernel,
        grid=(rounds,),
        in_specs=[SMEM, SMEM, pl.BlockSpec((block, cells), lambda i: (i, 0)), ANY],
        out_specs=[
            pl.BlockSpec((1, cells * SUB, LANES), lambda i: (i, 0, 0)),
            pl.BlockSpec((SUB, width, LANES), lambda i: (i, 0, 0)),
        ],
        out_shape=[
            jax.ShapeDtypeStruct((rounds, cells * SUB, LANES), F32),
            jax.ShapeDtypeStruct((-(-rows // LANES), width, LANES), F32),
        ],
        scratch_shapes=[pltpu.VMEM((width * SUB, LANES), F32)],
        compiler_params=params(),
        cost_estimate=pl.CostEstimate(
            flops=0, bytes_accessed=4 * rows * (2 * cells + width), transcendentals=0
        ),
        name="turned_cells",
    )(place, lists, dist, after)


def later_sends(place, lists, turned, i, tiles, after):
    height, width = turned.shape[1], lists.shape[1]
    return pl.pallas_call(
        send_kernel,
        grid=(1,),
        in_specs=[SMEM, SMEM, pl.BlockSpec((1, height, LANES), lambda _: (i, 0, 0)), ANY],
        out_specs=[whole(tiles, width, LANES)] * 3,
        out_shape=[jax.ShapeDtypeStruct((tiles, width, LANES), F32)] * 3,
        scratch_shapes=[pltpu.VMEM((width * SUB, LANES), F32)],
        compiler_params=params(),
        cost_estimate=pl.CostEstimate(
            flops=0, bytes_accessed=4 * LANES * (height + 3 * tiles * width), transcendentals=0
        ),
        name="later_sends",
    )(place, lists, turned, after)


def dist_moments(place, dist, after):
    rows, cells = dist.shape
    return pl.pallas_call(
        moment_kernel,
        grid=(rows // PLANE,),
        in_specs=[SMEM, planes_from(0, cells), ANY],
        out_specs=[whole(16, cells), whole(8, cells)],
        out_shape=[
            jax.ShapeDtypeStruct((16, cells), F32),
            jax.ShapeDtypeStruct((8, cells), F32),
        ],
        scratch_shapes=[pltpu.VMEM((14 * SUB, cells), F32)],
        compiler_params=params(),
        cost_estimate=pl.CostEstimate(
            flops=30 * rows * cells, bytes_accessed=4 * rows * cells, transcendentals=0
        ),
        name="dist_moments",
    )(place, dist, after)


def face_sums(place, time_step, index, normals, stream, dist, turned, volume, before, moved, pair, arrived, i):
    rows, cells = dist.shape
    width = pair.shape[1]
    tiles = arrived[0].shape[0]
    block = SUB * LANES
    extra, aliases = ((), {}) if moved is None else ((moved,), {13: 0})
    return pl.pallas_call(
        functools.partial(face_kernel, rows, i * block),
        grid=(1,),
        in_specs=[
            SMEM, SMEM, SMEM, SMEM,
            pl.BlockSpec((SUB, LANES), lambda _: (i, 0)),
            pl.BlockSpec((block, cells), lambda _: (i, 0)),
            pl.BlockSpec((1, cells * SUB, LANES), lambda _: (i, 0, 0)),
            whole(1, cells), whole(8, cells),
            pl.BlockSpec((SUB, width, LANES), lambda _: (i, 0, 0)),
        ]
        + [whole(tiles, width, LANES)] * 3
        + [ANY] * len(extra),
        out_specs=[pl.BlockSpec((block, cells), lambda _: (i, 0)), whole(8, cells)],
        out_shape=[
            jax.ShapeDtypeStruct((rows, cells), F32),
            jax.ShapeDtypeStruct((8, cells), F32),
        ],
        scratch_shapes=[
            pltpu.VMEM(((cells + 4 * width + 1) * SUB, LANES), F32),
            pltpu.VMEM((cells * SUB, LANES), F32),
            pltpu.VMEM((5 * SUB, cells), F32),
            pltpu.VMEM((SUB, cells), F32),
        ],
        input_output_aliases=aliases,
        compiler_params=params(),
        cost_estimate=pl.CostEstimate(
            flops=70 * block * cells,
            bytes_accessed=4 * block * (3 * cells + 4 * width),
            transcendentals=0,
        ),
        name="face_sums",
    )(place, time_step, index, normals, stream, dist, turned, volume, before, pair, *arrived, *extra)


def step_planes(planes):
    return 2 - planes % 2


def relaxed(place, time_step, moved, dist_sum, flux_sum, volume):
    rows, cells = moved.shape
    planes = step_planes(rows // PLANE)
    return pl.pallas_call(
        functools.partial(relax_kernel, planes),
        grid=(rows // PLANE // planes,),
        in_specs=[
            SMEM, SMEM, planes_from(0, cells, planes), whole(16, cells), whole(8, cells),
            whole(1, cells),
        ],
        out_specs=planes_from(0, cells, planes),
        out_shape=jax.ShapeDtypeStruct((rows, cells), F32),
        scratch_shapes=[
            pltpu.VMEM((3, SUB, cells), F32),
            pltpu.VMEM((3, NODES, SUB, cells), F32),
            pltpu.VMEM((3 * NODES, cells), F32),
            pltpu.VMEM((5 * SUB, cells), F32),
        ],
        compiler_params=params(),
        cost_estimate=pl.CostEstimate(
            flops=10 * rows * cells, bytes_accessed=8 * rows * cells, transcendentals=0
        ),
        name="relaxed",
    )(place, time_step, moved, dist_sum, flux_sum, volume)


def local(dist, free_stream, area_normal, cell_volume, face_nbr, face_type, send_list):
    rows, cells = dist.shape
    planes = rows // PLANE
    dirs, width = send_list.shape
    block = SUB * LANES
    rounds = -(-rows // block)
    place = jnp.stack([lax.axis_index("vel") * planes, lax.axis_index("space") % 2]).astype(jnp.int32)

    def sent(blocks):
        return (
            swapped(blocks[0], "space", 1),
            passed_along(blocks[1], "space", neighbour_steps[2]),
            passed_along(blocks[2], "space", neighbour_steps[3]),
        )

    blocks = first_sends(place, send_list, dist)
    arrived = [sent(blocks)]
    turned, pair = turned_cells(place, send_list, dist, blocks[0])
    pair = swapped(pair, "space", 0)
    if rounds > 1:
        arrived.append(sent(later_sends(place, send_list, turned, 1, tiles_of(rows, 1), turned)))

    top_speed = HALF * math.sqrt(3.0)
    normals = area_normal.reshape(FACES, 3, cells)
    face_areas = jnp.sqrt(jnp.sum(normals * normals, axis=1))
    cell_limit = cell_volume / (top_speed * jnp.sum(face_areas, axis=0))
    least = jnp.min(cell_limit).reshape(1, 1)
    shift = 1
    while shift < lax.axis_size("space"):
        least = jnp.minimum(least, passed_along(least, "space", shift))
        shift *= 2
    time_step = CFL * least

    own = jnp.arange(cells, dtype=jnp.int32)[None, :]
    inflow = cells + dirs * width
    index = jnp.where(face_type == 0, face_nbr, jnp.where(face_type == 1, inflow, own)) * SUB
    volume = cell_volume.reshape(1, cells)
    stream = jnp.pad(free_stream, (0, rounds * block - rows)).reshape(rounds * SUB, LANES)
    dist_sum, flux_sum = dist_moments(place, dist, turned)
    dist_sum = summed_over(dist_sum, "vel")
    moved = None
    for i in range(rounds):
        moved, flux_sum = face_sums(
            place, time_step, index, area_normal, stream, dist, turned, volume, flux_sum, moved,
            pair, arrived[i], i,
        )
        if i + 2 < rounds:
            blocks = later_sends(place, send_list, turned, i + 2, tiles_of(rows, i + 2), flux_sum)
            arrived.append(sent(blocks))
    flux_sum = summed_over(flux_sum, "vel")
    return relaxed(place, time_step, moved, dist_sum, flux_sum, volume)


def solution(mesh):
    return jax.shard_map(
        local,
        mesh=mesh,
        in_specs=(
            P("vel", "space"),
            P("vel"),
            P(None, "space"),
            P("space"),
            P(None, "space"),
            P(None, "space"),
            P(None, "space"),
        ),
        out_specs=P("vel", "space"),
        check_vma=False,
    )
```

time: 581 us -> 343 us (0.59); the launches traced: 572 us -> 342 us
  local copies, waits for them, and re-layouts: 238 us -> 8.03 us
  Pallas kernels: 0 us -> 188 us
  blocking collectives: 184 us -> 0 us
  other arithmetic: 117 us -> 6.53 us
  starting transfers between devices: 10.3 us -> 78.6 us
  waiting for transfers between devices: 0.01 us -> 57.1 us
  matrix products: 21.1 us -> 0 us
    pallas_call x0 -> x17, Pallas kernels: none -> 188 us  [the longest x7 115 us: face_sums(): pl.pallas_call(functools.partial(face_kernel, rows, i * block), grid=(1,)...]
    gather x10 -> x0, local copies, waits for them, and re-layouts: 172 us -> none  [the longest x6 138 us: local(): outside = jnp.take(extended, face_nbr[face_slot], axis=1)]
    pmin x1 -> x0, blocking collectives: 166 us -> none  [local(): time_step = CFL * lax.pmin(jnp.min(cell_limit), 'space')]
    ppermute x4 -> x18, starting transfers between devices: 10.3 us -> 67.1 us  [passed_along(): return lax.ppermute(block, axis, route)]
    ppermute x4 -> x18, waiting for transfers between devices: 0.01 us -> 55.3 us  [passed_along(): return lax.ppermute(block, axis, route)]
    add x2, other arithmetic: 50.4 us -> 1.92 us  [summed_over(): value + lax.ppermute(value, axis, [(i, i ^ reach) for i in range(count)])]
    unnamed x135 -> x46, local copies, waits for them, and re-layouts: 43.3 us -> 5.99 us
    div x3 -> x0, other arithmetic: 23.4 us -> none  [the longest x1 22.1 us: local(): return (transported + relax_ratio * shakhov) / (1.0 + relax_ratio)]
  transfers between devices with their start and end apart: 4 -> 28, of which waited for: 0 -> 10; matrix products, arithmetic and copies ran while one was open for 18% -> 2% of each run, Pallas kernels for 0% -> 45%
where the time goes in v2:
time: 343 us; the launch traced here: 342 us
  Pallas kernels  188 us (55%)
  starting transfers between devices  78.6 us (23%)
  waiting for transfers between devices  57.1 us (17%)
  local copies, waits for them, and re-layouts  8.03 us (2%)
  other arithmetic  6.53 us (2%)
    pallas_call x7, Pallas kernels, face_sums(): pl.pallas_call(functools.partial(face_kernel, rows, i * block), grid=(1,)...  115 us
    ppermute x18, starting transfers between devices, passed_along(): return lax.ppermute(block, axis, route)  67.1 us
    ppermute x18, waiting for transfers between devices, passed_along(): return lax.ppermute(block, axis, route)  55.3 us
    pallas_call x6, Pallas kernels, later_sends(): pl.pallas_call(send_kernel, grid=(1,), in_specs=[SMEM, SMEM, pl.BlockSpec...  24.6 us
    pallas_call x1, Pallas kernels, turned_cells(): pl.pallas_call(turn_kernel, grid=(rounds,), in_specs=[SMEM, SMEM, pl.Bloc...  16.5 us
    pallas_call x1, Pallas kernels, relaxed(): pl.pallas_call(functools.partial(relax_kernel, planes), grid=(rows // PLA...  13.9 us
    pallas_call x1, Pallas kernels, dist_moments(): pl.pallas_call(moment_kernel, grid=(rows // PLANE,), in_specs=[SMEM, plan...  13.7 us
    ppermute x8, starting transfers between devices, swapped(): return lax.ppermute(block, axis, route)  8.47 us
  transfers between devices with their start and end apart: 28, of which 10 were waited for; matrix products, arithmetic and copies ran while one was open for 2% of the time, Pallas kernels for 45%

profile of v2, /device:TPU:0, one launch (start us, length us, event | category | flops | bytes accessed | tf_op | source)
XLA Modules:
  0.0 341.6 jit_solution(10848151040525415023)
XLA Ops:
  0.0 0.6 pad_add_fusion.place_ref
  0.6 4.8 %first_sends.1 = (f32[8,128,128]{2,1,0:T(8,128)}, f32[8,128,128]{2,1,0:T(8,128)}, f32[8,128,128]{2,1,0:T(8,128)}) custom-call(s32[2]{0:T(128)} %pad_add_fusion.place_ref, s32[4,128]{1,0:T(4,128)} %list_ref.15, f32[6912,512]{1,0:T(8,128)} %dist_ref.19), custom_call_target="tpu_custom_call" | custom-call | bytes 3670016 | tf_op jit(solution)/shard_map/first_sends/pallas_call | solution.py:358
  5.4 16.5 %turned_cells.1 = (f32[7,4096,128]{2,1,0:T(8,128)}, f32[54,128,128]{2,1,0:T(8,128)}) custom-call(s32[2]{0:T(128)} %pad_add_fusion.place_ref, s32[4,128]{1,0:T(4,128)} %list_ref.15, f32[6912,512]{1,0:T(8,128)} %dist_ref.19, f32[8,128,128]{2,1,0:T(8,128)} %get-tuple-element.44.after_ref), custom_call_target="tpu_custom_call" | custom-call | bytes 31850496 | tf_op jit(solution)/shard_map/turned_cells/pallas_call | solution.py:377
  21.9 0.5 collective-permute-start.4
  22.4 5.7 %collective-permute-start.5 = (f32[8,128,128]{2,1,0:T(8,128)}, f32[8,128,128]{2,1,0:T(8,128)}, u32[]{:S(2)}, u32[]{:S(2)}) collective-permute-start(f32[8,128,128]{2,1,0:T(8,128)} %get-tuple-element.44.after_ref), channel_id=1, source_target_pairs={{2,4},{4,2},{6,8},{8,6},{10,12},{12,10},{14,16},{16,14},{18,20},{2... | collective-permute-start | bytes 1572872 | tf_op jit(solution)/shard_map/ppermute | solution.py:38
  28.0 4.7 %collective-permute-start.7 = (f32[8,128,128]{2,1,0:T(8,128)}, f32[8,128,128]{2,1,0:T(8,128)}, u32[]{:S(2)}, u32[]{:S(2)}) collective-permute-start(f32[8,128,128]{2,1,0:T(8,128)} %get-tuple-element.49), channel_id=1, source_target_pairs={{4,0},{6,2},{8,4},{10,6},{12,8},{14,10},{16,12},{18,14},{20,16},{2... | collective-permute-start | bytes 1572872 | tf_op jit(solution)/shard_map/ppermute | solution.py:30
  32.8 0.6 mul.25
  33.4 1.4 mul.26
  34.8 1.4 reduce_sum.18
  36.2 0.7 sqrt_reduce_fusion
  37.0 0.6 fusion
  37.6 4.2 %later_sends.6 = (f32[8,128,128]{2,1,0:T(8,128)}, f32[8,128,128]{2,1,0:T(8,128)}, f32[8,128,128]{2,1,0:T(8,128)}) custom-call(s32[2]{0:T(128)} %pad_add_fusion.place_ref, s32[4,128]{1,0:T(4,128)} %list_ref.15, f32[7,4096,128]{2,1,0:T(8,128)} %get-tuple-element.45.after_ref.turned_ref, f32[7,4096,128]{2,1,0:T(8,128)} %get-tuple-element.45.after_ref.turned_ref), custom_call_target="tpu_custom_call" | custom-call | bytes 3670016 | tf_op jit(solution)/shard_map/later_sends/pallas_call | solution.py:400
  41.8 4.6 %collective-permute-done = f32[1,1]{1,0:T(1,128)} collective-permute-done((f32[1,1]{1,0:T(1,128)}, f32[1,1]{1,0:T(1,128)}, u32[]{:S(2)}, u32[]{:S(2)}) %collective-permute-start) | collective-permute-done | bytes 36 | tf_op jit(solution)/shard_map/ppermute | solution.py:30
  47.6 16.7 %collective-permute-start.1 = (f32[1,1]{1,0:T(1,128)}, f32[1,1]{1,0:T(1,128)}, u32[]{:S(2)}, u32[]{:S(2)}) collective-permute-start(f32[1,1]{1,0:T(1,128)} %min.12), channel_id=1, source_target_pairs={{28,0},{30,2},{0,4},{2,6},{4,8},{6,10},{8,12},{10,14},{12,16},{14,... | collective-permute-start | bytes 20 | tf_op jit(solution)/shard_map/ppermute | solution.py:30
  64.3 3.4 collective-permute-done.1
  68.2 1.4 collective-permute-start.2
  69.6 4.1 %collective-permute-done.2 = f32[1,1]{1,0:T(1,128)} collective-permute-done((f32[1,1]{1,0:T(1,128)}, f32[1,1]{1,0:T(1,128)}, u32[]{:S(2)}, u32[]{:S(2)}) %collective-permute-start.2) | collective-permute-done | bytes 36 | tf_op jit(solution)/shard_map/ppermute | solution.py:30
  74.3 1.4 collective-permute-start.3
  75.6 3.2 collective-permute-done.3
  78.9 0.6 select_multiply_fusion.index_ref
  79.5 13.7 %dist_moments.1 = (f32[16,512]{1,0:T(8,128)}, f32[8,512]{1,0:T(8,128)}) custom-call(s32[2]{0:T(128)} %pad_add_fusion.place_ref, f32[6912,512]{1,0:T(8,128)} %dist_ref.19, f32[7,4096,128]{2,1,0:T(8,128)} %get-tuple-element.45.after_ref.turned_ref), custom_call_target="tpu_custom_call" | custom-call | flops 106168320 | bytes 14155776 | tf_op jit(solution)/shard_map/dist_moments/pallas_call | solution.py:417
  93.2 0.6 pad_bitcast_fusion.stream_ref
  94.5 4.7 %collective-permute-start.10 = (f32[8,128,128]{2,1,0:T(8,128)}, f32[8,128,128]{2,1,0:T(8,128)}, u32[]{:S(2)}, u32[]{:S(2)}) collective-permute-start(f32[8,128,128]{2,1,0:T(8,128)} %get-tuple-element.53), channel_id=1, source_target_pairs={{4,0},{6,2},{8,4},{10,6},{12,8},{14,10},{16,12},{18,14},{20,16},{2... | collective-permute-start | bytes 1572872 | tf_op jit(solution)/shard_map/ppermute | solution.py:30
  99.2 1.8 copy-done
  101.0 16.6 %face_sums.7 = (f32[6912,512]{1,0:T(8,128)}, f32[8,512]{1,0:T(8,128)}) custom-call(s32[2]{0:T(128)} %pad_add_fusion.place_ref, f32[1,1]{1,0:T(1,128)S(6)} %mul.29.time_ref, s32[6,512]{1,0:T(8,128)} %select_multiply_fusion.index_ref, f32[18,512]{1,0:T(8,128)} %normal_ref.13, f32[56,128]{1,0:T(8,128)} %pad_bitcast_fusion.stream_ref, f32[6912,512]{1,0:T(8,128)} %dist_ref.19, ...), custom_call_target="tpu_custom_call" | custom-call | flops 36700160 | bytes 8388608 | tf_op jit(solution)/shard_map/face_sums/pallas_call | solution.py:441
  117.6 4.1 %later_sends.7 = (f32[8,128,128]{2,1,0:T(8,128)}, f32[8,128,128]{2,1,0:T(8,128)}, f32[8,128,128]{2,1,0:T(8,128)}) custom-call(s32[2]{0:T(128)} %pad_add_fusion.place_ref, s32[4,128]{1,0:T(4,128)} %list_ref.15, f32[7,4096,128]{2,1,0:T(8,128)} %get-tuple-element.45.after_ref.turned_ref, f32[8,512]{1,0:T(8,128)} %get-tuple-element.50.before_ref.after_ref), custom_call_target="tpu_custom_call" | custom-call | bytes 3670016 | tf_op jit(solution)/shard_map/later_sends/pallas_call | solution.py:400
  121.7 1.2 collective-permute-start.11
  122.9 0.4 collective-permute-start.12
  123.2 4.4 %collective-permute-start.13 = (f32[8,128,128]{2,1,0:T(8,128)}, f32[8,128,128]{2,1,0:T(8,128)S(1)}, u32[]{:S(2)}, u32[]{:S(2)}) collective-permute-start(f32[8,128,128]{2,1,0:T(8,128)} %get-tuple-element.58), channel_id=1, source_target_pairs={{4,0},{6,2},{8,4},{10,6},{12,8},{14,10},{16,12},{18,14},{20,16},{2... | collective-permute-start | bytes 1572872 | tf_op jit(solution)/shard_map/ppermute | solution.py:30
  127.6 16.6 %face_sums.8 = (f32[6912,512]{1,0:T(8,128)}, f32[8,512]{1,0:T(8,128)}) custom-call(s32[2]{0:T(128)} %pad_add_fusion.place_ref, f32[1,1]{1,0:T(1,128)S(6)} %mul.29.time_ref, s32[6,512]{1,0:T(8,128)} %select_multiply_fusion.index_ref, f32[18,512]{1,0:T(8,128)} %normal_ref.13, f32[56,128]{1,0:T(8,128)} %pad_bitcast_fusion.stream_ref, ...), custom_call_target="tpu_custom_call", output_to_operand_aliasing={{0}: (13, {})} | custom-call | flops 36700160 | bytes 8388608 | tf_op jit(solution)/shard_map/face_sums/pallas_call | solution.py:441
  144.2 4.1 %later_sends.8 = (f32[8,128,128]{2,1,0:T(8,128)}, f32[8,128,128]{2,1,0:T(8,128)}, f32[8,128,128]{2,1,0:T(8,128)}) custom-call(s32[2]{0:T(128)} %pad_add_fusion.place_ref, s32[4,128]{1,0:T(4,128)} %list_ref.15, f32[7,4096,128]{2,1,0:T(8,128)} %get-tuple-element.45.after_ref.turned_ref, f32[8,512]{1,0:T(8,128)} %get-tuple-element.55.before_ref.after_ref), custom_call_target="tpu_custom_call" | custom-call | bytes 3670016 | tf_op jit(solution)/shard_map/later_sends/pallas_call | solution.py:400
  148.3 0.3 collective-permute-start.15
  148.6 18.9 %collective-permute-start.16 = (f32[8,128,128]{2,1,0:T(8,128)}, f32[8,128,128]{2,1,0:T(8,128)S(1)}, u32[]{:S(2)}, u32[]{:S(2)}) collective-permute-start(f32[8,128,128]{2,1,0:T(8,128)} %get-tuple-element.63), channel_id=1, source_target_pairs={{4,0},{6,2},{8,4},{10,6},{12,8},{14,10},{16,12},{18,14},{20,16},{2... | collective-permute-start | bytes 1572872 | tf_op jit(solution)/shard_map/ppermute | solution.py:30
  167.6 11.2 %collective-permute-done.13.back_ref = f32[8,128,128]{2,1,0:T(8,128)S(1)} collective-permute-done((f32[8,128,128]{2,1,0:T(8,128)}, f32[8,128,128]{2,1,0:T(8,128)S(1)}, u32[]{:S(2)}, u32[]{:S(2)}) %collective-permute-start.13) | collective-permute-done | bytes 524320 | tf_op jit(solution)/shard_map/ppermute | solution.py:30
  178.8 0.8 copy-done.12
  179.6 16.6 %face_sums.9 = (f32[6912,512]{1,0:T(8,128)}, f32[8,512]{1,0:T(8,128)}) custom-call(s32[2]{0:T(128)} %pad_add_fusion.place_ref, f32[1,1]{1,0:T(1,128)S(6)} %mul.29.time_ref, s32[6,512]{1,0:T(8,128)} %select_multiply_fusion.index_ref, f32[18,512]{1,0:T(8,128)} %normal_ref.13, f32[56,128]{1,0:T(8,128)} %pad_bitcast_fusion.stream_ref, ...), custom_call_target="tpu_custom_call", output_to_operand_aliasing={{0}: (13, {})} | custom-call | flops 36700160 | bytes 8388608 | tf_op jit(solution)/shard_map/face_sums/pallas_call | solution.py:441
  196.2 4.1 %later_sends.9 = (f32[8,128,128]{2,1,0:T(8,128)}, f32[8,128,128]{2,1,0:T(8,128)}, f32[8,128,128]{2,1,0:T(8,128)}) custom-call(s32[2]{0:T(128)} %pad_add_fusion.place_ref, s32[4,128]{1,0:T(4,128)} %list_ref.15, f32[7,4096,128]{2,1,0:T(8,128)} %get-tuple-element.45.after_ref.turned_ref, f32[8,512]{1,0:T(8,128)} %get-tuple-element.60.before_ref.after_ref), custom_call_target="tpu_custom_call" | custom-call | bytes 3670016 | tf_op jit(solution)/shard_map/later_sends/pallas_call | solution.py:400
  200.3 4.7 %collective-permute-start.19 = (f32[8,128,128]{2,1,0:T(8,128)}, f32[8,128,128]{2,1,0:T(8,128)S(1)}, u32[]{:S(2)}, u32[]{:S(2)}) collective-permute-start(f32[8,128,128]{2,1,0:T(8,128)} %get-tuple-element.68), channel_id=1, source_target_pairs={{4,0},{6,2},{8,4},{10,6},{12,8},{14,10},{16,12},{18,14},{20,16},{2... | collective-permute-start | bytes 1572872 | tf_op jit(solution)/shard_map/ppermute | solution.py:30
  205.1 0.8 copy-done.9
  205.9 0.2 copy-done.13
  206.1 16.6 %face_sums.10 = (f32[6912,512]{1,0:T(8,128)}, f32[8,512]{1,0:T(8,128)}) custom-call(s32[2]{0:T(128)} %pad_add_fusion.place_ref, f32[1,1]{1,0:T(1,128)S(6)} %mul.29.time_ref, s32[6,512]{1,0:T(8,128)} %select_multiply_fusion.index_ref, f32[18,512]{1,0:T(8,128)} %normal_ref.13, f32[56,128]{1,0:T(8,128)} %pad_bitcast_fusion.stream_ref, ...), custom_call_target="tpu_custom_call", output_to_operand_aliasing={{0}: (13, {})} | custom-call | flops 36700160 | bytes 8388608 | tf_op jit(solution)/shard_map/face_sums/pallas_call | solution.py:441
  222.6 4.1 %later_sends.10 = (f32[8,128,128]{2,1,0:T(8,128)}, f32[8,128,128]{2,1,0:T(8,128)}, f32[8,128,128]{2,1,0:T(8,128)}) custom-call(s32[2]{0:T(128)} %pad_add_fusion.place_ref, s32[4,128]{1,0:T(4,128)} %list_ref.15, f32[7,4096,128]{2,1,0:T(8,128)} %get-tuple-element.45.after_ref.turned_ref, f32[8,512]{1,0:T(8,128)} %get-tuple-element.65.before_ref.after_ref), custom_call_target="tpu_custom_call" | custom-call | bytes 3670016 | tf_op jit(solution)/shard_map/later_sends/pallas_call | solution.py:400
  226.8 1.2 collective-permute-start.20
  227.9 0.3 collective-permute-start.21
  228.3 4.4 %collective-permute-start.22 = (f32[8,128,128]{2,1,0:T(8,128)}, f32[8,128,128]{2,1,0:T(8,128)S(1)}, u32[]{:S(2)}, u32[]{:S(2)}) collective-permute-start(f32[8,128,128]{2,1,0:T(8,128)} %get-tuple-element.73), channel_id=1, source_target_pairs={{4,0},{6,2},{8,4},{10,6},{12,8},{14,10},{16,12},{18,14},{20,16},{2... | collective-permute-start | bytes 1572872 | tf_op jit(solution)/shard_map/ppermute | solution.py:30
  232.6 8.4 %collective-permute-done.18.ahead_ref = f32[8,128,128]{2,1,0:T(8,128)S(1)} collective-permute-done((f32[8,128,128]{2,1,0:T(8,128)}, f32[8,128,128]{2,1,0:T(8,128)S(1)}, u32[]{:S(2)}, u32[]{:S(2)}) %collective-permute-start.18) | collective-permute-done | bytes 524320 | tf_op jit(solution)/shard_map/ppermute | solution.py:30
  241.0 13.8 %collective-permute-done.19.back_ref = f32[8,128,128]{2,1,0:T(8,128)S(1)} collective-permute-done((f32[8,128,128]{2,1,0:T(8,128)}, f32[8,128,128]{2,1,0:T(8,128)S(1)}, u32[]{:S(2)}, u32[]{:S(2)}) %collective-permute-start.19) | collective-permute-done | bytes 524320 | tf_op jit(solution)/shard_map/ppermute | solution.py:30
  254.8 0.8 copy-done.14
  255.6 16.6 %face_sums.11 = (f32[6912,512]{1,0:T(8,128)}, f32[8,512]{1,0:T(8,128)}) custom-call(s32[2]{0:T(128)} %pad_add_fusion.place_ref, f32[1,1]{1,0:T(1,128)S(6)} %mul.29.time_ref, s32[6,512]{1,0:T(8,128)} %select_multiply_fusion.index_ref, f32[18,512]{1,0:T(8,128)} %normal_ref.13, f32[56,128]{1,0:T(8,128)} %pad_bitcast_fusion.stream_ref, ...), custom_call_target="tpu_custom_call", output_to_operand_aliasing={{0}: (13, {})} | custom-call | flops 36700160 | bytes 8388608 | tf_op jit(solution)/shard_map/face_sums/pallas_call | solution.py:441
  272.2 3.9 %later_sends.11 = (f32[6,128,128]{2,1,0:T(8,128)}, f32[6,128,128]{2,1,0:T(8,128)}, f32[6,128,128]{2,1,0:T(8,128)}) custom-call(s32[2]{0:T(128)} %pad_add_fusion.place_ref, s32[4,128]{1,0:T(4,128)} %list_ref.15, f32[7,4096,128]{2,1,0:T(8,128)} %get-tuple-element.45.after_ref.turned_ref, f32[8,512]{1,0:T(8,128)} %get-tuple-element.70.before_ref.after_ref), custom_call_target="tpu_custom_call" | custom-call | bytes 3276800 | tf_op jit(solution)/shard_map/later_sends/pallas_call | solution.py:400
  276.2 3.2 collective-permute-start.24
  279.3 1.6 collective-permute-start.25
  280.9 1.6 collective-permute-start.26
  282.5 0.8 copy-done.11
  283.3 16.6 %face_sums.12 = (f32[6912,512]{1,0:T(8,128)}, f32[8,512]{1,0:T(8,128)}) custom-call(s32[2]{0:T(128)} %pad_add_fusion.place_ref, f32[1,1]{1,0:T(1,128)S(6)} %mul.29.time_ref, s32[6,512]{1,0:T(8,128)} %select_multiply_fusion.index_ref, f32[18,512]{1,0:T(8,128)} %normal_ref.13, f32[56,128]{1,0:T(8,128)} %pad_bitcast_fusion.stream_ref, ...), custom_call_target="tpu_custom_call", output_to_operand_aliasing={{0}: (13, {})} | custom-call | flops 36700160 | bytes 8388608 | tf_op jit(solution)/shard_map/face_sums/pallas_call | solution.py:441
  299.9 1.9 collective-permute-done.24.ahead_ref
  301.8 4.5 %collective-permute-done.25.back_ref = f32[6,128,128]{2,1,0:T(8,128)S(1)} collective-permute-done((f32[6,128,128]{2,1,0:T(8,128)}, f32[6,128,128]{2,1,0:T(8,128)S(1)}, u32[]{:S(2)}, u32[]{:S(2)}) %collective-permute-start.25) | collective-permute-done | bytes 393248 | tf_op jit(solution)/shard_map/ppermute | solution.py:30
  306.4 0.7 copy-done.17
  307.1 15.4 %face_sums.13 = (f32[6912,512]{1,0:T(8,128)}, f32[8,512]{1,0:T(8,128)}) custom-call(s32[2]{0:T(128)} %pad_add_fusion.place_ref, f32[1,1]{1,0:T(1,128)S(6)} %mul.29.time_ref, s32[6,512]{1,0:T(8,128)} %select_multiply_fusion.index_ref, f32[18,512]{1,0:T(8,128)} %normal_ref.13, f32[56,128]{1,0:T(8,128)} %pad_bitcast_fusion.stream_ref, ...), custom_call_target="tpu_custom_call", output_to_operand_aliasing={{0}: (13, {})} | custom-call | flops 36700160 | bytes 8388608 | tf_op jit(solution)/shard_map/face_sums/pallas_call | solution.py:441
  322.5 1.5 collective-permute-start.27
  324.0 0.6 add.13.dist_sum_ref
  324.6 1.9 collective-permute-done.27
  326.4 1.3 add.14.flux_sum_ref
  327.7 13.9 %relaxed.1 = f32[6912,512]{1,0:T(8,128)} custom-call(s32[2]{0:T(128)} %pad_add_fusion.place_ref, f32[1,1]{1,0:T(1,128)S(6)} %mul.29.time_ref, f32[6912,512]{1,0:T(8,128)} %get-tuple-element.80.moved_ref, f32[16,512]{1,0:T(8,128)} %add.13.dist_sum_ref, f32[8,512]{1,0:T(8,128)} %add.14.flux_sum_ref, f32[1,512]{1,0:T(1,128)} %bitcast.13), custom_call_target="tpu_custom_call" | custom-call | flops 35389440 | bytes 28311552 | tf_op jit(solution)/shard_map/relaxed/pallas_call | solution.py:483
  (65 shorter events, 0.2 us)
Async XLA Ops:
  0.6 32.1 %copy-start.1 = (f32[18,512]{1,0:T(8,128)S(1)}, f32[18,512]{1,0:T(8,128)}, u32[]{:S(2)}) copy-start(f32[18,512]{1,0:T(8,128)} %normal_ref.13) | copy-start | bytes 110596
  0.6 36.4 %copy-start.18 = (f32[512]{0:T(512)S(1)}, f32[512]{0:T(512)}, u32[]{:S(2)}) copy-start(f32[512]{0:T(512)} %param.10) | copy-start | bytes 6148
  21.9 77.3 %collective-permute-start.4 = (f32[54,128,128]{2,1,0:T(8,128)}, f32[54,128,128]{2,1,0:T(8,128)S(1)}, u32[]{:S(2)}, u32[]{:S(2)}) collective-permute-start(f32[54,128,128]{2,1,0:T(8,128)} %get-tuple-element.47), channel_id=1, source_target_pairs={{0,2},{2,0},{4,6},{6,4},{8,10},{10,8},{12,14},{14,12},{16,18},{18,... | collective-permute-start | bytes 10616840 | tf_op jit(solution)/shard_map/ppermute | solution.py:38
  22.4 72.0 %collective-permute-start.5 = (f32[8,128,128]{2,1,0:T(8,128)}, f32[8,128,128]{2,1,0:T(8,128)}, u32[]{:S(2)}, u32[]{:S(2)}) collective-permute-start(f32[8,128,128]{2,1,0:T(8,128)} %get-tuple-element.44.after_ref), channel_id=1, source_target_pairs={{2,4},{4,2},{6,8},{8,6},{10,12},{12,10},{14,16},{16,14},{18,20},{2... | collective-permute-start | bytes 1572872 | tf_op jit(solution)/shard_map/ppermute | solution.py:38
  28.0 66.4 %collective-permute-start.6 = (f32[8,128,128]{2,1,0:T(8,128)}, f32[8,128,128]{2,1,0:T(8,128)}, u32[]{:S(2)}, u32[]{:S(2)}) collective-permute-start(f32[8,128,128]{2,1,0:T(8,128)} %get-tuple-element.48), channel_id=1, source_target_pairs={{28,0},{30,2},{0,4},{2,6},{4,8},{6,10},{8,12},{10,14},{12,16},{14,... | collective-permute-start | bytes 1572872 | tf_op jit(solution)/shard_map/ppermute | solution.py:30
  28.0 71.2 %collective-permute-start.7 = (f32[8,128,128]{2,1,0:T(8,128)}, f32[8,128,128]{2,1,0:T(8,128)}, u32[]{:S(2)}, u32[]{:S(2)}) collective-permute-start(f32[8,128,128]{2,1,0:T(8,128)} %get-tuple-element.49), channel_id=1, source_target_pairs={{4,0},{6,2},{8,4},{10,6},{12,8},{14,10},{16,12},{18,14},{20,16},{2... | collective-permute-start | bytes 1572872 | tf_op jit(solution)/shard_map/ppermute | solution.py:30
  37.6 8.8 %collective-permute-start = (f32[1,1]{1,0:T(1,128)}, f32[1,1]{1,0:T(1,128)}, u32[]{:S(2)}, u32[]{:S(2)}) collective-permute-start(f32[1,1]{1,0:T(1,128)} %bitcast.2), channel_id=1, source_target_pairs={{30,0},{0,2},{2,4},{4,6},{6,8},{8,10},{10,12},{12,14},{14,16},{16,... | collective-permute-start | bytes 20 | tf_op jit(solution)/shard_map/ppermute | solution.py:30
  37.6 41.3 %copy-start.21 = (s32[6,512]{1,0:T(8,128)S(1)}, s32[6,512]{1,0:T(8,128)}, u32[]{:S(2)}) copy-start(s32[6,512]{1,0:T(8,128)} %param.11) | copy-start | bytes 36868
  37.6 41.3 %copy-start.22 = (s32[6,512]{1,0:T(8,128)S(1)}, s32[6,512]{1,0:T(8,128)}, u32[]{:S(2)}) copy-start(s32[6,512]{1,0:T(8,128)} %param.12) | copy-start | bytes 36868
  47.6 20.1 %collective-permute-start.1 = (f32[1,1]{1,0:T(1,128)}, f32[1,1]{1,0:T(1,128)}, u32[]{:S(2)}, u32[]{:S(2)}) collective-permute-start(f32[1,1]{1,0:T(1,128)} %min.12), channel_id=1, source_target_pairs={{28,0},{30,2},{0,4},{2,6},{4,8},{6,10},{8,12},{10,14},{12,16},{14,... | collective-permute-start | bytes 20 | tf_op jit(solution)/shard_map/ppermute | solution.py:30
  68.2 5.5 %collective-permute-start.2 = (f32[1,1]{1,0:T(1,128)}, f32[1,1]{1,0:T(1,128)}, u32[]{:S(2)}, u32[]{:S(2)}) collective-permute-start(f32[1,1]{1,0:T(1,128)} %min.13), channel_id=1, source_target_pairs={{24,0},{26,2},{28,4},{30,6},{0,8},{2,10},{4,12},{6,14},{8,16},{10,... | collective-permute-start | bytes 20 | tf_op jit(solution)/shard_map/ppermute | solution.py:30
  74.3 4.6 %collective-permute-start.3 = (f32[1,1]{1,0:T(1,128)}, f32[1,1]{1,0:T(1,128)}, u32[]{:S(2)}, u32[]{:S(2)}) collective-permute-start(f32[1,1]{1,0:T(1,128)} %min.14), channel_id=1, source_target_pairs={{16,0},{18,2},{20,4},{22,6},{24,8},{26,10},{28,12},{30,14},{0,16},... | collective-permute-start | bytes 20 | tf_op jit(solution)/shard_map/ppermute | solution.py:30
  78.9 44.3 %collective-permute-start.8 = (f32[8,128,128]{2,1,0:T(8,128)}, f32[8,128,128]{2,1,0:T(8,128)S(1)}, u32[]{:S(2)}, u32[]{:S(2)}) collective-permute-start(f32[8,128,128]{2,1,0:T(8,128)} %get-tuple-element.51), channel_id=1, source_target_pairs={{2,4},{4,2},{6,8},{8,6},{10,12},{12,10},{14,16},{16,14},{18,20},{2... | collective-permute-start | bytes 1572872 | tf_op jit(solution)/shard_map/ppermute | solution.py:38
  79.5 13.7 %copy-start.20 = (f32[6912]{0:T(1024)S(1)}, f32[6912]{0:T(1024)}, u32[]{:S(2)}) copy-start(f32[6912]{0:T(1024)} %param.8) | copy-start | bytes 82948
  94.4 33.2 %collective-permute-start.9 = (f32[8,128,128]{2,1,0:T(8,128)}, f32[8,128,128]{2,1,0:T(8,128)}, u32[]{:S(2)}, u32[]{:S(2)}) collective-permute-start(f32[8,128,128]{2,1,0:T(8,128)} %get-tuple-element.52), channel_id=1, source_target_pairs={{28,0},{30,2},{0,4},{2,6},{4,8},{6,10},{8,12},{10,14},{12,16},{14,... | collective-permute-start | bytes 1572872 | tf_op jit(solution)/shard_map/ppermute | solution.py:30
  94.5 33.1 %collective-permute-start.10 = (f32[8,128,128]{2,1,0:T(8,128)}, f32[8,128,128]{2,1,0:T(8,128)}, u32[]{:S(2)}, u32[]{:S(2)}) collective-permute-start(f32[8,128,128]{2,1,0:T(8,128)} %get-tuple-element.53), channel_id=1, source_target_pairs={{4,0},{6,2},{8,4},{10,6},{12,8},{14,10},{16,12},{18,14},{20,16},{2... | collective-permute-start | bytes 1572872 | tf_op jit(solution)/shard_map/ppermute | solution.py:30
  99.2 1.8 copy-start
  121.7 27.0 %collective-permute-start.11 = (f32[8,128,128]{2,1,0:T(8,128)}, f32[8,128,128]{2,1,0:T(8,128)S(1)}, u32[]{:S(2)}, u32[]{:S(2)}) collective-permute-start(f32[8,128,128]{2,1,0:T(8,128)} %get-tuple-element.56), channel_id=1, source_target_pairs={{2,4},{4,2},{6,8},{8,6},{10,12},{12,10},{14,16},{16,14},{18,20},{2... | collective-permute-start | bytes 1572872 | tf_op jit(solution)/shard_map/ppermute | solution.py:38
  122.9 44.7 %collective-permute-start.12 = (f32[8,128,128]{2,1,0:T(8,128)}, f32[8,128,128]{2,1,0:T(8,128)S(1)}, u32[]{:S(2)}, u32[]{:S(2)}) collective-permute-start(f32[8,128,128]{2,1,0:T(8,128)} %get-tuple-element.57), channel_id=1, source_target_pairs={{28,0},{30,2},{0,4},{2,6},{4,8},{6,10},{8,12},{10,14},{12,16},{14,... | collective-permute-start | bytes 1572872 | tf_op jit(solution)/shard_map/ppermute | solution.py:30
  123.2 4.4 %copy-start.2 = (f32[8,128,128]{2,1,0:T(8,128)}, f32[8,128,128]{2,1,0:T(8,128)S(1)}, u32[]{:S(2)}) copy-start(f32[8,128,128]{2,1,0:T(8,128)S(1)} %collective-permute-done.8.cross_ref) | copy-start | bytes 1572868
  123.2 55.6 %collective-permute-start.13 = (f32[8,128,128]{2,1,0:T(8,128)}, f32[8,128,128]{2,1,0:T(8,128)S(1)}, u32[]{:S(2)}, u32[]{:S(2)}) collective-permute-start(f32[8,128,128]{2,1,0:T(8,128)} %get-tuple-element.58), channel_id=1, source_target_pairs={{4,0},{6,2},{8,4},{10,6},{12,8},{14,10},{16,12},{18,14},{20,16},{2... | collective-permute-start | bytes 1572872 | tf_op jit(solution)/shard_map/ppermute | solution.py:30
  148.3 52.0 %collective-permute-start.14 = (f32[8,128,128]{2,1,0:T(8,128)}, f32[8,128,128]{2,1,0:T(8,128)S(1)}, u32[]{:S(2)}, u32[]{:S(2)}) collective-permute-start(f32[8,128,128]{2,1,0:T(8,128)} %get-tuple-element.61), channel_id=1, source_target_pairs={{2,4},{4,2},{6,8},{8,6},{10,12},{12,10},{14,16},{16,14},{18,20},{2... | collective-permute-start | bytes 1572872 | tf_op jit(solution)/shard_map/ppermute | solution.py:38
  148.3 56.8 %collective-permute-start.15 = (f32[8,128,128]{2,1,0:T(8,128)}, f32[8,128,128]{2,1,0:T(8,128)S(1)}, u32[]{:S(2)}, u32[]{:S(2)}) collective-permute-start(f32[8,128,128]{2,1,0:T(8,128)} %get-tuple-element.62), channel_id=1, source_target_pairs={{28,0},{30,2},{0,4},{2,6},{4,8},{6,10},{8,12},{10,14},{12,16},{14,... | collective-permute-start | bytes 1572872 | tf_op jit(solution)/shard_map/ppermute | solution.py:30
  148.6 30.2 %copy-start.5 = (f32[8,128,128]{2,1,0:T(8,128)}, f32[8,128,128]{2,1,0:T(8,128)S(1)}, u32[]{:S(2)}) copy-start(f32[8,128,128]{2,1,0:T(8,128)S(1)} %collective-permute-done.11.cross_ref) | copy-start | bytes 1572868
  148.6 56.4 %collective-permute-start.16 = (f32[8,128,128]{2,1,0:T(8,128)}, f32[8,128,128]{2,1,0:T(8,128)S(1)}, u32[]{:S(2)}, u32[]{:S(2)}) collective-permute-start(f32[8,128,128]{2,1,0:T(8,128)} %get-tuple-element.63), channel_id=1, source_target_pairs={{4,0},{6,2},{8,4},{10,6},{12,8},{14,10},{16,12},{18,14},{20,16},{2... | collective-permute-start | bytes 1572872 | tf_op jit(solution)/shard_map/ppermute | solution.py:30
  167.6 11.3 %copy-start.8 = (f32[8,128,128]{2,1,0:T(8,128)}, f32[8,128,128]{2,1,0:T(8,128)S(1)}, u32[]{:S(2)}) copy-start(f32[8,128,128]{2,1,0:T(8,128)S(1)} %collective-permute-done.12.ahead_ref) | copy-start | bytes 1572868
  178.8 0.8 copy-start.12
  200.3 28.0 %collective-permute-start.17 = (f32[8,128,128]{2,1,0:T(8,128)}, f32[8,128,128]{2,1,0:T(8,128)S(1)}, u32[]{:S(2)}, u32[]{:S(2)}) collective-permute-start(f32[8,128,128]{2,1,0:T(8,128)} %get-tuple-element.66), channel_id=1, source_target_pairs={{2,4},{4,2},{6,8},{8,6},{10,12},{12,10},{14,16},{16,14},{18,20},{2... | collective-permute-start | bytes 1572872 | tf_op jit(solution)/shard_map/ppermute | solution.py:38
  200.3 40.7 %collective-permute-start.18 = (f32[8,128,128]{2,1,0:T(8,128)}, f32[8,128,128]{2,1,0:T(8,128)S(1)}, u32[]{:S(2)}, u32[]{:S(2)}) collective-permute-start(f32[8,128,128]{2,1,0:T(8,128)} %get-tuple-element.67), channel_id=1, source_target_pairs={{28,0},{30,2},{0,4},{2,6},{4,8},{6,10},{8,12},{10,14},{12,16},{14,... | collective-permute-start | bytes 1572872 | tf_op jit(solution)/shard_map/ppermute | solution.py:30
  200.3 4.8 %copy-start.6 = (f32[8,128,128]{2,1,0:T(8,128)}, f32[8,128,128]{2,1,0:T(8,128)S(1)}, u32[]{:S(2)}) copy-start(f32[8,128,128]{2,1,0:T(8,128)S(1)} %collective-permute-done.14.cross_ref) | copy-start | bytes 1572868
  200.3 54.5 %collective-permute-start.19 = (f32[8,128,128]{2,1,0:T(8,128)}, f32[8,128,128]{2,1,0:T(8,128)S(1)}, u32[]{:S(2)}, u32[]{:S(2)}) collective-permute-start(f32[8,128,128]{2,1,0:T(8,128)} %get-tuple-element.68), channel_id=1, source_target_pairs={{4,0},{6,2},{8,4},{10,6},{12,8},{14,10},{16,12},{18,14},{20,16},{2... | collective-permute-start | bytes 1572872 | tf_op jit(solution)/shard_map/ppermute | solution.py:30
  205.1 0.8 copy-start.9
  205.1 1.0 copy-start.13
  226.8 52.6 %collective-permute-start.20 = (f32[8,128,128]{2,1,0:T(8,128)}, f32[8,128,128]{2,1,0:T(8,128)S(1)}, u32[]{:S(2)}, u32[]{:S(2)}) collective-permute-start(f32[8,128,128]{2,1,0:T(8,128)} %get-tuple-element.71), channel_id=1, source_target_pairs={{2,4},{4,2},{6,8},{8,6},{10,12},{12,10},{14,16},{16,14},{18,20},{2... | collective-permute-start | bytes 1572872 | tf_op jit(solution)/shard_map/ppermute | solution.py:38
  227.9 53.0 %collective-permute-start.21 = (f32[8,128,128]{2,1,0:T(8,128)}, f32[8,128,128]{2,1,0:T(8,128)S(1)}, u32[]{:S(2)}, u32[]{:S(2)}) collective-permute-start(f32[8,128,128]{2,1,0:T(8,128)} %get-tuple-element.72), channel_id=1, source_target_pairs={{28,0},{30,2},{0,4},{2,6},{4,8},{6,10},{8,12},{10,14},{12,16},{14,... | collective-permute-start | bytes 1572872 | tf_op jit(solution)/shard_map/ppermute | solution.py:30
  228.3 26.6 %copy-start.7 = (f32[8,128,128]{2,1,0:T(8,128)}, f32[8,128,128]{2,1,0:T(8,128)S(1)}, u32[]{:S(2)}) copy-start(f32[8,128,128]{2,1,0:T(8,128)S(1)} %collective-permute-done.17.cross_ref) | copy-start | bytes 1572868
  228.3 54.2 %collective-permute-start.22 = (f32[8,128,128]{2,1,0:T(8,128)}, f32[8,128,128]{2,1,0:T(8,128)S(1)}, u32[]{:S(2)}, u32[]{:S(2)}) collective-permute-start(f32[8,128,128]{2,1,0:T(8,128)} %get-tuple-element.73), channel_id=1, source_target_pairs={{4,0},{6,2},{8,4},{10,6},{12,8},{14,10},{16,12},{18,14},{20,16},{2... | collective-permute-start | bytes 1572872 | tf_op jit(solution)/shard_map/ppermute | solution.py:30
  241.0 13.8 %copy-start.10 = (f32[8,128,128]{2,1,0:T(8,128)}, f32[8,128,128]{2,1,0:T(8,128)S(1)}, u32[]{:S(2)}) copy-start(f32[8,128,128]{2,1,0:T(8,128)S(1)} %collective-permute-done.18.ahead_ref) | copy-start | bytes 1572868
  254.8 0.8 copy-start.14
  272.2 8.7 %copy-start.19 = (f32[16,512]{1,0:T(8,128)S(1)}, f32[16,512]{1,0:T(8,128)}, u32[]{:S(2)}) copy-start(f32[16,512]{1,0:T(8,128)} %get-tuple-element.81) | copy-start | bytes 98308
  276.1 23.8 %collective-permute-start.23 = (f32[6,128,128]{2,1,0:T(8,128)}, f32[6,128,128]{2,1,0:T(8,128)S(1)}, u32[]{:S(2)}, u32[]{:S(2)}) collective-permute-start(f32[6,128,128]{2,1,0:T(8,128)} %get-tuple-element.76), channel_id=1, source_target_pairs={{2,4},{4,2},{6,8},{8,6},{10,12},{12,10},{14,16},{16,14},{18,20},{2... | collective-permute-start | bytes 1179656 | tf_op jit(solution)/shard_map/ppermute | solution.py:38
  276.2 25.7 %collective-permute-start.24 = (f32[6,128,128]{2,1,0:T(8,128)}, f32[6,128,128]{2,1,0:T(8,128)S(1)}, u32[]{:S(2)}, u32[]{:S(2)}) collective-permute-start(f32[6,128,128]{2,1,0:T(8,128)} %get-tuple-element.77), channel_id=1, source_target_pairs={{28,0},{30,2},{0,4},{2,6},{4,8},{6,10},{8,12},{10,14},{12,16},{14,... | collective-permute-start | bytes 1179656 | tf_op jit(solution)/shard_map/ppermute | solution.py:30
  279.3 3.2 copy-start.3
  279.3 27.0 %collective-permute-start.25 = (f32[6,128,128]{2,1,0:T(8,128)}, f32[6,128,128]{2,1,0:T(8,128)S(1)}, u32[]{:S(2)}, u32[]{:S(2)}) collective-permute-start(f32[6,128,128]{2,1,0:T(8,128)} %get-tuple-element.78), channel_id=1, source_target_pairs={{4,0},{6,2},{8,4},{10,6},{12,8},{14,10},{16,12},{18,14},{20,16},{2... | collective-permute-start | bytes 1179656 | tf_op jit(solution)/shard_map/ppermute | solution.py:30
  280.9 1.6 copy-start.4
  280.9 43.1 %collective-permute-start.26 = (f32[16,512]{1,0:T(8,128)S(1)}, f32[16,512]{1,0:T(8,128)S(1)}, u32[]{:S(2)}, u32[]{:S(2)}) collective-permute-start(f32[16,512]{1,0:T(8,128)S(1)} %copy-done.19), channel_id=1, source_target_pairs={{0,1},{1,0},{2,3},{3,2},{4,5},{5,4},{6,7},{7,6},{8,9},{9,8},{10,11... | collective-permute-start | bytes 98312 | tf_op jit(solution)/shard_map/ppermute | solution.py:47
  282.5 0.9 copy-start.11
  299.9 6.4 %copy-start.15 = (f32[6,128,128]{2,1,0:T(8,128)}, f32[6,128,128]{2,1,0:T(8,128)S(1)}, u32[]{:S(2)}) copy-start(f32[6,128,128]{2,1,0:T(8,128)S(1)} %collective-permute-done.23.cross_ref) | copy-start | bytes 1179652
  301.8 4.5 %copy-start.16 = (f32[6,128,128]{2,1,0:T(8,128)}, f32[6,128,128]{2,1,0:T(8,128)S(1)}, u32[]{:S(2)}) copy-start(f32[6,128,128]{2,1,0:T(8,128)S(1)} %collective-permute-done.24.ahead_ref) | copy-start | bytes 1179652
  306.3 0.7 copy-start.17
  322.5 3.9 %collective-permute-start.27 = (f32[8,512]{1,0:T(8,128)}, f32[8,512]{1,0:T(8,128)S(1)}, u32[]{:S(2)}, u32[]{:S(2)}) collective-permute-start(f32[8,512]{1,0:T(8,128)} %get-tuple-element.82), channel_id=1, source_target_pairs={{0,1},{1,0},{2,3},{3,2},{4,5},{5,4},{6,7},{7,6},{8,9},{9,8},{10,11... | collective-permute-start | bytes 49160 | tf_op jit(solution)/shard_map/ppermute | solution.py:47

commit v3 on v2

v3 whole, which is shorter than its diff:
```python
import functools
import math

import jax
import jax.numpy as jnp
from jax import lax
from jax.experimental import pallas as pl
from jax.experimental.pallas import tpu as pltpu
from jax.sharding import PartitionSpec as P

NODES = 24
PLANE = NODES * NODES
HALF = (NODES - 1) / 2.0
FACES = 6
CFL = 0.9
MU_REF = 60.0
OMEGA = 0.81
PRANDTL = 2.0 / 3.0
neighbour_steps = (1, -1, 2, -2)

LANES = 128
SUB = 8
F32 = jnp.float32
VMEM_LIMIT = 63_400_000


def passed_along(block, axis, distance):
    count = lax.axis_size(axis)
    route = [((i - distance) % count, i) for i in range(count)]
    return lax.ppermute(block, axis, route)


def swapped(block, axis, start):
    count = lax.axis_size(axis)
    route = []
    for i in range(start, start + count, 2):
        route += [(i % count, (i + 1) % count), ((i + 1) % count, i % count)]
    return lax.ppermute(block, axis, route)


def summed_over(value, axis):
    count = lax.axis_size(axis)
    if count & (count - 1):
        return lax.psum(value, axis)
    reach = 1
    while reach < count:
        value = value + lax.ppermute(value, axis, [(i, i ^ reach) for i in range(count)])
        reach *= 2
    return value


def round_plan(rows):
    tiles = -(-rows // LANES)
    groups = -(-tiles // SUB)
    sizes = [1, 1] if groups > 2 else []
    sizes += [2] * max(0, (groups - len(sizes) - 1) // 2)
    sizes += [1] * (groups - sum(sizes))
    plan, first = [], 0
    for size in sizes:
        plan.append((first, size, min(size * SUB, tiles - first * SUB)))
        first += size
    return plan


def turn(dist_ref, turned_ref):
    cells = dist_ref.shape[1]
    for s in range(SUB):
        for t in range(cells // LANES):
            block = dist_ref[s * LANES : (s + 1) * LANES, t * LANES : (t + 1) * LANES]
            turned_ref[pl.ds(t * LANES * SUB + s, LANES, stride=SUB), :] = block.T


def pick_rows(list_ref, row, turned_ref, picked_ref, out_ref, tiles):
    width = out_ref.shape[1]

    @pl.loop(0, width, unroll=8)
    def _(j):
        source = pl.ds(pl.multiple_of(list_ref[row, j] * SUB, SUB), SUB)
        picked_ref[pl.ds(pl.multiple_of(j * SUB, SUB), SUB), :] = turned_ref[source, :]

    for s in range(tiles):
        out_ref[s] = picked_ref[pl.ds(s, width, stride=SUB), :]


def first_send_kernel(
    place_ref, list_ref, dist_ref, normal_ref, volume_ref, cross_ref, ahead_ref, back_ref, least_ref,
    turned_ref, picked_ref,
):
    turn(dist_ref, turned_ref)
    for row, out_ref in ((2, ahead_ref), (3, back_ref), (1 - place_ref[1], cross_ref)):
        pick_rows(list_ref, row, turned_ref, picked_ref, out_ref, out_ref.shape[0])
    area = jnp.zeros_like(volume_ref)
    for k in range(FACES):
        part = [normal_ref[3 * k + a : 3 * k + a + 1, :] for a in range(3)]
        area = area + jnp.sqrt(part[0] * part[0] + part[1] * part[1] + part[2] * part[2])
    limit = volume_ref[...] / (HALF * math.sqrt(3.0) * area)
    least_ref[...] = jnp.broadcast_to(jnp.min(limit, axis=1, keepdims=True), least_ref.shape)


def turn_kernel(
    plan, place_ref, list_ref, dist_ref, after_ref, turned_ref, pair_ref, *refs,
):
    outs, picked_ref = refs[:-1], refs[-1]
    step = pl.program_id(0)
    turn(dist_ref, turned_ref.at[0])
    pick_rows(list_ref, place_ref[1], turned_ref.at[0], picked_ref, pair_ref, SUB)
    for i, (first, groups, tiles) in enumerate(plan):
        for g in range(groups):

            @pl.when(step == first + g)
            def _(i=i, g=g, tiles=tiles):
                here = min(SUB, tiles - g * SUB)
                for row, out_ref in zip((1 - place_ref[1], 2, 3), outs[3 * i : 3 * i + 3]):
                    pick_rows(list_ref, row, turned_ref.at[0], picked_ref, out_ref, here)


def rows8(row):
    return jnp.broadcast_to(row, (SUB, row.shape[-1]))


def last_speeds():
    index = lax.broadcasted_iota(jnp.int32, (SUB, LANES), 0).astype(F32) - HALF
    return [index + float(j * SUB) for j in range(NODES // SUB)]


def z_sums(tiles, speeds, powers):
    sums, terms = [], list(tiles)
    for p in range(powers):
        if p:
            terms = [t * c for t, c in zip(terms, speeds)]
        sums.append(terms[0] + terms[1] + terms[2])
    return sums


def rest_of_moments(sums, first):
    energy = 0.5 * (first * first * sums[0, 0] + sums[0, 1 + 1] + sums[2, 0])
    return [sums[0, 0], first * sums[0, 0], sums[0, 1], sums[1, 0], energy]


def add_rows(acc_ref, values, lanes):
    for m, value in enumerate(values):
        acc_ref[m * SUB : (m + 1) * SUB, lanes] += value


def sum_rows(acc_ref, count):
    return [jnp.sum(acc_ref[m * SUB : (m + 1) * SUB, :], axis=0, keepdims=True) for m in range(count)]


FLUX_KEYS = ((0, 0), (0, 1), (0, 2), (1, 0), (2, 0))
DIST_KEYS = ((0, 0), (0, 1), (0, 2), (0, 3), (1, 0), (1, 1), (1, 2), (2, 0), (2, 1), (3, 0))


def grow(carry, keys, sums, second):
    powers = [None, second, second * second, second * second * second]
    return tuple(
        c + (sums[i] if j == 0 else sums[i] * powers[j]) for c, (i, j) in zip(carry, keys)
    )


def moment_kernel(place_ref, dist_ref, after_ref, dist_sum_ref, dist_acc):
    step = pl.program_id(0)
    cells = dist_ref.shape[1]

    @pl.when(step == 0)
    def _():
        dist_acc[...] = jnp.zeros_like(dist_acc)

    speeds = last_speeds()
    tiles = range(NODES // SUB)
    first = (place_ref[0] + step).astype(F32) - HALF
    for t in range(cells // LANES):
        lanes = slice(t * LANES, (t + 1) * LANES)

        def body(y, carry, lanes=lanes):
            second = y.astype(F32) - HALF
            rows = [pl.ds(pl.multiple_of(y * NODES + j * SUB, SUB), SUB) for j in tiles]
            own = [dist_ref[r, lanes] for r in rows]
            return grow(carry, DIST_KEYS, z_sums(own, speeds, 4), second)

        zero = jnp.zeros((SUB, LANES), F32)
        part = lax.fori_loop(0, NODES, body, (zero,) * len(DIST_KEYS), unroll=4)
        s = dict(zip(DIST_KEYS, part))
        square = first * first
        add_rows(
            dist_acc,
            rest_of_moments(s, first)
            + [
                square * s[0, 0], s[0, 2], s[2, 0],
                first * s[0, 1], first * s[1, 0], s[1, 1],
                first * (square * s[0, 0] + s[0, 2] + s[2, 0]),
                square * s[0, 1] + s[0, 3] + s[2, 1],
                square * s[1, 0] + s[1, 2] + s[3, 0],
            ],
            lanes,
        )

    @pl.when(step == pl.num_programs(0) - 1)
    def _():
        dist_sum_ref[...] = jnp.concatenate(
            sum_rows(dist_acc, 14) + [jnp.zeros((2, cells), F32)], axis=0
        )


def speeds_at(index):
    first = jnp.floor((index + 0.5) * (1.0 / PLANE))
    rest = index - PLANE * first
    second = jnp.floor((rest + 0.5) * (1.0 / NODES))
    return first - HALF, second - HALF, rest - NODES * second - HALF


def time_row(least_ref, cells):
    return CFL * jnp.concatenate([least_ref[0:1, :]] * (cells // LANES), axis=1)


def face_kernel(
    rows, start, groups, rounds, place_ref, index_ref, normal_ref, stream_ref, turned_ref,
    before_ref, *refs,
):
    pairs, refs = refs[:groups], refs[groups:]
    received = [refs[3 * i : 3 * i + 3] for i in range(len(rounds))]
    flux_out_ref, flux_sum_ref, table_ref, flux_ref, flux_acc = refs[-5:]
    cells, width = flux_out_ref.shape[1], pairs[0].shape[1]
    odd = place_ref[1]
    block = SUB * LANES
    place_of, tiles = [], 0
    for i, count in enumerate(rounds):
        for g in range(count):
            place_of.append((received[i], g, min(SUB, received[i][0].shape[0] - g * SUB)))
            tiles += place_of[-1][2]

    speeds = []
    for g in range(groups):
        table_ref[g, 0 : cells * SUB, :] = turned_ref[g]
        (cross_ref, ahead_ref, back_ref), h, count = place_of[g]
        sources = ((pairs[g], 0, 1 - odd), (cross_ref, h, odd), (ahead_ref, h, 2), (back_ref, h, 3))
        for block_ref, part, slot in sources:
            for s in range(count):
                base = (cells + slot * width) * SUB + s
                table_ref[g, pl.ds(base, width, stride=SUB), :] = block_ref[part * SUB + s]
        inflow = cells + 4 * width
        table_ref[g, inflow * SUB : (inflow + 1) * SUB, :] = stream_ref[g * SUB : (g + 1) * SUB, :]
        at = lax.broadcasted_iota(jnp.int32, (SUB, LANES), 0) * LANES
        at = at + lax.broadcasted_iota(jnp.int32, (SUB, LANES), 1)
        at = at + (place_ref[0] * PLANE + start + g * block)
        speeds.append(speeds_at(at.astype(F32)))

    @pl.loop(0, cells, unroll=4)
    def _(c):
        here = pl.ds(pl.multiple_of(c * SUB, SUB), SUB)
        acc, low, full = ([None] * groups for _ in range(3))
        for k in range(FACES):
            source = pl.ds(pl.multiple_of(index_ref[k, c], SUB), SUB)
            normal = [normal_ref[3 * k + a, c] for a in range(3)]
            for g in range(groups):
                speed = sum(speeds[g][a] * normal[a] for a in range(1, 3)) + speeds[g][0] * normal[0]
                inward = jnp.minimum(speed, 0.0)
                part = inward * table_ref[g, source, :]
                acc[g] = part if k == 0 else acc[g] + part
                low[g] = inward if k == 0 else low[g] + inward
                full[g] = speed if k == 0 else full[g] + speed
        for g in range(groups):
            flux_ref[g, here, :] = acc[g] + (full[g] - low[g]) * table_ref[g, here, :]

    flux_acc[...] = jnp.zeros_like(flux_acc)
    parts = [slice(t * LANES, (t + 1) * LANES) for t in range(cells // LANES)]
    for q in range(tiles):
        g, s = divmod(q, SUB)
        turned = [
            flux_ref[g, pl.ds(t * LANES * SUB + s, LANES, stride=SUB), :].T for t in range(len(parts))
        ]
        sums = [[None] * 5 for _ in parts]
        for r in range(LANES // SUB):
            row = q * LANES + r * SUB
            counted = start + row < rows
            index = lax.broadcasted_iota(jnp.int32, (SUB, LANES), 0) + (
                place_ref[0] * PLANE + start + row
            )
            c = speeds_at(index.astype(F32))
            square = 0.5 * (c[0] * c[0] + c[1] * c[1] + c[2] * c[2])
            for t, lanes in enumerate(parts):
                flux = turned[t][r * SUB : (r + 1) * SUB, :]
                flux_out_ref[row : row + SUB, lanes] = flux
                if counted:
                    terms = [flux, c[0] * flux, c[1] * flux, c[2] * flux, square * flux]
                    sums[t] = [p if z is None else z + p for z, p in zip(sums[t], terms)]
        for t, lanes in enumerate(parts):
            if sums[t][0] is not None:
                add_rows(flux_acc, sums[t], lanes)
    flux_sum_ref[...] = before_ref[...] + jnp.concatenate(
        sum_rows(flux_acc, 5) + [jnp.zeros((3, cells), F32)], axis=0
    )


def hydrodynamic_variables(moments):
    density = moments[0]
    mean = [moments[1 + axis] / density for axis in range(3)]
    square = mean[0] ** 2 + mean[1] ** 2 + mean[2] ** 2
    return density, mean, (2.0 * moments[4] / density - square) / 3.0


def relax_kernel(
    planes, place_ref, least_ref, dist_ref, flux_ref, dist_sum_ref, flux_sum_ref, volume_ref, out_ref,
    x_ref, y_ref, z_ref, cell_ref,
):
    step = pl.program_id(0)
    cells = dist_ref.shape[1]

    @pl.when(step == 0)
    def _():
        time_step = time_row(least_ref, cells)
        ratio = time_step / volume_ref[...]
        sums = [dist_sum_ref[m : m + 1, :] for m in range(14)]
        density, mean, _ = hydrodynamic_variables(sums)
        xx, yy, zz, xy, xz, yz = sums[5:11]
        pairs = ((xx, xy, xz), (xy, yy, yz), (xz, yz, zz))
        square = mean[0] ** 2 + mean[1] ** 2 + mean[2] ** 2
        heat = []
        for a in range(3):
            cross = mean[0] * pairs[a][0] + mean[1] * pairs[a][1] + mean[2] * pairs[a][2]
            heat.append(
                0.5
                * (
                    sums[11 + a] - mean[a] * (2.0 * sums[4]) - 2.0 * cross
                    + 2.0 * mean[a] * square * density
                )
            )
        new = [sums[m] - ratio * flux_sum_ref[m : m + 1, :] for m in range(5)]
        density, mean, temp = hydrodynamic_variables(new)
        relax_time = MU_REF * jnp.exp(OMEGA * jnp.log(temp)) / (density * temp)
        relax = time_step / relax_time
        keep = 1.0 / (1.0 + relax)
        root = lax.rsqrt(2.0 * math.pi * temp)
        front = relax * keep * density * root * root * root
        along = (1.0 - PRANDTL) / (5.0 * density * temp * temp)
        for m, row in enumerate((keep, mean[0], temp, heat[0] * along, front, keep * ratio)):
            cell_ref[m * SUB : (m + 1) * SUB, :] = rows8(row)
        nodes = lax.broadcasted_iota(jnp.int32, (NODES, cells), 0).astype(F32) - HALF
        for a, ref in ((1, y_ref), (2, z_ref)):
            rel = nodes - mean[a]
            square = rel * rel / temp
            for i, table in enumerate((jnp.exp(-0.5 * square), square, rel * heat[a] * along)):
                if a == 2:
                    ref[i * NODES : (i + 1) * NODES, :] = table
                    continue
                for y in range(NODES):
                    ref[i, y] = rows8(table[y : y + 1, :])

    keep, mean, temp, heat, front = [
        cell_ref[m * SUB : (m + 1) * SUB, :] for m in range(5)
    ]
    for p in range(planes):
        rel = (place_ref[0] + step * planes + p).astype(F32) - HALF - mean
        square = rel * rel / temp
        x_ref[0] = front * jnp.exp(-0.5 * square)
        x_ref[1] = square - 5.0
        x_ref[2] = rel * heat

        for t in range(cells // LANES):
            lanes = slice(t * LANES, (t + 1) * LANES)
            from_x = [x_ref[i, :, lanes] for i in range(3)]
            tiles = range(NODES // SUB)
            from_z = [
                [z_ref[i * NODES + j * SUB : i * NODES + (j + 1) * SUB, lanes] for j in tiles]
                for i in range(3)
            ]
            share, flow = cell_ref[0:SUB, lanes], cell_ref[5 * SUB : 6 * SUB, lanes]

            @pl.loop(0, NODES, unroll=4)
            def _(y, p=p, lanes=lanes, from_x=from_x, from_z=from_z, share=share, flow=flow):
                peak = from_x[0] * y_ref[0, y, :, lanes]
                square = from_x[1] + y_ref[1, y, :, lanes]
                along = from_x[2] + y_ref[2, y, :, lanes]
                for j in range(NODES // SUB):
                    row = pl.ds(pl.multiple_of(p * PLANE + y * NODES + j * SUB, SUB), SUB)
                    moved = dist_ref[row, lanes] * share - flux_ref[row, lanes] * flow
                    shape = (along + from_z[2][j]) * (square + from_z[1][j]) + 1.0
                    out_ref[row, lanes] = moved + peak * from_z[0][j] * shape


def params():
    return pltpu.CompilerParams(
        vmem_limit_bytes=VMEM_LIMIT, dimension_semantics=("arbitrary",)
    )


def whole(*shape):
    return pl.BlockSpec(shape, lambda i: (0,) * len(shape))


def planes_from(first, width, planes=1):
    return pl.BlockSpec((planes * PLANE, width), lambda i: (first // planes + i, 0))


SMEM = pl.BlockSpec(memory_space=pltpu.SMEM)
ANY = pl.BlockSpec(memory_space=pl.ANY)


def hint(amount):
    return pl.CostEstimate(flops=0, bytes_accessed=amount, transcendentals=0)


def gate_kernel(*refs):
    pass


def gated(blocks, after):
    blocks = list(blocks)
    return pl.pallas_call(
        gate_kernel,
        in_specs=[ANY] * (len(blocks) + len(after)),
        out_specs=[ANY] * len(blocks),
        out_shape=[jax.ShapeDtypeStruct(block.shape, block.dtype) for block in blocks],
        input_output_aliases={i: i for i in range(len(blocks))},
        cost_estimate=hint(0),
        name="gate",
    )(*blocks, *after)


def first_sends(place, lists, dist, normals, volume, tiles):
    cells, width = dist.shape[1], lists.shape[1]
    return pl.pallas_call(
        first_send_kernel,
        grid=(1,),
        in_specs=[
            SMEM, SMEM, pl.BlockSpec((SUB * LANES, cells), lambda i: (0, 0)),
            whole(3 * FACES, cells), whole(1, cells),
        ],
        out_specs=[whole(tiles, width, LANES)] * 3 + [whole(SUB, LANES)],
        out_shape=[jax.ShapeDtypeStruct((tiles, width, LANES), F32)] * 3
        + [jax.ShapeDtypeStruct((SUB, LANES), F32)],
        scratch_shapes=[pltpu.VMEM((cells * SUB, LANES), F32), pltpu.VMEM((width * SUB, LANES), F32)],
        compiler_params=params(),
        cost_estimate=hint(4096),
        name="first_sends",
    )(place, lists, dist, normals, volume)


def turned_cells(place, lists, dist, plan, after):
    (rows, cells), width = dist.shape, lists.shape[1]
    block = SUB * LANES
    rounds = -(-rows // block)

    def part_of(first, groups):
        return pl.BlockSpec(
            (SUB, width, LANES), lambda i: (jnp.clip(i - first, 0, groups - 1), 0, 0)
        )

    outs = [(part_of(first, groups), tiles) for first, groups, tiles in plan for _ in range(3)]
    return pl.pallas_call(
        functools.partial(turn_kernel, plan),
        grid=(rounds,),
        in_specs=[
            SMEM, SMEM, pl.BlockSpec((block, cells), lambda i: (i, 0)), ANY,
        ],
        out_specs=[
            pl.BlockSpec((1, cells * SUB, LANES), lambda i: (i, 0, 0)),
            pl.BlockSpec((SUB, width, LANES), lambda i: (i, 0, 0)),
        ]
        + [spec for spec, _ in outs],
        out_shape=[
            jax.ShapeDtypeStruct((rounds, cells * SUB, LANES), F32),
            jax.ShapeDtypeStruct((-(-rows // LANES), width, LANES), F32),
        ]
        + [jax.ShapeDtypeStruct((tiles, width, LANES), F32) for _, tiles in outs],
        scratch_shapes=[pltpu.VMEM((width * SUB, LANES), F32)],
        compiler_params=params(),
        cost_estimate=hint(4096),
        name="turned_cells",
    )(place, lists, dist, after)


def dist_moments(place, dist, after):
    rows, cells = dist.shape
    return pl.pallas_call(
        moment_kernel,
        grid=(rows // PLANE,),
        in_specs=[SMEM, planes_from(0, cells), ANY],
        out_specs=whole(16, cells),
        out_shape=jax.ShapeDtypeStruct((16, cells), F32),
        scratch_shapes=[pltpu.VMEM((14 * SUB, cells), F32)],
        compiler_params=params(),
        cost_estimate=hint(4096),
        name="dist_moments",
    )(place, dist, after)


def face_sums(shape, place, index, normals, stream, turned, before, flux, pair, arrived, parts, after):
    (rows, cells), width = shape, pair.shape[1]
    first, counts = parts[0][0], [groups for _, groups, _ in parts]
    groups = sum(counts)
    block = SUB * LANES
    offset = first // groups
    extra = () if flux is None else (flux,)
    received = [block for group in arrived for block in group]
    aliases = {6 + groups + len(received): 0} if extra else {}
    return pl.pallas_call(
        functools.partial(face_kernel, rows, first * block, groups, counts),
        grid=(1,),
        in_specs=[
            SMEM, SMEM, SMEM,
            pl.BlockSpec((groups * SUB, LANES), lambda _: (offset, 0)),
            pl.BlockSpec((groups, cells * SUB, LANES), lambda _: (offset, 0, 0)),
            whole(8, cells),
        ]
        + [
            pl.BlockSpec((SUB, width, LANES), lambda _, g=g: (first + g, 0, 0))
            for g in range(groups)
        ]
        + [whole(*block.shape) for block in received]
        + [ANY] * (len(extra) + len(after)),
        out_specs=[
            pl.BlockSpec((groups * block, cells), lambda _: (offset, 0)), whole(8, cells),
        ],
        out_shape=[
            jax.ShapeDtypeStruct((rows, cells), F32),
            jax.ShapeDtypeStruct((8, cells), F32),
        ],
        scratch_shapes=[
            pltpu.VMEM((groups, (cells + 4 * width + 1) * SUB, LANES), F32),
            pltpu.VMEM((groups, cells * SUB, LANES), F32),
            pltpu.VMEM((5 * SUB, cells), F32),
        ],
        input_output_aliases=aliases,
        compiler_params=params(),
        cost_estimate=hint(4096),
        name="face_sums",
    )(place, index, normals, stream, turned, before, *([pair] * groups), *received, *extra, *after)


def step_planes(planes):
    return 2 - planes % 2


def relaxed(place, least, dist, flux, dist_sum, flux_sum, volume):
    rows, cells = dist.shape
    planes = step_planes(rows // PLANE)
    return pl.pallas_call(
        functools.partial(relax_kernel, planes),
        grid=(rows // PLANE // planes,),
        in_specs=[
            SMEM, whole(SUB, LANES), planes_from(0, cells, planes), planes_from(0, cells, planes),
            whole(16, cells), whole(8, cells), whole(1, cells),
        ],
        out_specs=planes_from(0, cells, planes),
        out_shape=jax.ShapeDtypeStruct((rows, cells), F32),
        scratch_shapes=[
            pltpu.VMEM((3, SUB, cells), F32),
            pltpu.VMEM((3, NODES, SUB, cells), F32),
            pltpu.VMEM((3 * NODES, cells), F32),
            pltpu.VMEM((6 * SUB, cells), F32),
        ],
        compiler_params=params(),
        cost_estimate=pl.CostEstimate(
            flops=10 * rows * cells, bytes_accessed=8 * rows * cells, transcendentals=0
        ),
        name="relaxed",
    )(place, least, dist, flux, dist_sum, flux_sum, volume)


def local(dist, free_stream, area_normal, cell_volume, face_nbr, face_type, send_list):
    rows, cells = dist.shape
    planes = rows // PLANE
    dirs, width = send_list.shape
    block = SUB * LANES
    rounds = -(-rows // block)
    place = jnp.stack([lax.axis_index("vel") * planes, lax.axis_index("space") % 2]).astype(jnp.int32)

    def sent(blocks):
        return (
            swapped(blocks[0], "space", 1),
            passed_along(blocks[1], "space", neighbour_steps[2]),
            passed_along(blocks[2], "space", neighbour_steps[3]),
        )

    plan = round_plan(rows)
    volume = cell_volume.reshape(1, cells)
    own = jnp.arange(cells, dtype=jnp.int32)[None, :]
    inflow = cells + dirs * width
    index = jnp.where(face_type == 0, face_nbr, jnp.where(face_type == 1, inflow, own)) * SUB
    stream = jnp.pad(free_stream, (0, rounds * block - rows)).reshape(rounds * SUB, LANES)

    shift, n_space = 1, lax.axis_size("space")
    *blocks, least = first_sends(place, send_list, dist, area_normal, volume, plan[0][2])
    turned, pair, *later = turned_cells(place, send_list, dist, plan[1:], blocks[0])
    arrived, pending, gate_after = [], [], []
    flux, flux_sum, dist_sum = None, jnp.zeros((8, cells), F32), None
    for i, part in enumerate(plan):
        arrived.append(sent(blocks))
        if shift < n_space:
            least = jnp.minimum(least, passed_along(least, "space", shift))
            shift *= 2
        if i == 0:
            gate_after = [turned]
        elif i == 1:
            pair = swapped(pair, "space", 0)
            dist_sum = dist_moments(place, dist, blocks[0])
            gate_after = [dist_sum, pair]
        else:
            parts = plan[0:2] if i == 2 else plan[i - 1 : i]
            flux, flux_sum = face_sums(
                dist.shape, place, index, area_normal, stream, turned, flux_sum, flux,
                pair, arrived[0:2] if i == 2 else arrived[i - 1 : i], parts, [blocks[0]],
            )
            gate_after = [flux_sum]
        if i == 2:
            dist_sum = summed_over(dist_sum, "vel")
            gate_after.append(dist_sum)
        if i + 1 < len(plan):
            blocks = later[3 * i : 3 * i + 3]
            rest = [least, pair] if i == 0 else [least]
            gated_arrays = gated([*blocks, *rest], [*arrived[-1], *gate_after])
            blocks, least = gated_arrays[:3], gated_arrays[3]
            if i == 0:
                pair = gated_arrays[4]
    if len(plan) == 1:
        dist_sum = dist_moments(place, dist, blocks[0])
        pair = swapped(pair, "space", 0)
    if len(plan) < 3:
        dist_sum = summed_over(dist_sum, "vel")
    done = 0 if len(plan) < 3 else len(plan) - 1
    flux, flux_sum = face_sums(
        dist.shape, place, index, area_normal, stream, turned, flux_sum, flux,
        pair, arrived[done:], plan[done:], [],
    )
    while shift < n_space:
        least = jnp.minimum(least, passed_along(least, "space", shift))
        shift *= 2
    flux_sum = summed_over(flux_sum, "vel")
    return relaxed(place, least, dist, flux, dist_sum, flux_sum, volume)


def solution(mesh):
    return jax.shard_map(
        local,
        mesh=mesh,
        in_specs=(
            P("vel", "space"),
            P("vel"),
            P(None, "space"),
            P("space"),
            P(None, "space"),
            P(None, "space"),
            P(None, "space"),
        ),
        out_specs=P("vel", "space"),
        check_vma=False,
    )
```

time: 343 us -> 294 us (0.86)
  Pallas kernels: 188 us -> 134 us
  waiting for transfers between devices: 57.1 us -> 79.9 us
  starting transfers between devices: 78.6 us -> 61.8 us
    pallas_call x14 -> x9, Pallas kernels: 156 us -> 97.6 us  [the longest x4 75.1 us: face_sums(): pl.pallas_call(functools.partial(face_kernel, rows, first * block, groups...]
    ppermute x18 -> x14, waiting for transfers between devices: 55.3 us -> 76.2 us  [passed_along(): return lax.ppermute(block, axis, route)]
    ppermute x18 -> x14, starting transfers between devices: 67.1 us -> 47 us  [passed_along(): return lax.ppermute(block, axis, route)]
    pallas_call x1, Pallas kernels: 13.9 us -> 17.8 us  [relaxed(): pl.pallas_call(functools.partial(relax_kernel, planes), grid=(rows // PLA...]
    ppermute x8 -> x6, starting transfers between devices: 8.47 us -> 11.7 us  [swapped(): return lax.ppermute(block, axis, route)]
  transfers between devices with their start and end apart: 28 -> 22, of which waited for: 10 -> 12; matrix products, arithmetic and copies ran while one was open for 2% -> 2% of each run, Pallas kernels for 45% -> 33%
where the time goes in v3:
time: 294 us; the launch traced here: 291 us
  Pallas kernels  134 us (46%)
  waiting for transfers between devices  79.9 us (27%)
  starting transfers between devices  61.8 us (21%)
  local copies, waits for them, and re-layouts  8.49 us (3%)
  other arithmetic  6.99 us (2%)
    ppermute x14, waiting for transfers between devices, passed_along(): return lax.ppermute(block, axis, route)  76.2 us
    pallas_call x4, Pallas kernels, face_sums(): pl.pallas_call(functools.partial(face_kernel, rows, first * block, groups...  75.1 us
    ppermute x14, starting transfers between devices, passed_along(): return lax.ppermute(block, axis, route)  47 us
    pallas_call x1, Pallas kernels, turned_cells(): pl.pallas_call(functools.partial(turn_kernel, plan), grid=(rounds,), in_s...  22.6 us
    pallas_call x1, Pallas kernels, relaxed(): pl.pallas_call(functools.partial(relax_kernel, planes), grid=(rows // PLA...  17.8 us
    pallas_call x1, Pallas kernels, dist_moments(): pl.pallas_call(moment_kernel, grid=(rows // PLANE,), in_specs=[SMEM, plan...  13.6 us
    ppermute x6, starting transfers between devices, swapped(): return lax.ppermute(block, axis, route)  11.7 us
    unnamed x36, local copies, waits for them, and re-layouts  6.54 us
  transfers between devices with their start and end apart: 22, of which 12 were waited for; matrix products, arithmetic and copies ran while one was open for 2% of the time, Pallas kernels for 33%

profile of v3, /device:TPU:0, one launch (start us, length us, event | category | flops | bytes accessed | tf_op | source)
XLA Modules:
  0.0 291.1 jit_solution(5835006551430458576)
XLA Ops:
  0.0 0.6 pad_add_fusion.place_ref
  0.6 4.8 %first_sends.1 = (f32[8,128,128]{2,1,0:T(8,128)}, f32[8,128,128]{2,1,0:T(8,128)}, f32[8,128,128]{2,1,0:T(8,128)}, f32[8,128]{1,0:T(8,128)}) custom-call(s32[2]{0:T(128)} %pad_add_fusion.place_ref, s32[4,128]{1,0:T(4,128)} %list_ref.3, f32[6912,512]{1,0:T(8,128)} %dist_ref.7, f32[18,512]{1,0:T(8,128)} %normal_ref.9, f32[1,512]{1,0:T(1,128)} %bitcast.5), custom_call_target="tpu_custom_call" | custom-call | bytes 4096 | tf_op jit(solution)/shard_map/first_sends/pallas_call | solution.py:421
  5.4 3.0 %collective-permute-start.2 = (f32[8,128,128]{2,1,0:T(8,128)}, f32[8,128,128]{2,1,0:T(8,128)S(1)}, u32[]{:S(2)}, u32[]{:S(2)}) collective-permute-start(f32[8,128,128]{2,1,0:T(8,128)} %get-tuple-element.63), channel_id=1, source_target_pairs={{28,0},{30,2},{0,4},{2,6},{4,8},{6,10},{8,12},{10,14},{12,16},{14,... | collective-permute-start | bytes 1572872 | tf_op jit(solution)/shard_map/ppermute | solution.py:30
  8.4 3.1 %collective-permute-start.3 = (f32[8,128,128]{2,1,0:T(8,128)}, f32[8,128,128]{2,1,0:T(8,128)S(1)}, u32[]{:S(2)}, u32[]{:S(2)}) collective-permute-start(f32[8,128,128]{2,1,0:T(8,128)} %get-tuple-element.64), channel_id=1, source_target_pairs={{4,0},{6,2},{8,4},{10,6},{12,8},{14,10},{16,12},{18,14},{20,16},{2... | collective-permute-start | bytes 1572872 | tf_op jit(solution)/shard_map/ppermute | solution.py:30
  11.5 0.8 collective-permute-start.1
  12.3 22.6 %turned_cells.1 = (f32[7,4096,128]{2,1,0:T(8,128)}, f32[54,128,128]{2,1,0:T(8,128)}, f32[8,128,128]{2,1,0:T(8,128)}, f32[8,128,128]{2,1,0:T(8,128)}, f32[8,128,1...) custom-call(s32[2]{0:T(128)} %pad_add_fusion.place_ref, ...), custom_call_target="tpu_custom_call" | custom-call | bytes 4096 | tf_op jit(solution)/shard_map/turned_cells/pallas_call | solution.py:449
  34.9 0.0 collective-permute-done
  34.9 0.6 min.12.refs_3_
  35.5 2.4 collective-permute-done.2.refs_6_.refs_3_
  37.9 1.0 collective-permute-done.3.refs_7_.refs_4_
  38.9 0.0 collective-permute-done.1.refs_5_.refs_2_
  38.9 0.8 copy-done.8
  39.7 0.2 copy-done.9
  39.9 5.3 %collective-permute-start.8 = (f32[54,128,128]{2,1,0:T(8,128)}, f32[54,128,128]{2,1,0:T(8,128)S(1)}, u32[]{:S(2)}, u32[]{:S(2)}) collective-permute-start(f32[54,128,128]{2,1,0:T(8,128)} %get-tuple-element.70), channel_id=1, source_target_pairs={{0,2},{2,0},{4,6},{6,4},{8,10},{10,8},{12,14},{14,12},{16,18},{18,... | collective-permute-start | bytes 10616840 | tf_op jit(solution)/shard_map/ppermute | solution.py:38
  45.1 1.5 collective-permute-start.6
  46.6 3.3 %collective-permute-start.7 = (f32[8,128,128]{2,1,0:T(8,128)}, f32[8,128,128]{2,1,0:T(8,128)}, u32[]{:S(2)}, u32[]{:S(2)}) collective-permute-start(f32[8,128,128]{2,1,0:T(8,128)} %get-tuple-element.69), channel_id=1, source_target_pairs={{4,0},{6,2},{8,4},{10,6},{12,8},{14,10},{16,12},{18,14},{20,16},{2... | collective-permute-start | bytes 1572872 | tf_op jit(solution)/shard_map/ppermute | solution.py:30
  49.9 1.3 collective-permute-start.5
  51.2 0.3 collective-permute-start.4
  51.5 13.6 %dist_moments.1.refs_7_ = f32[16,512]{1,0:T(8,128)} custom-call(s32[2]{0:T(128)} %pad_add_fusion.place_ref, f32[6912,512]{1,0:T(8,128)} %dist_ref.7, f32[8,128,128]{2,1,0:T(8,128)} %get-tuple-element.67.after_ref), custom_call_target="tpu_custom_call" | custom-call | bytes 4096 | tf_op jit(solution)/shard_map/dist_moments/pallas_call | solution.py:474
  65.1 11.0 %collective-permute-done.4 = f32[8,128]{1,0:T(8,128)S(1)} collective-permute-done((f32[8,128]{1,0:T(8,128)}, f32[8,128]{1,0:T(8,128)S(1)}, u32[]{:S(2)}, u32[]{:S(2)}) %collective-permute-start.4) | collective-permute-done | bytes 4128 | tf_op jit(solution)/shard_map/ppermute | solution.py:30
  76.0 0.6 min.13.refs_3_
  76.6 1.2 collective-permute-done.7.refs_6_.refs_7_
  77.9 0.0 collective-permute-done.8.refs_8_.refs_0_.refs_1_
  77.9 1.8 copy-done
  79.7 5.8 %collective-permute-start.11 = (f32[16,128,128]{2,1,0:T(8,128)}, f32[16,128,128]{2,1,0:T(8,128)S(1)}, u32[]{:S(2)}, u32[]{:S(2)}) collective-permute-start(f32[16,128,128]{2,1,0:T(8,128)} %get-tuple-element.73), channel_id=1, source_target_pairs={{28,0},{30,2},{0,4},{2,6},{4,8},{6,10},{8,12},{10,14},{12,16},{14,... | collective-permute-start | bytes 3145736 | tf_op jit(solution)/shard_map/ppermute | solution.py:30
  85.5 3.0 %collective-permute-start.12 = (f32[16,128,128]{2,1,0:T(8,128)}, f32[16,128,128]{2,1,0:T(8,128)S(1)}, u32[]{:S(2)}, u32[]{:S(2)}) collective-permute-start(f32[16,128,128]{2,1,0:T(8,128)} %get-tuple-element.74), channel_id=1, source_target_pairs={{4,0},{6,2},{8,4},{10,6},{12,8},{14,10},{16,12},{18,14},{20,16},{2... | collective-permute-start | bytes 3145736 | tf_op jit(solution)/shard_map/ppermute | solution.py:30
  88.6 1.8 collective-permute-start.10
  90.4 1.3 select_multiply_fusion.index_ref
  91.7 1.5 collective-permute-start.13
  93.2 0.0 collective-permute-start.9
  93.2 1.3 pad_bitcast_fusion.stream_ref
  94.5 1.3 collective-permute-done.13
  95.8 1.4 add.13.refs_8_.dist_sum_ref
  97.2 0.6 broadcast_in_dim.18.before_ref
  97.8 20.1 %face_sums.4 = (f32[6912,512]{1,0:T(8,128)}, f32[8,512]{1,0:T(8,128)}) custom-call(s32[2]{0:T(128)} %pad_add_fusion.place_ref, s32[6,512]{1,0:T(8,128)} %select_multiply_fusion.index_ref, f32[18,512]{1,0:T(8,128)} %normal_ref.9, f32[56,128]{1,0:T(8,128)} %pad_bitcast_fusion.stream_ref, f32[7,4096,128]{2,1,0:T(8,128)} %get-tuple-element.65.refs_8_.turned_ref, ...), custom_call_target="tpu_custom_call" | custom-call | bytes 4096 | tf_op jit(solution)/shard_map/face_sums/pallas_call | solution.py:496
  117.9 6.9 %collective-permute-done.9 = f32[8,128]{1,0:T(8,128)S(1)} collective-permute-done((f32[8,128]{1,0:T(8,128)}, f32[8,128]{1,0:T(8,128)S(1)}, u32[]{:S(2)}, u32[]{:S(2)}) %collective-permute-start.9) | collective-permute-done | bytes 4128 | tf_op jit(solution)/shard_map/ppermute | solution.py:30
  124.7 0.6 min.14.refs_3_
  125.3 17.8 %collective-permute-done.11.refs_5_.refs_3_ = f32[16,128,128]{2,1,0:T(8,128)S(1)} collective-permute-done((f32[16,128,128]{2,1,0:T(8,128)}, f32[16,128,128]{2,1,0:T(8,128)S(1)}, u32[]{:S(2)}, u32[]{:S(2)}) %collective-permute-start.11) | collective-permute-done | bytes 1048608 | tf_op jit(solution)/shard_map/ppermute | solution.py:30
  143.1 1.9 collective-permute-done.12.refs_6_.refs_4_
  145.0 1.0 copy-done.5
  145.9 0.4 copy-done.6
  146.3 11.2 %collective-permute-start.16 = (f32[16,128,128]{2,1,0:T(8,128)}, f32[16,128,128]{2,1,0:T(8,128)S(1)}, u32[]{:S(2)}, u32[]{:S(2)}) collective-permute-start(f32[16,128,128]{2,1,0:T(8,128)} %get-tuple-element.78), channel_id=1, source_target_pairs={{28,0},{30,2},{0,4},{2,6},{4,8},{6,10},{8,12},{10,14},{12,16},{14,... | collective-permute-start | bytes 3145736 | tf_op jit(solution)/shard_map/ppermute | solution.py:30
  157.5 3.0 %collective-permute-start.17 = (f32[16,128,128]{2,1,0:T(8,128)}, f32[16,128,128]{2,1,0:T(8,128)S(1)}, u32[]{:S(2)}, u32[]{:S(2)}) collective-permute-start(f32[16,128,128]{2,1,0:T(8,128)} %get-tuple-element.79), channel_id=1, source_target_pairs={{4,0},{6,2},{8,4},{10,6},{12,8},{14,10},{16,12},{18,14},{20,16},{2... | collective-permute-start | bytes 3145736 | tf_op jit(solution)/shard_map/ppermute | solution.py:30
  160.5 0.6 collective-permute-start.15
  161.1 20.2 %face_sums.5 = (f32[6912,512]{1,0:T(8,128)}, f32[8,512]{1,0:T(8,128)}) custom-call(s32[2]{0:T(128)} %pad_add_fusion.place_ref, s32[6,512]{1,0:T(8,128)} %select_multiply_fusion.index_ref, f32[18,512]{1,0:T(8,128)} %normal_ref.9, f32[56,128]{1,0:T(8,128)} %pad_bitcast_fusion.stream_ref, ...), custom_call_target="tpu_custom_call", output_to_operand_aliasing={{0}: (11, {})} | custom-call | bytes 4096 | tf_op jit(solution)/shard_map/face_sums/pallas_call | solution.py:496
  181.3 14.3 %collective-permute-done.14 = f32[8,128]{1,0:T(8,128)S(1)} collective-permute-done((f32[8,128]{1,0:T(8,128)}, f32[8,128]{1,0:T(8,128)S(1)}, u32[]{:S(2)}, u32[]{:S(2)}) %collective-permute-start.14) | collective-permute-done | bytes 4128 | tf_op jit(solution)/shard_map/ppermute | solution.py:30
  195.6 0.6 min.15.refs_3_
  196.2 18.8 %collective-permute-done.16.refs_5_.refs_3_ = f32[16,128,128]{2,1,0:T(8,128)S(1)} collective-permute-done((f32[16,128,128]{2,1,0:T(8,128)}, f32[16,128,128]{2,1,0:T(8,128)S(1)}, u32[]{:S(2)}, u32[]{:S(2)}) %collective-permute-start.16) | collective-permute-done | bytes 1048608 | tf_op jit(solution)/shard_map/ppermute | solution.py:30
  215.1 0.9 collective-permute-done.17.refs_6_.refs_4_
  216.0 0.0 copy-done.1
  216.0 1.0 copy-done.2
  217.0 0.4 copy-done.3
  217.4 11.2 %collective-permute-start.19 = (f32[6,128,128]{2,1,0:T(8,128)}, f32[6,128,128]{2,1,0:T(8,128)S(1)}, u32[]{:S(2)}, u32[]{:S(2)}) collective-permute-start(f32[6,128,128]{2,1,0:T(8,128)} %get-tuple-element.86), channel_id=1, source_target_pairs={{28,0},{30,2},{0,4},{2,6},{4,8},{6,10},{8,12},{10,14},{12,16},{14,... | collective-permute-start | bytes 1179656 | tf_op jit(solution)/shard_map/ppermute | solution.py:30
  228.5 1.7 collective-permute-start.20
  230.2 1.9 collective-permute-start.18
  232.2 20.2 %face_sums.6 = (f32[6912,512]{1,0:T(8,128)}, f32[8,512]{1,0:T(8,128)}) custom-call(s32[2]{0:T(128)} %pad_add_fusion.place_ref, s32[6,512]{1,0:T(8,128)} %select_multiply_fusion.index_ref, f32[18,512]{1,0:T(8,128)} %normal_ref.9, f32[56,128]{1,0:T(8,128)} %pad_bitcast_fusion.stream_ref, ...), custom_call_target="tpu_custom_call", output_to_operand_aliasing={{0}: (11, {})} | custom-call | bytes 4096 | tf_op jit(solution)/shard_map/face_sums/pallas_call | solution.py:496
  252.4 0.7 copy-done.10
  253.1 0.1 copy-done.11
  253.3 0.2 copy-done.12
  253.4 14.6 %face_sums.7 = (f32[6912,512]{1,0:T(8,128)}, f32[8,512]{1,0:T(8,128)}) custom-call(s32[2]{0:T(128)} %pad_add_fusion.place_ref, s32[6,512]{1,0:T(8,128)} %select_multiply_fusion.index_ref, f32[18,512]{1,0:T(8,128)} %normal_ref.9, f32[56,128]{1,0:T(8,128)} %pad_bitcast_fusion.stream_ref, ...), custom_call_target="tpu_custom_call", output_to_operand_aliasing={{0}: (10, {})} | custom-call | bytes 4096 | tf_op jit(solution)/shard_map/face_sums/pallas_call | solution.py:496
  268.0 1.5 collective-permute-start.21
  269.5 2.5 collective-permute-done.21
  272.0 1.3 add.14.flux_sum_ref
  273.3 17.8 %relaxed.1 = f32[6912,512]{1,0:T(8,128)} custom-call(s32[2]{0:T(128)} %pad_add_fusion.place_ref, f32[8,128]{1,0:T(8,128)} %get-tuple-element.82.least_ref, f32[6912,512]{1,0:T(8,128)} %dist_ref.7, f32[6912,512]{1,0:T(8,128)} %get-tuple-element.89.flux_ref, f32[16,512]{1,0:T(8,128)} %add.13.refs_8_.dist_sum_ref, f32[8,512]{1,0:T(8,128)} %add.14.flux_sum_ref, ...), custom_call_target="tpu_custom_call" | custom-call | flops 35389440 | bytes 28311552 | tf_op jit(solution)/shard_map/relaxed/pallas_call | solution.py:537
  (38 shorter events, 0.1 us)
Async XLA Ops:
  5.4 29.5 %copy-start.17 = (f32[8,128]{1,0:T(8,128)S(1)}, f32[8,128]{1,0:T(8,128)}, u32[]{:S(2)}) copy-start(f32[8,128]{1,0:T(8,128)} %get-tuple-element.61) | copy-start | bytes 12292
  5.4 32.5 %collective-permute-start.2 = (f32[8,128,128]{2,1,0:T(8,128)}, f32[8,128,128]{2,1,0:T(8,128)S(1)}, u32[]{:S(2)}, u32[]{:S(2)}) collective-permute-start(f32[8,128,128]{2,1,0:T(8,128)} %get-tuple-element.63), channel_id=1, source_target_pairs={{28,0},{30,2},{0,4},{2,6},{4,8},{6,10},{8,12},{10,14},{12,16},{14,... | collective-permute-start | bytes 1572872 | tf_op jit(solution)/shard_map/ppermute | solution.py:30
  8.4 30.5 %collective-permute-start.3 = (f32[8,128,128]{2,1,0:T(8,128)}, f32[8,128,128]{2,1,0:T(8,128)S(1)}, u32[]{:S(2)}, u32[]{:S(2)}) collective-permute-start(f32[8,128,128]{2,1,0:T(8,128)} %get-tuple-element.64), channel_id=1, source_target_pairs={{4,0},{6,2},{8,4},{10,6},{12,8},{14,10},{16,12},{18,14},{20,16},{2... | collective-permute-start | bytes 1572872 | tf_op jit(solution)/shard_map/ppermute | solution.py:30
  11.5 27.4 %collective-permute-start.1 = (f32[8,128,128]{2,1,0:T(8,128)}, f32[8,128,128]{2,1,0:T(8,128)S(1)}, u32[]{:S(2)}, u32[]{:S(2)}) collective-permute-start(f32[8,128,128]{2,1,0:T(8,128)} %get-tuple-element.48.after_ref), channel_id=1, source_target_pairs={{2,4},{4,2},{6,8},{8,6},{10,12},{12,10},{14,16},{16,14},{18,20},{2... | collective-permute-start | bytes 1572872 | tf_op jit(solution)/shard_map/ppermute | solution.py:38
  12.3 22.6 %collective-permute-start = (f32[8,128]{1,0:T(8,128)}, f32[8,128]{1,0:T(8,128)S(1)}, u32[]{:S(2)}, u32[]{:S(2)}) collective-permute-start(f32[8,128]{1,0:T(8,128)} %get-tuple-element.61), channel_id=1, source_target_pairs={{30,0},{0,2},{2,4},{4,6},{6,8},{8,10},{10,12},{12,14},{14,16},{16,... | collective-permute-start | bytes 12296 | tf_op jit(solution)/shard_map/ppermute | solution.py:30
  37.9 1.0 copy-start.7
  38.9 0.8 copy-start.8
  38.9 1.0 copy-start.9
  39.9 36.2 %copy-start.14 = (f32[8,128]{1,0:T(8,128)S(1)}, f32[8,128]{1,0:T(8,128)}, u32[]{:S(2)}) copy-start(f32[8,128]{1,0:T(8,128)} %get-tuple-element.66) | copy-start | bytes 12292
  39.9 50.5 %copy-start.16 = (s32[6,512]{1,0:T(8,128)S(1)}, s32[6,512]{1,0:T(8,128)}, u32[]{:S(2)}) copy-start(s32[6,512]{1,0:T(8,128)} %param.11) | copy-start | bytes 36868
  39.9 38.0 %collective-permute-start.8 = (f32[54,128,128]{2,1,0:T(8,128)}, f32[54,128,128]{2,1,0:T(8,128)S(1)}, u32[]{:S(2)}, u32[]{:S(2)}) collective-permute-start(f32[54,128,128]{2,1,0:T(8,128)} %get-tuple-element.70), channel_id=1, source_target_pairs={{0,2},{2,0},{4,6},{6,4},{8,10},{10,8},{12,14},{14,12},{16,18},{18,... | collective-permute-start | bytes 10616840 | tf_op jit(solution)/shard_map/ppermute | solution.py:38
  45.1 31.5 %collective-permute-start.6 = (f32[8,128,128]{2,1,0:T(8,128)}, f32[8,128,128]{2,1,0:T(8,128)}, u32[]{:S(2)}, u32[]{:S(2)}) collective-permute-start(f32[8,128,128]{2,1,0:T(8,128)} %get-tuple-element.68), channel_id=1, source_target_pairs={{28,0},{30,2},{0,4},{2,6},{4,8},{6,10},{8,12},{10,14},{12,16},{14,... | collective-permute-start | bytes 1572872 | tf_op jit(solution)/shard_map/ppermute | solution.py:30
  46.6 31.3 %collective-permute-start.7 = (f32[8,128,128]{2,1,0:T(8,128)}, f32[8,128,128]{2,1,0:T(8,128)}, u32[]{:S(2)}, u32[]{:S(2)}) collective-permute-start(f32[8,128,128]{2,1,0:T(8,128)} %get-tuple-element.69), channel_id=1, source_target_pairs={{4,0},{6,2},{8,4},{10,6},{12,8},{14,10},{16,12},{18,14},{20,16},{2... | collective-permute-start | bytes 1572872 | tf_op jit(solution)/shard_map/ppermute | solution.py:30
  49.9 28.0 %collective-permute-start.5 = (f32[8,128,128]{2,1,0:T(8,128)}, f32[8,128,128]{2,1,0:T(8,128)}, u32[]{:S(2)}, u32[]{:S(2)}) collective-permute-start(f32[8,128,128]{2,1,0:T(8,128)} %get-tuple-element.67.after_ref), channel_id=1, source_target_pairs={{2,4},{4,2},{6,8},{8,6},{10,12},{12,10},{14,16},{16,14},{18,20},{2... | collective-permute-start | bytes 1572872 | tf_op jit(solution)/shard_map/ppermute | solution.py:38
  51.2 24.9 %collective-permute-start.4 = (f32[8,128]{1,0:T(8,128)}, f32[8,128]{1,0:T(8,128)S(1)}, u32[]{:S(2)}, u32[]{:S(2)}) collective-permute-start(f32[8,128]{1,0:T(8,128)} %get-tuple-element.66), channel_id=1, source_target_pairs={{28,0},{30,2},{0,4},{2,6},{4,8},{6,10},{8,12},{10,14},{12,16},{14,... | collective-permute-start | bytes 12296 | tf_op jit(solution)/shard_map/ppermute | solution.py:30
  77.9 1.8 copy-start
  79.7 45.0 %copy-start.13 = (f32[8,128]{1,0:T(8,128)S(1)}, f32[8,128]{1,0:T(8,128)}, u32[]{:S(2)}) copy-start(f32[8,128]{1,0:T(8,128)} %get-tuple-element.71) | copy-start | bytes 12292
  79.7 63.4 %collective-permute-start.11 = (f32[16,128,128]{2,1,0:T(8,128)}, f32[16,128,128]{2,1,0:T(8,128)S(1)}, u32[]{:S(2)}, u32[]{:S(2)}) collective-permute-start(f32[16,128,128]{2,1,0:T(8,128)} %get-tuple-element.73), channel_id=1, source_target_pairs={{28,0},{30,2},{0,4},{2,6},{4,8},{6,10},{8,12},{10,14},{12,16},{14,... | collective-permute-start | bytes 3145736 | tf_op jit(solution)/shard_map/ppermute | solution.py:30
  85.5 59.4 %collective-permute-start.12 = (f32[16,128,128]{2,1,0:T(8,128)}, f32[16,128,128]{2,1,0:T(8,128)S(1)}, u32[]{:S(2)}, u32[]{:S(2)}) collective-permute-start(f32[16,128,128]{2,1,0:T(8,128)} %get-tuple-element.74), channel_id=1, source_target_pairs={{4,0},{6,2},{8,4},{10,6},{12,8},{14,10},{16,12},{18,14},{20,16},{2... | collective-permute-start | bytes 3145736 | tf_op jit(solution)/shard_map/ppermute | solution.py:30
  88.6 56.4 %collective-permute-start.10 = (f32[16,128,128]{2,1,0:T(8,128)}, f32[16,128,128]{2,1,0:T(8,128)S(1)}, u32[]{:S(2)}, u32[]{:S(2)}) collective-permute-start(f32[16,128,128]{2,1,0:T(8,128)} %get-tuple-element.72.refs_8_), channel_id=1, source_target_pairs={{2,4},{4,2},{6,8},{8,6},{10,12},{12,10},{14,16},{16,14},{18,20},{2... | collective-permute-start | bytes 3145736 | tf_op jit(solution)/shard_map/ppermute | solution.py:38
  91.7 4.1 %collective-permute-start.13 = (f32[16,512]{1,0:T(8,128)}, f32[16,512]{1,0:T(8,128)S(1)}, u32[]{:S(2)}, u32[]{:S(2)}) collective-permute-start(f32[16,512]{1,0:T(8,128)} %dist_moments.1.refs_7_), channel_id=1, source_target_pairs={{0,1},{1,0},{2,3},{3,2},{4,5},{5,4},{6,7},{7,6},{8,9},{9,8},{10,11... | collective-permute-start | bytes 98312 | tf_op jit(solution)/shard_map/ppermute | solution.py:47
  93.2 31.5 %collective-permute-start.9 = (f32[8,128]{1,0:T(8,128)}, f32[8,128]{1,0:T(8,128)S(1)}, u32[]{:S(2)}, u32[]{:S(2)}) collective-permute-start(f32[8,128]{1,0:T(8,128)} %get-tuple-element.71), channel_id=1, source_target_pairs={{24,0},{26,2},{28,4},{30,6},{0,8},{2,10},{4,12},{6,14},{8,16},{10,... | collective-permute-start | bytes 12296 | tf_op jit(solution)/shard_map/ppermute | solution.py:30
  143.1 1.9 copy-start.4
  145.0 1.0 copy-start.5
  145.0 1.3 copy-start.6
  146.3 68.7 %collective-permute-start.16 = (f32[16,128,128]{2,1,0:T(8,128)}, f32[16,128,128]{2,1,0:T(8,128)S(1)}, u32[]{:S(2)}, u32[]{:S(2)}) collective-permute-start(f32[16,128,128]{2,1,0:T(8,128)} %get-tuple-element.78), channel_id=1, source_target_pairs={{28,0},{30,2},{0,4},{2,6},{4,8},{6,10},{8,12},{10,14},{12,16},{14,... | collective-permute-start | bytes 3145736 | tf_op jit(solution)/shard_map/ppermute | solution.py:30
  157.5 58.5 %collective-permute-start.17 = (f32[16,128,128]{2,1,0:T(8,128)}, f32[16,128,128]{2,1,0:T(8,128)S(1)}, u32[]{:S(2)}, u32[]{:S(2)}) collective-permute-start(f32[16,128,128]{2,1,0:T(8,128)} %get-tuple-element.79), channel_id=1, source_target_pairs={{4,0},{6,2},{8,4},{10,6},{12,8},{14,10},{16,12},{18,14},{20,16},{2... | collective-permute-start | bytes 3145736 | tf_op jit(solution)/shard_map/ppermute | solution.py:30
  160.5 55.5 %collective-permute-start.15 = (f32[16,128,128]{2,1,0:T(8,128)}, f32[16,128,128]{2,1,0:T(8,128)S(1)}, u32[]{:S(2)}, u32[]{:S(2)}) collective-permute-start(f32[16,128,128]{2,1,0:T(8,128)} %get-tuple-element.77.refs_6_), channel_id=1, source_target_pairs={{2,4},{4,2},{6,8},{8,6},{10,12},{12,10},{14,16},{16,14},{18,20},{2... | collective-permute-start | bytes 3145736 | tf_op jit(solution)/shard_map/ppermute | solution.py:38
  161.1 34.5 %collective-permute-start.14 = (f32[8,128]{1,0:T(8,128)}, f32[8,128]{1,0:T(8,128)S(1)}, u32[]{:S(2)}, u32[]{:S(2)}) collective-permute-start(f32[8,128]{1,0:T(8,128)} %get-tuple-element.76), channel_id=1, source_target_pairs={{16,0},{18,2},{20,4},{22,6},{24,8},{26,10},{28,12},{30,14},{0,16},... | collective-permute-start | bytes 12296 | tf_op jit(solution)/shard_map/ppermute | solution.py:30
  161.1 34.5 %copy-start.15 = (f32[8,128]{1,0:T(8,128)S(1)}, f32[8,128]{1,0:T(8,128)}, u32[]{:S(2)}) copy-start(f32[8,128]{1,0:T(8,128)} %get-tuple-element.76) | copy-start | bytes 12292
  215.0 1.0 copy-start.1
  216.0 1.0 copy-start.2
  216.0 1.4 copy-start.3
  217.4 35.0 %collective-permute-start.19 = (f32[6,128,128]{2,1,0:T(8,128)}, f32[6,128,128]{2,1,0:T(8,128)S(1)}, u32[]{:S(2)}, u32[]{:S(2)}) collective-permute-start(f32[6,128,128]{2,1,0:T(8,128)} %get-tuple-element.86), channel_id=1, source_target_pairs={{28,0},{30,2},{0,4},{2,6},{4,8},{6,10},{8,12},{10,14},{12,16},{14,... | collective-permute-start | bytes 1179656 | tf_op jit(solution)/shard_map/ppermute | solution.py:30
  228.5 23.8 %collective-permute-start.20 = (f32[6,128,128]{2,1,0:T(8,128)}, f32[6,128,128]{2,1,0:T(8,128)S(1)}, u32[]{:S(2)}, u32[]{:S(2)}) collective-permute-start(f32[6,128,128]{2,1,0:T(8,128)} %get-tuple-element.87), channel_id=1, source_target_pairs={{4,0},{6,2},{8,4},{10,6},{12,8},{14,10},{16,12},{18,14},{20,16},{2... | collective-permute-start | bytes 1179656 | tf_op jit(solution)/shard_map/ppermute | solution.py:30
  230.2 22.2 %collective-permute-start.18 = (f32[6,128,128]{2,1,0:T(8,128)}, f32[6,128,128]{2,1,0:T(8,128)S(1)}, u32[]{:S(2)}, u32[]{:S(2)}) collective-permute-start(f32[6,128,128]{2,1,0:T(8,128)} %get-tuple-element.84.refs_6_), channel_id=1, source_target_pairs={{2,4},{4,2},{6,8},{8,6},{10,12},{12,10},{14,16},{16,14},{18,20},{2... | collective-permute-start | bytes 1179656 | tf_op jit(solution)/shard_map/ppermute | solution.py:38
  252.4 0.7 copy-start.10
  252.4 0.9 copy-start.11
  252.4 1.0 copy-start.12
  268.0 3.9 %collective-permute-start.21 = (f32[8,512]{1,0:T(8,128)}, f32[8,512]{1,0:T(8,128)S(1)}, u32[]{:S(2)}, u32[]{:S(2)}) collective-permute-start(f32[8,512]{1,0:T(8,128)} %get-tuple-element.90), channel_id=1, source_target_pairs={{0,1},{1,0},{2,3},{3,2},{4,5},{5,4},{6,7},{7,6},{8,9},{9,8},{10,11... | collective-permute-start | bytes 49160 | tf_op jit(solution)/shard_map/ppermute | solution.py:47

commit v4 on v3

--- a/solution.py
+++ b/solution.py
@@ -21,7 +21,7 @@
 LANES = 128
 SUB = 8
 F32 = jnp.float32
-VMEM_LIMIT = 63_400_000
+VMEM_LIMIT = 66_900_000
 
 
 def passed_along(block, axis, distance):
@@ -38,15 +38,16 @@
     return lax.ppermute(block, axis, route)
 
 
-def summed_over(value, axis):
+def halves_over(value, axis):
     count = lax.axis_size(axis)
     if count & (count - 1):
-        return lax.psum(value, axis)
-    reach = 1
+        return lax.psum(value, axis), jnp.zeros_like(value)
+    reach, other = 1, jnp.zeros_like(value)
     while reach < count:
-        value = value + lax.ppermute(value, axis, [(i, i ^ reach) for i in range(count)])
+        value = value if reach == 1 else value + other
+        other = lax.ppermute(value, axis, [(i, i ^ reach) for i in range(count)])
         reach *= 2
-    return value
+    return value, other
 
 
 def round_plan(rows):
@@ -213,12 +214,39 @@
 
 
 def face_kernel(
-    rows, start, groups, rounds, place_ref, index_ref, normal_ref, stream_ref, turned_ref,
+    rows, start, groups, rounds, timed, moves, place_ref, index_ref, normal_ref, stream_ref, turned_ref,
     before_ref, *refs,
 ):
     pairs, refs = refs[:groups], refs[groups:]
     received = [refs[3 * i : 3 * i + 3] for i in range(len(rounds))]
-    flux_out_ref, flux_sum_ref, table_ref, flux_ref, flux_acc = refs[-5:]
+    flux_out_ref, flux_sum_ref, table_ref, flux_ref, flux_acc, ratio_ref = refs[-6:]
+    if timed:
+        least_ref, dist_ref, volume_ref, earlier_ref = refs[3 * len(rounds) :][:4]
+        ratio_ref[...] = rows8(time_row(least_ref, flux_out_ref.shape[1]) / volume_ref[...])
+
+    if moves:
+
+        @pl.when(pl.program_id(0) > 0)
+        def _():
+            @pl.loop(0, flux_out_ref.shape[0] // SUB, unroll=8)
+            def _(i):
+                here = pl.ds(pl.multiple_of(i * SUB, SUB), SUB)
+                flux_out_ref[here, :] = dist_ref[here, :] - ratio_ref[...] * earlier_ref[here, :]
+
+    @pl.when(pl.program_id(0) == 0)
+    def _():
+        face_flux(
+            rows, start, groups, rounds, place_ref, index_ref, normal_ref, stream_ref, turned_ref,
+            before_ref, pairs, received, dist_ref if timed else None,
+            flux_out_ref, flux_sum_ref, table_ref, flux_ref, flux_acc, ratio_ref,
+        )
+
+
+def face_flux(
+    rows, start, groups, rounds, place_ref, index_ref, normal_ref, stream_ref, turned_ref,
+    before_ref, pairs, received, dist_ref,
+    flux_out_ref, flux_sum_ref, table_ref, flux_ref, flux_acc, ratio_ref,
+):
     cells, width = flux_out_ref.shape[1], pairs[0].shape[1]
     odd = place_ref[1]
     block = SUB * LANES
@@ -279,7 +307,10 @@
             square = 0.5 * (c[0] * c[0] + c[1] * c[1] + c[2] * c[2])
             for t, lanes in enumerate(parts):
                 flux = turned[t][r * SUB : (r + 1) * SUB, :]
-                flux_out_ref[row : row + SUB, lanes] = flux
+                here = slice(row, row + SUB), lanes
+                flux_out_ref[here] = (
+                    flux if dist_ref is None else dist_ref[here] - ratio_ref[:, lanes] * flux
+                )
                 if counted:
                     terms = [flux, c[0] * flux, c[1] * flux, c[2] * flux, square * flux]
                     sums[t] = [p if z is None else z + p for z, p in zip(sums[t], terms)]
@@ -299,17 +330,19 @@
 
 
 def relax_kernel(
-    planes, place_ref, least_ref, dist_ref, flux_ref, dist_sum_ref, flux_sum_ref, volume_ref, out_ref,
+    planes, place_ref, least_ref, moved_ref, dist_sum_ref, other_dist_ref, flux_sum_ref,
+    other_flux_ref, volume_ref, out_ref,
     x_ref, y_ref, z_ref, cell_ref,
 ):
     step = pl.program_id(0)
-    cells = dist_ref.shape[1]
+    cells = moved_ref.shape[1]
 
     @pl.when(step == 0)
     def _():
         time_step = time_row(least_ref, cells)
         ratio = time_step / volume_ref[...]
-        sums = [dist_sum_ref[m : m + 1, :] for m in range(14)]
+        sums = [dist_sum_ref[m : m + 1, :] + other_dist_ref[m : m + 1, :] for m in range(14)]
+        flux = [flux_sum_ref[m : m + 1, :] + other_flux_ref[m : m + 1, :] for m in range(5)]
         density, mean, _ = hydrodynamic_variables(sums)
         xx, yy, zz, xy, xz, yz = sums[5:11]
         pairs = ((xx, xy, xz), (xy, yy, yz), (xz, yz, zz))
@@ -324,7 +357,7 @@
                     + 2.0 * mean[a] * square * density
                 )
             )
-        new = [sums[m] - ratio * flux_sum_ref[m : m + 1, :] for m in range(5)]
+        new = [sums[m] - ratio * flux[m] for m in range(5)]
         density, mean, temp = hydrodynamic_variables(new)
         relax_time = MU_REF * jnp.exp(OMEGA * jnp.log(temp)) / (density * temp)
         relax = time_step / relax_time
@@ -332,7 +365,7 @@
         root = lax.rsqrt(2.0 * math.pi * temp)
         front = relax * keep * density * root * root * root
         along = (1.0 - PRANDTL) / (5.0 * density * temp * temp)
-        for m, row in enumerate((keep, mean[0], temp, heat[0] * along, front, keep * ratio)):
+        for m, row in enumerate((keep, mean[0], temp, heat[0] * along, front)):
             cell_ref[m * SUB : (m + 1) * SUB, :] = rows8(row)
         nodes = lax.broadcasted_iota(jnp.int32, (NODES, cells), 0).astype(F32) - HALF
         for a, ref in ((1, y_ref), (2, z_ref)):
@@ -363,16 +396,16 @@
                 [z_ref[i * NODES + j * SUB : i * NODES + (j + 1) * SUB, lanes] for j in tiles]
                 for i in range(3)
             ]
-            share, flow = cell_ref[0:SUB, lanes], cell_ref[5 * SUB : 6 * SUB, lanes]
+            share = cell_ref[0:SUB, lanes]
 
             @pl.loop(0, NODES, unroll=4)
-            def _(y, p=p, lanes=lanes, from_x=from_x, from_z=from_z, share=share, flow=flow):
+            def _(y, p=p, lanes=lanes, from_x=from_x, from_z=from_z, share=share):
                 peak = from_x[0] * y_ref[0, y, :, lanes]
                 square = from_x[1] + y_ref[1, y, :, lanes]
                 along = from_x[2] + y_ref[2, y, :, lanes]
                 for j in range(NODES // SUB):
                     row = pl.ds(pl.multiple_of(p * PLANE + y * NODES + j * SUB, SUB), SUB)
-                    moved = dist_ref[row, lanes] * share - flux_ref[row, lanes] * flow
+                    moved = moved_ref[row, lanes] * share
                     shape = (along + from_z[2][j]) * (square + from_z[1][j]) + 1.0
                     out_ref[row, lanes] = moved + peak * from_z[0][j] * shape
 
@@ -393,6 +426,7 @@
 
 SMEM = pl.BlockSpec(memory_space=pltpu.SMEM)
 ANY = pl.BlockSpec(memory_space=pl.ANY)
+HBM = pl.BlockSpec(memory_space=pltpu.HBM)
 
 
 def hint(amount):
@@ -407,8 +441,8 @@
     blocks = list(blocks)
     return pl.pallas_call(
         gate_kernel,
-        in_specs=[ANY] * (len(blocks) + len(after)),
-        out_specs=[ANY] * len(blocks),
+        in_specs=[HBM] * (len(blocks) + len(after)),
+        out_specs=[HBM] * len(blocks),
         out_shape=[jax.ShapeDtypeStruct(block.shape, block.dtype) for block in blocks],
         input_output_aliases={i: i for i in range(len(blocks))},
         cost_estimate=hint(0),
@@ -484,18 +518,30 @@
     )(place, dist, after)
 
 
-def face_sums(shape, place, index, normals, stream, turned, before, flux, pair, arrived, parts, after):
+def face_sums(
+    shape, place, index, normals, stream, turned, before, flux, pair, arrived, parts, after,
+    timed=(), earlier=False,
+):
     (rows, cells), width = shape, pair.shape[1]
     first, counts = parts[0][0], [groups for _, groups, _ in parts]
     groups = sum(counts)
     block = SUB * LANES
     offset = first // groups
     extra = () if flux is None else (flux,)
+    steps = 1 + (offset if earlier else 0)
+    here = pl.BlockSpec(
+        (groups * block, cells), lambda i: (jnp.where(i == 0, offset, i - 1) if steps > 1 else offset, 0)
+    )
+    done = pl.BlockSpec((groups * block, cells), lambda i: (jnp.maximum(i - 1, 0), 0))
+    timed_specs = [whole(SUB, LANES), here, whole(1, cells), done if steps > 1 else ANY]
     received = [block for group in arrived for block in group]
-    aliases = {6 + groups + len(received): 0} if extra else {}
+    if timed and not extra:
+        aliases, extra = {}, (timed[1],)
+    else:
+        aliases = {6 + groups + len(received) + len(timed): 0} if extra else {}
     return pl.pallas_call(
-        functools.partial(face_kernel, rows, first * block, groups, counts),
-        grid=(1,),
+        functools.partial(face_kernel, rows, first * block, groups, counts, bool(timed), steps > 1),
+        grid=(steps,),
         in_specs=[
             SMEM, SMEM, SMEM,
             pl.BlockSpec((groups * SUB, LANES), lambda _: (offset, 0)),
@@ -507,10 +553,9 @@
             for g in range(groups)
         ]
         + [whole(*block.shape) for block in received]
-        + [ANY] * (len(extra) + len(after)),
-        out_specs=[
-            pl.BlockSpec((groups * block, cells), lambda _: (offset, 0)), whole(8, cells),
-        ],
+        + (timed_specs if timed else [ANY] * len(extra))
+        + [ANY] * len(after),
+        out_specs=[here, whole(8, cells)],
         out_shape=[
             jax.ShapeDtypeStruct((rows, cells), F32),
             jax.ShapeDtypeStruct((8, cells), F32),
@@ -519,27 +564,31 @@
             pltpu.VMEM((groups, (cells + 4 * width + 1) * SUB, LANES), F32),
             pltpu.VMEM((groups, cells * SUB, LANES), F32),
             pltpu.VMEM((5 * SUB, cells), F32),
+            pltpu.VMEM((SUB, cells), F32),
         ],
         input_output_aliases=aliases,
         compiler_params=params(),
         cost_estimate=hint(4096),
         name="face_sums",
-    )(place, index, normals, stream, turned, before, *([pair] * groups), *received, *extra, *after)
+    )(
+        place, index, normals, stream, turned, before,
+        *([pair] * groups), *received, *timed, *extra, *after,
+    )
 
 
 def step_planes(planes):
     return 2 - planes % 2
 
 
-def relaxed(place, least, dist, flux, dist_sum, flux_sum, volume):
-    rows, cells = dist.shape
+def relaxed(place, least, moved, dist_sums, flux_sums, volume):
+    rows, cells = moved.shape
     planes = step_planes(rows // PLANE)
     return pl.pallas_call(
         functools.partial(relax_kernel, planes),
         grid=(rows // PLANE // planes,),
         in_specs=[
-            SMEM, whole(SUB, LANES), planes_from(0, cells, planes), planes_from(0, cells, planes),
-            whole(16, cells), whole(8, cells), whole(1, cells),
+            SMEM, whole(SUB, LANES), planes_from(0, cells, planes), whole(16, cells),
+            whole(16, cells), whole(8, cells), whole(8, cells), whole(1, cells),
         ],
         out_specs=planes_from(0, cells, planes),
         out_shape=jax.ShapeDtypeStruct((rows, cells), F32),
@@ -547,14 +596,14 @@
             pltpu.VMEM((3, SUB, cells), F32),
             pltpu.VMEM((3, NODES, SUB, cells), F32),
             pltpu.VMEM((3 * NODES, cells), F32),
-            pltpu.VMEM((6 * SUB, cells), F32),
+            pltpu.VMEM((5 * SUB, cells), F32),
         ],
         compiler_params=params(),
         cost_estimate=pl.CostEstimate(
             flops=10 * rows * cells, bytes_accessed=8 * rows * cells, transcendentals=0
         ),
         name="relaxed",
-    )(place, least, dist, flux, dist_sum, flux_sum, volume)
+    )(place, least, moved, *dist_sums, *flux_sums, volume)
 
 
 def local(dist, free_stream, area_normal, cell_volume, face_nbr, face_type, send_list):
@@ -583,28 +632,33 @@
     *blocks, least = first_sends(place, send_list, dist, area_normal, volume, plan[0][2])
     turned, pair, *later = turned_cells(place, send_list, dist, plan[1:], blocks[0])
     arrived, pending, gate_after = [], [], []
-    flux, flux_sum, dist_sum = None, jnp.zeros((8, cells), F32), None
+    flux, flux_sum, dist_sum, moved = None, jnp.zeros((8, cells), F32), None, False
     for i, part in enumerate(plan):
         arrived.append(sent(blocks))
-        if shift < n_space:
-            least = jnp.minimum(least, passed_along(least, "space", shift))
-            shift *= 2
+        least_now, least_known = least, shift >= n_space
+        for _ in range(2 if i == 2 else 1):
+            if shift < n_space:
+                least = jnp.minimum(least, passed_along(least, "space", shift))
+                shift *= 2
         if i == 0:
-            gate_after = [turned]
+            gate_after = []
         elif i == 1:
             pair = swapped(pair, "space", 0)
             dist_sum = dist_moments(place, dist, blocks[0])
             gate_after = [dist_sum, pair]
         else:
             parts = plan[0:2] if i == 2 else plan[i - 1 : i]
+            timed = (least_now, dist, volume) if least_known else ()
             flux, flux_sum = face_sums(
                 dist.shape, place, index, area_normal, stream, turned, flux_sum, flux,
                 pair, arrived[0:2] if i == 2 else arrived[i - 1 : i], parts, [blocks[0]],
+                timed, bool(timed) and not moved,
             )
+            moved = bool(timed)
             gate_after = [flux_sum]
         if i == 2:
-            dist_sum = summed_over(dist_sum, "vel")
-            gate_after.append(dist_sum)
+            dist_sum = halves_over(dist_sum, "vel")
+            gate_after += dist_sum
         if i + 1 < len(plan):
             blocks = later[3 * i : 3 * i + 3]
             rest = [least, pair] if i == 0 else [least]
@@ -616,17 +670,16 @@
         dist_sum = dist_moments(place, dist, blocks[0])
         pair = swapped(pair, "space", 0)
     if len(plan) < 3:
-        dist_sum = summed_over(dist_sum, "vel")
+        dist_sum = halves_over(dist_sum, "vel")
+    while shift < n_space:
+        least = jnp.minimum(least, passed_along(least, "space", shift))
+        shift *= 2
     done = 0 if len(plan) < 3 else len(plan) - 1
     flux, flux_sum = face_sums(
         dist.shape, place, index, area_normal, stream, turned, flux_sum, flux,
-        pair, arrived[done:], plan[done:], [],
+        pair, arrived[done:], plan[done:], [], (least, dist, volume), done > 0 and not moved,
     )
-    while shift < n_space:
-        least = jnp.minimum(least, passed_along(least, "space", shift))
-        shift *= 2
-    flux_sum = summed_over(flux_sum, "vel")
-    return relaxed(place, least, dist, flux, dist_sum, flux_sum, volume)
+    return relaxed(place, least, flux, dist_sum, halves_over(flux_sum, "vel"), volume)
 
 
 def solution(mesh):

time: 294 us -> 285 us (0.969)
  local copies, waits for them, and re-layouts: 8.49 us -> 2.42 us
  Pallas kernels: 134 us -> 138 us
  other arithmetic: 6.99 us -> 3.73 us
    pallas_call x4, Pallas kernels: 75.1 us -> 81.8 us  [face_sums(): pl.pallas_call(functools.partial(face_kernel, rows, first * block, groups...]
    unnamed x36 -> x14, local copies, waits for them, and re-layouts: 6.54 us -> 1.2 us
    pallas_call x1, Pallas kernels: 17.8 us -> 14.7 us  [relaxed(): pl.pallas_call(functools.partial(relax_kernel, planes), grid=(rows // PLA...]
  transfers between devices with their start and end apart: 22 -> 22, of which waited for: 12 -> 8; matrix products, arithmetic and copies ran while one was open for 2% -> 2% of each run, Pallas kernels for 33% -> 36%
where the time goes in v4:
time: 285 us; the launch traced here: 284 us
  Pallas kernels  138 us (48%)
  waiting for transfers between devices  80.6 us (28%)
  starting transfers between devices  59.5 us (21%)
  other arithmetic  3.73 us (1%)
    pallas_call x4, Pallas kernels, face_sums(): pl.pallas_call(functools.partial(face_kernel, rows, first * block, groups...  81.8 us
    ppermute x14, waiting for transfers between devices, passed_along(): return lax.ppermute(block, axis, route)  78.2 us
    ppermute x14, starting transfers between devices, passed_along(): return lax.ppermute(block, axis, route)  44.8 us
    pallas_call x1, Pallas kernels, turned_cells(): pl.pallas_call(functools.partial(turn_kernel, plan), grid=(rounds,), in_s...  22.6 us
    pallas_call x1, Pallas kernels, relaxed(): pl.pallas_call(functools.partial(relax_kernel, planes), grid=(rows // PLA...  14.7 us
    pallas_call x1, Pallas kernels, dist_moments(): pl.pallas_call(moment_kernel, grid=(rows // PLANE,), in_specs=[SMEM, plan...  13.6 us
    ppermute x6, starting transfers between devices, swapped(): return lax.ppermute(block, axis, route)  11.8 us
  transfers between devices with their start and end apart: 22, of which 8 were waited for; matrix products, arithmetic and copies ran while one was open for 2% of the time, Pallas kernels for 36%

profile of v4, /device:TPU:0, one launch (start us, length us, event | category | flops | bytes accessed | tf_op | source)
XLA Modules:
  0.0 284.0 jit_solution(5163267291944958909)
XLA Ops:
  0.0 0.6 pad_add_fusion.place_ref
  0.6 4.8 %first_sends.1 = (f32[8,128,128]{2,1,0:T(8,128)}, f32[8,128,128]{2,1,0:T(8,128)}, f32[8,128,128]{2,1,0:T(8,128)}, f32[8,128]{1,0:T(8,128)}) custom-call(s32[2]{0:T(128)} %pad_add_fusion.place_ref, s32[4,128]{1,0:T(4,128)} %list_ref.3, f32[6912,512]{1,0:T(8,128)} %refs_5_.1, f32[18,512]{1,0:T(8,128)} %normal_ref.9, f32[1,512]{1,0:T(1,128)} %bitcast.5), custom_call_target="tpu_custom_call" | custom-call | bytes 4096 | tf_op jit(solution)/shard_map/first_sends/pallas_call | solution.py:455
  5.5 3.0 %collective-permute-start.2 = (f32[8,128,128]{2,1,0:T(8,128)}, f32[8,128,128]{2,1,0:T(8,128)}, u32[]{:S(2)}, u32[]{:S(2)}) collective-permute-start(f32[8,128,128]{2,1,0:T(8,128)} %get-tuple-element.63), channel_id=1, source_target_pairs={{28,0},{30,2},{0,4},{2,6},{4,8},{6,10},{8,12},{10,14},{12,16},{14,... | collective-permute-start | bytes 1572872 | tf_op jit(solution)/shard_map/ppermute | solution.py:30
  8.4 3.1 %collective-permute-start.3 = (f32[8,128,128]{2,1,0:T(8,128)}, f32[8,128,128]{2,1,0:T(8,128)}, u32[]{:S(2)}, u32[]{:S(2)}) collective-permute-start(f32[8,128,128]{2,1,0:T(8,128)} %get-tuple-element.64), channel_id=1, source_target_pairs={{4,0},{6,2},{8,4},{10,6},{12,8},{14,10},{16,12},{18,14},{20,16},{2... | collective-permute-start | bytes 1572872 | tf_op jit(solution)/shard_map/ppermute | solution.py:30
  11.5 0.8 collective-permute-start.1
  12.4 0.0 collective-permute-start
  12.4 22.6 %turned_cells.1 = (f32[7,4096,128]{2,1,0:T(8,128)}, f32[54,128,128]{2,1,0:T(8,128)}, f32[8,128,128]{2,1,0:T(8,128)}, f32[8,128,128]{2,1,0:T(8,128)}, f32[8,128,1...) custom-call(s32[2]{0:T(128)} %pad_add_fusion.place_ref, ...), custom_call_target="tpu_custom_call" | custom-call | bytes 4096 | tf_op jit(solution)/shard_map/turned_cells/pallas_call | solution.py:483
  35.0 0.0 collective-permute-done
  35.0 0.6 min.12.refs_3_
  35.6 2.3 collective-permute-done.2.refs_6_.refs_3_
  37.9 1.1 collective-permute-done.3.refs_7_.refs_4_
  39.0 0.0 collective-permute-done.1.refs_5_.refs_2_
  39.1 5.5 %collective-permute-start.8 = (f32[54,128,128]{2,1,0:T(8,128)}, f32[54,128,128]{2,1,0:T(8,128)}, u32[]{:S(2)}, u32[]{:S(2)}) collective-permute-start(f32[54,128,128]{2,1,0:T(8,128)} %get-tuple-element.69), channel_id=1, source_target_pairs={{0,2},{2,0},{4,6},{6,4},{8,10},{10,8},{12,14},{14,12},{16,18},{18,... | collective-permute-start | bytes 10616840 | tf_op jit(solution)/shard_map/ppermute | solution.py:38
  44.5 1.1 collective-permute-start.6
  45.7 3.6 %collective-permute-start.7 = (f32[8,128,128]{2,1,0:T(8,128)}, f32[8,128,128]{2,1,0:T(8,128)}, u32[]{:S(2)}, u32[]{:S(2)}) collective-permute-start(f32[8,128,128]{2,1,0:T(8,128)} %get-tuple-element.68), channel_id=1, source_target_pairs={{4,0},{6,2},{8,4},{10,6},{12,8},{14,10},{16,12},{18,14},{20,16},{2... | collective-permute-start | bytes 1572872 | tf_op jit(solution)/shard_map/ppermute | solution.py:30
  49.3 1.0 collective-permute-start.5
  50.2 0.3 collective-permute-start.4
  50.5 13.6 %dist_moments.1.refs_7_.refs_8_.dist_sum_ref = f32[16,512]{1,0:T(8,128)} custom-call(s32[2]{0:T(128)} %pad_add_fusion.place_ref, f32[6912,512]{1,0:T(8,128)} %refs_5_.1, f32[8,128,128]{2,1,0:T(8,128)} %get-tuple-element.66.after_ref), custom_call_target="tpu_custom_call" | custom-call | bytes 4096 | tf_op jit(solution)/shard_map/dist_moments/pallas_call | solution.py:508
  64.1 11.0 %collective-permute-done.4 = f32[8,128]{1,0:T(8,128)S(1)} collective-permute-done((f32[8,128]{1,0:T(8,128)}, f32[8,128]{1,0:T(8,128)S(1)}, u32[]{:S(2)}, u32[]{:S(2)}) %collective-permute-start.4) | collective-permute-done | bytes 4128 | tf_op jit(solution)/shard_map/ppermute | solution.py:30
  75.1 0.6 min.13.refs_3_
  75.7 0.0 collective-permute-done.6.refs_5_.refs_6_
  75.7 1.2 collective-permute-done.7.refs_6_.refs_7_
  76.9 0.0 collective-permute-done.5.refs_4_.refs_5_
  76.9 0.0 collective-permute-done.8.refs_8_.refs_0_.refs_1_
  76.9 5.9 %collective-permute-start.12 = (f32[16,128,128]{2,1,0:T(8,128)}, f32[16,128,128]{2,1,0:T(8,128)}, u32[]{:S(2)}, u32[]{:S(2)}) collective-permute-start(f32[16,128,128]{2,1,0:T(8,128)} %get-tuple-element.72), channel_id=1, source_target_pairs={{28,0},{30,2},{0,4},{2,6},{4,8},{6,10},{8,12},{10,14},{12,16},{14,... | collective-permute-start | bytes 3145736 | tf_op jit(solution)/shard_map/ppermute | solution.py:30
  82.8 3.1 %collective-permute-start.13 = (f32[16,128,128]{2,1,0:T(8,128)}, f32[16,128,128]{2,1,0:T(8,128)}, u32[]{:S(2)}, u32[]{:S(2)}) collective-permute-start(f32[16,128,128]{2,1,0:T(8,128)} %get-tuple-element.73), channel_id=1, source_target_pairs={{4,0},{6,2},{8,4},{10,6},{12,8},{14,10},{16,12},{18,14},{20,16},{2... | collective-permute-start | bytes 3145736 | tf_op jit(solution)/shard_map/ppermute | solution.py:30
  85.9 1.8 collective-permute-start.11
  87.7 0.0 collective-permute-start.9
  87.7 0.0 copy-done.5
  87.7 0.6 select_multiply_fusion.index_ref
  88.3 1.5 collective-permute-start.14
  89.8 32.2 %collective-permute-done.9 = f32[8,128]{1,0:T(8,128)S(1)} collective-permute-done((f32[8,128]{1,0:T(8,128)}, f32[8,128]{1,0:T(8,128)S(1)}, u32[]{:S(2)}, u32[]{:S(2)}) %collective-permute-start.9) | collective-permute-done | bytes 4128 | tf_op jit(solution)/shard_map/ppermute | solution.py:30
  122.0 0.7 min.14
  122.7 0.0 collective-permute-start.10
  122.7 0.0 copy-done.2
  122.7 0.6 pad_bitcast_fusion.stream_ref
  123.3 0.6 broadcast_in_dim.18.before_ref
  123.9 20.1 %face_sums.4 = (f32[6912,512]{1,0:T(8,128)}, f32[8,512]{1,0:T(8,128)}) custom-call(s32[2]{0:T(128)} %pad_add_fusion.place_ref, s32[6,512]{1,0:T(8,128)} %select_multiply_fusion.index_ref, f32[18,512]{1,0:T(8,128)} %normal_ref.9, f32[56,128]{1,0:T(8,128)} %pad_bitcast_fusion.stream_ref, f32[7,4096,128]{2,1,0:T(8,128)} %get-tuple-element.74.turned_ref, ...), custom_call_target="tpu_custom_call" | custom-call | bytes 4096 | tf_op jit(solution)/shard_map/face_sums/pallas_call | solution.py:542
  144.0 0.0 collective-permute-done.10
  144.0 0.6 min.15.refs_3_
  144.6 0.0 collective-permute-done.14.refs_9_.other_dist_ref
  144.6 0.0 collective-permute-done.12.refs_5_.refs_3_
  144.6 0.0 collective-permute-done.13.refs_6_.refs_4_
  144.7 0.0 collective-permute-done.11.refs_4_.refs_2_
  144.7 0.6 copy-done
  145.2 8.7 %collective-permute-start.16 = (f32[16,128,128]{2,1,0:T(8,128)}, f32[16,128,128]{2,1,0:T(8,128)}, u32[]{:S(2)}, u32[]{:S(2)}) collective-permute-start(f32[16,128,128]{2,1,0:T(8,128)} %get-tuple-element.78), channel_id=1, source_target_pairs={{28,0},{30,2},{0,4},{2,6},{4,8},{6,10},{8,12},{10,14},{12,16},{14,... | collective-permute-start | bytes 3145736 | tf_op jit(solution)/shard_map/ppermute | solution.py:30
  153.9 3.0 %collective-permute-start.17 = (f32[16,128,128]{2,1,0:T(8,128)}, f32[16,128,128]{2,1,0:T(8,128)}, u32[]{:S(2)}, u32[]{:S(2)}) collective-permute-start(f32[16,128,128]{2,1,0:T(8,128)} %get-tuple-element.79), channel_id=1, source_target_pairs={{4,0},{6,2},{8,4},{10,6},{12,8},{14,10},{16,12},{18,14},{20,16},{2... | collective-permute-start | bytes 3145736 | tf_op jit(solution)/shard_map/ppermute | solution.py:30
  157.0 0.6 collective-permute-start.15
  157.5 24.7 %face_sums.5 = (f32[6912,512]{1,0:T(8,128)}, f32[8,512]{1,0:T(8,128)}) custom-call(s32[2]{0:T(128)} %pad_add_fusion.place_ref, s32[6,512]{1,0:T(8,128)} %select_multiply_fusion.index_ref, f32[18,512]{1,0:T(8,128)} %normal_ref.9, f32[56,128]{1,0:T(8,128)} %pad_bitcast_fusion.stream_ref, ...), custom_call_target="tpu_custom_call", output_to_operand_aliasing={{0}: (14, {})} | custom-call | bytes 4096 | tf_op jit(solution)/shard_map/face_sums/pallas_call | solution.py:542
  182.3 29.2 %collective-permute-done.16.refs_5_.refs_3_ = f32[16,128,128]{2,1,0:T(8,128)} collective-permute-done((f32[16,128,128]{2,1,0:T(8,128)}, f32[16,128,128]{2,1,0:T(8,128)}, u32[]{:S(2)}, u32[]{:S(2)}) %collective-permute-start.16) | collective-permute-done | bytes 1048608 | tf_op jit(solution)/shard_map/ppermute | solution.py:30
  211.5 1.0 collective-permute-done.17.refs_6_.refs_4_
  212.5 0.0 collective-permute-done.15.refs_4_.refs_2_
  212.5 11.5 %collective-permute-start.19 = (f32[6,128,128]{2,1,0:T(8,128)}, f32[6,128,128]{2,1,0:T(8,128)}, u32[]{:S(2)}, u32[]{:S(2)}) collective-permute-start(f32[6,128,128]{2,1,0:T(8,128)} %get-tuple-element.86), channel_id=1, source_target_pairs={{28,0},{30,2},{0,4},{2,6},{4,8},{6,10},{8,12},{10,14},{12,16},{14,... | collective-permute-start | bytes 1179656 | tf_op jit(solution)/shard_map/ppermute | solution.py:30
  224.1 1.5 collective-permute-start.20
  225.6 2.1 collective-permute-start.18
  227.7 21.7 %face_sums.6 = (f32[6912,512]{1,0:T(8,128)}, f32[8,512]{1,0:T(8,128)}) custom-call(s32[2]{0:T(128)} %pad_add_fusion.place_ref, s32[6,512]{1,0:T(8,128)} %select_multiply_fusion.index_ref, f32[18,512]{1,0:T(8,128)} %normal_ref.9, f32[56,128]{1,0:T(8,128)} %pad_bitcast_fusion.stream_ref, ...), custom_call_target="tpu_custom_call", output_to_operand_aliasing={{0}: (14, {})} | custom-call | bytes 4096 | tf_op jit(solution)/shard_map/face_sums/pallas_call | solution.py:542
  249.4 0.0 collective-permute-done.19.refs_2_
  249.4 0.0 collective-permute-done.20.refs_3_
  249.4 0.0 collective-permute-done.18.refs_1_
  249.4 15.2 %face_sums.7 = (f32[6912,512]{1,0:T(8,128)}, f32[8,512]{1,0:T(8,128)}) custom-call(s32[2]{0:T(128)} %pad_add_fusion.place_ref, s32[6,512]{1,0:T(8,128)} %select_multiply_fusion.index_ref, f32[18,512]{1,0:T(8,128)} %normal_ref.9, f32[56,128]{1,0:T(8,128)} %pad_bitcast_fusion.stream_ref, ...), custom_call_target="tpu_custom_call", output_to_operand_aliasing={{0}: (13, {})} | custom-call | bytes 4096 | tf_op jit(solution)/shard_map/face_sums/pallas_call | solution.py:542
  264.7 1.5 collective-permute-start.21
  266.2 2.5 collective-permute-done.21.other_flux_ref
  268.6 0.6 copy-done.3
  269.2 14.7 %relaxed.1 = f32[6912,512]{1,0:T(8,128)} custom-call(s32[2]{0:T(128)} %pad_add_fusion.place_ref, f32[8,128]{1,0:T(8,128)} %get-tuple-element.82.refs_5_.refs_4_.least_ref, f32[6912,512]{1,0:T(8,128)} %get-tuple-element.89.moved_ref, f32[16,512]{1,0:T(8,128)} %dist_moments.1.refs_7_.refs_8_.dist_sum_ref, f32[16,512]{1,0:T(8,128)} %copy-done, ...), custom_call_target="tpu_custom_call" | custom-call | flops 35389440 | bytes 28311552 | tf_op jit(solution)/shard_map/relaxed/pallas_call | solution.py:586
  (14 shorter events, 0.0 us)
Async XLA Ops:
  5.5 29.5 %copy-start.6 = (f32[8,128]{1,0:T(8,128)S(1)}, f32[8,128]{1,0:T(8,128)}, u32[]{:S(2)}) copy-start(f32[8,128]{1,0:T(8,128)} %get-tuple-element.61) | copy-start | bytes 12292
  5.5 32.5 %collective-permute-start.2 = (f32[8,128,128]{2,1,0:T(8,128)}, f32[8,128,128]{2,1,0:T(8,128)}, u32[]{:S(2)}, u32[]{:S(2)}) collective-permute-start(f32[8,128,128]{2,1,0:T(8,128)} %get-tuple-element.63), channel_id=1, source_target_pairs={{28,0},{30,2},{0,4},{2,6},{4,8},{6,10},{8,12},{10,14},{12,16},{14,... | collective-permute-start | bytes 1572872 | tf_op jit(solution)/shard_map/ppermute | solution.py:30
  8.4 30.6 %collective-permute-start.3 = (f32[8,128,128]{2,1,0:T(8,128)}, f32[8,128,128]{2,1,0:T(8,128)}, u32[]{:S(2)}, u32[]{:S(2)}) collective-permute-start(f32[8,128,128]{2,1,0:T(8,128)} %get-tuple-element.64), channel_id=1, source_target_pairs={{4,0},{6,2},{8,4},{10,6},{12,8},{14,10},{16,12},{18,14},{20,16},{2... | collective-permute-start | bytes 1572872 | tf_op jit(solution)/shard_map/ppermute | solution.py:30
  11.5 27.5 %collective-permute-start.1 = (f32[8,128,128]{2,1,0:T(8,128)}, f32[8,128,128]{2,1,0:T(8,128)}, u32[]{:S(2)}, u32[]{:S(2)}) collective-permute-start(f32[8,128,128]{2,1,0:T(8,128)} %get-tuple-element.48.after_ref), channel_id=1, source_target_pairs={{2,4},{4,2},{6,8},{8,6},{10,12},{12,10},{14,16},{16,14},{18,20},{2... | collective-permute-start | bytes 1572872 | tf_op jit(solution)/shard_map/ppermute | solution.py:38
  12.4 22.6 %collective-permute-start = (f32[8,128]{1,0:T(8,128)}, f32[8,128]{1,0:T(8,128)S(1)}, u32[]{:S(2)}, u32[]{:S(2)}) collective-permute-start(f32[8,128]{1,0:T(8,128)} %get-tuple-element.61), channel_id=1, source_target_pairs={{30,0},{0,2},{2,4},{4,6},{6,8},{8,10},{10,12},{12,14},{14,16},{16,... | collective-permute-start | bytes 12296 | tf_op jit(solution)/shard_map/ppermute | solution.py:30
  39.0 48.7 %copy-start.4 = (s32[6,512]{1,0:T(8,128)S(1)}, s32[6,512]{1,0:T(8,128)}, u32[]{:S(2)}) copy-start(s32[6,512]{1,0:T(8,128)} %param.11) | copy-start | bytes 36868
  39.0 48.7 %copy-start.5 = (s32[6,512]{1,0:T(8,128)S(1)}, s32[6,512]{1,0:T(8,128)}, u32[]{:S(2)}) copy-start(s32[6,512]{1,0:T(8,128)} %param.12) | copy-start | bytes 36868
  39.0 83.7 %copy-start.2 = (f32[6912]{0:T(1024)S(1)}, f32[6912]{0:T(1024)}, u32[]{:S(2)}) copy-start(f32[6912]{0:T(1024)} %param.8) | copy-start | bytes 82948
  39.0 36.1 %copy-start.1 = (f32[8,128]{1,0:T(8,128)S(1)}, f32[8,128]{1,0:T(8,128)}, u32[]{:S(2)}) copy-start(f32[8,128]{1,0:T(8,128)} %get-tuple-element.65) | copy-start | bytes 12292
  39.1 37.9 %collective-permute-start.8 = (f32[54,128,128]{2,1,0:T(8,128)}, f32[54,128,128]{2,1,0:T(8,128)}, u32[]{:S(2)}, u32[]{:S(2)}) collective-permute-start(f32[54,128,128]{2,1,0:T(8,128)} %get-tuple-element.69), channel_id=1, source_target_pairs={{0,2},{2,0},{4,6},{6,4},{8,10},{10,8},{12,14},{14,12},{16,18},{18,... | collective-permute-start | bytes 10616840 | tf_op jit(solution)/shard_map/ppermute | solution.py:38
  44.5 31.2 %collective-permute-start.6 = (f32[8,128,128]{2,1,0:T(8,128)}, f32[8,128,128]{2,1,0:T(8,128)}, u32[]{:S(2)}, u32[]{:S(2)}) collective-permute-start(f32[8,128,128]{2,1,0:T(8,128)} %get-tuple-element.67), channel_id=1, source_target_pairs={{28,0},{30,2},{0,4},{2,6},{4,8},{6,10},{8,12},{10,14},{12,16},{14,... | collective-permute-start | bytes 1572872 | tf_op jit(solution)/shard_map/ppermute | solution.py:30
  45.7 31.2 %collective-permute-start.7 = (f32[8,128,128]{2,1,0:T(8,128)}, f32[8,128,128]{2,1,0:T(8,128)}, u32[]{:S(2)}, u32[]{:S(2)}) collective-permute-start(f32[8,128,128]{2,1,0:T(8,128)} %get-tuple-element.68), channel_id=1, source_target_pairs={{4,0},{6,2},{8,4},{10,6},{12,8},{14,10},{16,12},{18,14},{20,16},{2... | collective-permute-start | bytes 1572872 | tf_op jit(solution)/shard_map/ppermute | solution.py:30
  49.3 27.7 %collective-permute-start.5 = (f32[8,128,128]{2,1,0:T(8,128)}, f32[8,128,128]{2,1,0:T(8,128)}, u32[]{:S(2)}, u32[]{:S(2)}) collective-permute-start(f32[8,128,128]{2,1,0:T(8,128)} %get-tuple-element.66.after_ref), channel_id=1, source_target_pairs={{2,4},{4,2},{6,8},{8,6},{10,12},{12,10},{14,16},{16,14},{18,20},{2... | collective-permute-start | bytes 1572872 | tf_op jit(solution)/shard_map/ppermute | solution.py:38
  50.2 24.9 %collective-permute-start.4 = (f32[8,128]{1,0:T(8,128)}, f32[8,128]{1,0:T(8,128)S(1)}, u32[]{:S(2)}, u32[]{:S(2)}) collective-permute-start(f32[8,128]{1,0:T(8,128)} %get-tuple-element.65), channel_id=1, source_target_pairs={{28,0},{30,2},{0,4},{2,6},{4,8},{6,10},{8,12},{10,14},{12,16},{14,... | collective-permute-start | bytes 12296 | tf_op jit(solution)/shard_map/ppermute | solution.py:30
  76.9 67.7 %collective-permute-start.12 = (f32[16,128,128]{2,1,0:T(8,128)}, f32[16,128,128]{2,1,0:T(8,128)}, u32[]{:S(2)}, u32[]{:S(2)}) collective-permute-start(f32[16,128,128]{2,1,0:T(8,128)} %get-tuple-element.72), channel_id=1, source_target_pairs={{28,0},{30,2},{0,4},{2,6},{4,8},{6,10},{8,12},{10,14},{12,16},{14,... | collective-permute-start | bytes 3145736 | tf_op jit(solution)/shard_map/ppermute | solution.py:30
  82.8 61.9 %collective-permute-start.13 = (f32[16,128,128]{2,1,0:T(8,128)}, f32[16,128,128]{2,1,0:T(8,128)}, u32[]{:S(2)}, u32[]{:S(2)}) collective-permute-start(f32[16,128,128]{2,1,0:T(8,128)} %get-tuple-element.73), channel_id=1, source_target_pairs={{4,0},{6,2},{8,4},{10,6},{12,8},{14,10},{16,12},{18,14},{20,16},{2... | collective-permute-start | bytes 3145736 | tf_op jit(solution)/shard_map/ppermute | solution.py:30
  85.9 58.8 %collective-permute-start.11 = (f32[16,128,128]{2,1,0:T(8,128)}, f32[16,128,128]{2,1,0:T(8,128)}, u32[]{:S(2)}, u32[]{:S(2)}) collective-permute-start(f32[16,128,128]{2,1,0:T(8,128)} %get-tuple-element.71.refs_8_), channel_id=1, source_target_pairs={{2,4},{4,2},{6,8},{8,6},{10,12},{12,10},{14,16},{16,14},{18,20},{2... | collective-permute-start | bytes 3145736 | tf_op jit(solution)/shard_map/ppermute | solution.py:38
  87.7 34.3 %collective-permute-start.9 = (f32[8,128]{1,0:T(8,128)}, f32[8,128]{1,0:T(8,128)S(1)}, u32[]{:S(2)}, u32[]{:S(2)}) collective-permute-start(f32[8,128]{1,0:T(8,128)} %get-tuple-element.70), channel_id=1, source_target_pairs={{24,0},{26,2},{28,4},{30,6},{0,8},{2,10},{4,12},{6,14},{8,16},{10,... | collective-permute-start | bytes 12296 | tf_op jit(solution)/shard_map/ppermute | solution.py:30
  88.3 56.3 %collective-permute-start.14 = (f32[16,512]{1,0:T(8,128)}, f32[16,512]{1,0:T(8,128)S(1)}, u32[]{:S(2)}, u32[]{:S(2)}) collective-permute-start(f32[16,512]{1,0:T(8,128)} %dist_moments.1.refs_7_.refs_8_.dist_sum_ref), channel_id=1, source_target_pairs={{0,1},{1,0},{2,3},{3,2},{4,5},{5,4},{6,7},{7,6},{8,9},{9,8},{10,11... | collective-permute-start | bytes 98312 | tf_op jit(solution)/shard_map/ppermute | solution.py:48
  122.7 21.3 %collective-permute-start.10 = (f32[8,128]{1,0:T(8,128)S(1)}, f32[8,128]{1,0:T(8,128)S(1)}, u32[]{:S(2)}, u32[]{:S(2)}) collective-permute-start(f32[8,128]{1,0:T(8,128)S(1)} %min.14), channel_id=1, source_target_pairs={{16,0},{18,2},{20,4},{22,6},{24,8},{26,10},{28,12},{30,14},{0,16},... | collective-permute-start | bytes 12296 | tf_op jit(solution)/shard_map/ppermute | solution.py:30
  144.6 0.6 copy-start
  145.2 66.2 %collective-permute-start.16 = (f32[16,128,128]{2,1,0:T(8,128)}, f32[16,128,128]{2,1,0:T(8,128)}, u32[]{:S(2)}, u32[]{:S(2)}) collective-permute-start(f32[16,128,128]{2,1,0:T(8,128)} %get-tuple-element.78), channel_id=1, source_target_pairs={{28,0},{30,2},{0,4},{2,6},{4,8},{6,10},{8,12},{10,14},{12,16},{14,... | collective-permute-start | bytes 3145736 | tf_op jit(solution)/shard_map/ppermute | solution.py:30
  153.9 58.6 %collective-permute-start.17 = (f32[16,128,128]{2,1,0:T(8,128)}, f32[16,128,128]{2,1,0:T(8,128)}, u32[]{:S(2)}, u32[]{:S(2)}) collective-permute-start(f32[16,128,128]{2,1,0:T(8,128)} %get-tuple-element.79), channel_id=1, source_target_pairs={{4,0},{6,2},{8,4},{10,6},{12,8},{14,10},{16,12},{18,14},{20,16},{2... | collective-permute-start | bytes 3145736 | tf_op jit(solution)/shard_map/ppermute | solution.py:30
  157.0 55.6 %collective-permute-start.15 = (f32[16,128,128]{2,1,0:T(8,128)}, f32[16,128,128]{2,1,0:T(8,128)}, u32[]{:S(2)}, u32[]{:S(2)}) collective-permute-start(f32[16,128,128]{2,1,0:T(8,128)} %get-tuple-element.77.refs_9_), channel_id=1, source_target_pairs={{2,4},{4,2},{6,8},{8,6},{10,12},{12,10},{14,16},{16,14},{18,20},{2... | collective-permute-start | bytes 3145736 | tf_op jit(solution)/shard_map/ppermute | solution.py:38
  212.5 36.9 %collective-permute-start.19 = (f32[6,128,128]{2,1,0:T(8,128)}, f32[6,128,128]{2,1,0:T(8,128)}, u32[]{:S(2)}, u32[]{:S(2)}) collective-permute-start(f32[6,128,128]{2,1,0:T(8,128)} %get-tuple-element.86), channel_id=1, source_target_pairs={{28,0},{30,2},{0,4},{2,6},{4,8},{6,10},{8,12},{10,14},{12,16},{14,... | collective-permute-start | bytes 1179656 | tf_op jit(solution)/shard_map/ppermute | solution.py:30
  224.1 25.4 %collective-permute-start.20 = (f32[6,128,128]{2,1,0:T(8,128)}, f32[6,128,128]{2,1,0:T(8,128)}, u32[]{:S(2)}, u32[]{:S(2)}) collective-permute-start(f32[6,128,128]{2,1,0:T(8,128)} %get-tuple-element.87), channel_id=1, source_target_pairs={{4,0},{6,2},{8,4},{10,6},{12,8},{14,10},{16,12},{18,14},{20,16},{2... | collective-permute-start | bytes 1179656 | tf_op jit(solution)/shard_map/ppermute | solution.py:30
  225.6 23.8 %collective-permute-start.18 = (f32[6,128,128]{2,1,0:T(8,128)}, f32[6,128,128]{2,1,0:T(8,128)}, u32[]{:S(2)}, u32[]{:S(2)}) collective-permute-start(f32[6,128,128]{2,1,0:T(8,128)} %get-tuple-element.84.refs_9_), channel_id=1, source_target_pairs={{2,4},{4,2},{6,8},{8,6},{10,12},{12,10},{14,16},{16,14},{18,20},{2... | collective-permute-start | bytes 1179656 | tf_op jit(solution)/shard_map/ppermute | solution.py:38
  264.7 3.9 %collective-permute-start.21 = (f32[8,512]{1,0:T(8,128)}, f32[8,512]{1,0:T(8,128)S(1)}, u32[]{:S(2)}, u32[]{:S(2)}) collective-permute-start(f32[8,512]{1,0:T(8,128)} %get-tuple-element.90.flux_sum_ref), channel_id=1, source_target_pairs={{0,1},{1,0},{2,3},{3,2},{4,5},{5,4},{6,7},{7,6},{8,9},{9,8},{10,11... | collective-permute-start | bytes 49160 | tf_op jit(solution)/shard_map/ppermute | solution.py:48
  268.6 0.6 copy-start.3
